TPU v7x, 32 devices: a whole 2x2x4 slice. The times are simulated.
32 devices in a mesh: ctx: 8 (over z, x), batch: 4 (over y, core).
Axes of the slice: x: 2, y: 2, z: 4, core: 2. Of those that a mesh axis runs over, the one named last changes fastest.
Arguments:
- kda_query: bfloat16 [4096, 2048], P(('batch', 'ctx')), parts along dimension 0, may hold values from -6 to 6
- kda_key: bfloat16 [4096, 2048], P(('batch', 'ctx')), parts along dimension 0, may hold values from -6 to 6
- kda_value: bfloat16 [4096, 2048], P(('batch', 'ctx')), parts along dimension 0, may hold values from -6 to 6
- log_decay: bfloat16 [4096, 2048], P(('batch', 'ctx')), parts along dimension 0, may hold values from -2 to 0
- write_rate: float32 [4096, 16], P(('batch', 'ctx')), parts along dimension 0, may hold values from 0.01 to 0.9
- mla_query: bfloat16 [4096, 3072], P(('batch', 'ctx')), parts along dimension 0, may hold values from -8 to 8
- latents: bfloat16 [4096, 576], P(('batch', 'ctx')), parts along dimension 0, may hold values from -8 to 8
- key_up: bfloat16 [512, 2048], replicated, may hold values from -0.25 to 0.25
- value_up: bfloat16 [512, 2048], replicated, may hold values from -0.25 to 0.25
- doc_lengths: int32 [32], P('batch'), parts along dimension 0, may hold values from 1 to 512, 1024 in all
Outputs:
- kda_out: bfloat16 [4096, 2048], P(('batch', 'ctx')), parts along dimension 0
- mla_out: bfloat16 [4096, 2048], P(('batch', 'ctx')), parts along dimension 0
There are 4 independent parts, one for each index of `batch`. A program takes and returns all parts, laid end to end along the dimension named above; an argument that names none is the same for every part. Nothing has to cross between parts.
Inputs may be any that keep to these rules, and one draw needn't show every extreme that they name: `doc_lengths`: 8 lengths of the documents of one context in order; they sum to 1024 and the longest is exactly 512.
All inputs are finite; a program needn't handle non-finite values.
Results may differ from a plain program's by a relative error of at most 0.009.
Values may be sent and summed in bfloat16 or wider, within the bound.
No kernel may reach another device: no remote copies, remote signals or barrier semaphores. Data moves between devices by JAX's collectives and lax.ppermute only.
A program may use at most 192 MiB of HBM per device.

v0:
```python
import math

import jax
import jax.numpy as jnp
from jax import lax
from jax.sharding import PartitionSpec as P

NOPE = 128
ROPE = 64
LATENT = 512
BLOCK = 64


PRECISE_PRODUCT = lax.Precision.HIGHEST


def prefix(array, axis, join, neutral):
    place = lax.axis_index(axis)
    gathered = jax.tree.map(
        lambda a, kind: lax.all_gather(a.astype(kind), axis),
        array,
        jax.tree.map(lambda a: jnp.bfloat16 if a.dtype == jnp.float32 else a.dtype, array),
    )
    state = jax.tree.map(lambda a, e: jnp.zeros_like(a) + jnp.asarray(e, a.dtype), array, neutral)

    def one(step, state):
        return join(
            state,
            jax.tree.map(
                lambda a, own: lax.dynamic_index_in_dim(a, step, 0, False).astype(own.dtype),
                gathered,
                array,
            ),
        )

    return lax.fori_loop(0, place, one, state)


def shifted(block, axis, distance):
    devices = range(lax.axis_size(axis))
    route = [(i - distance, i) for i in devices if i - distance in devices]
    return lax.ppermute(block, axis, route)


def unit_rows(values):
    return values * lax.rsqrt(jnp.sum(values * values, axis=-1, keepdims=True) + 1e-06)


def doc_of(positions, doc_starts):
    match_count = (doc_starts[None, :] <= positions[:, None]).astype(jnp.int32)
    return jnp.sum(match_count, axis=1) - 1


def unit_lower_inverse(strictly_lower):
    length = strictly_lower.shape[-1]
    identity = jnp.eye(length, dtype=jnp.float32)[None]
    result = identity - strictly_lower
    power_term = strictly_lower
    for level_index in range(length.bit_length() - 2):
        power_term = jnp.einsum("hij,hjk->hik", power_term, power_term, precision=PRECISE_PRODUCT)
        result = jnp.einsum(
            "hij,hjk->hik", result, identity + power_term, precision=PRECISE_PRODUCT
        )
    return result


def block_terms(query_unit, keyvec, valvec, logarithm_decay, write_gain, docids, prevdoc):
    length = docids.shape[0]
    cumulative = jnp.cumsum(logarithm_decay, axis=0)
    growth = jnp.exp(cumulative)
    key_plus = keyvec * growth
    key_minus = keyvec * jnp.exp(-cumulative)
    query_plus = query_unit * growth
    places = jnp.arange(length)
    same_doc = docids[:, None] == docids[None, :]
    strict = (places[:, None] > places[None, :]) & same_doc
    causal = (places[:, None] >= places[None, :]) & same_doc
    follow = (docids == prevdoc).astype(jnp.float32)
    inner_prod = jnp.einsum("thk,shk->hts", key_plus, key_minus, precision=PRECISE_PRODUCT)
    strictly_lower = (
        jnp.where(strict[None], inner_prod, 0.0) * jnp.transpose(write_gain)[:, :, None]
    )
    inverse = unit_lower_inverse(strictly_lower)
    value_rhs = jnp.transpose(valvec * write_gain[:, :, None], (1, 0, 2))
    key_rhs = jnp.transpose(key_plus * (write_gain * follow[:, None])[:, :, None], (1, 0, 2))
    value_solution = jnp.einsum("hts,hsv->htv", inverse, value_rhs, precision=PRECISE_PRODUCT)
    solved_key = jnp.einsum("hts,hsk->htk", inverse, key_rhs, precision=PRECISE_PRODUCT)
    mixing = jnp.where(
        causal[None],
        jnp.einsum("thk,shk->hts", query_plus, key_minus, precision=PRECISE_PRODUCT),
        0.0,
    )
    local_output = jnp.einsum("hts,hsv->htv", mixing, value_solution, precision=PRECISE_PRODUCT)
    query_effective = jnp.transpose(query_plus * follow[:, None, None], (1, 0, 2)) - jnp.einsum(
        "hts,hsk->htk", mixing, solved_key, precision=PRECISE_PRODUCT
    )
    last_doc = (docids == docids[length - 1]).astype(jnp.float32)
    key_trailing = (
        keyvec * jnp.exp(cumulative[length - 1][None] - cumulative) * last_doc[:, None, None]
    )
    growth_last = growth[length - 1]
    diagonal_map = growth_last[:, :, None] * jnp.eye(keyvec.shape[2], dtype=jnp.float32)[None]
    handed_operator = follow[length - 1] * diagonal_map - jnp.einsum(
        "shk,hsj->hkj", key_trailing, solved_key, precision=PRECISE_PRODUCT
    )
    handed_update = jnp.einsum(
        "omt,mor->mtr", key_trailing, value_solution, precision=PRECISE_PRODUCT
    )
    return (local_output, query_effective, handed_operator, handed_update)


def compose(prior_slab, successor_slab):
    joined_map = jnp.einsum(
        "hkj,hjl->hkl", successor_slab[0], prior_slab[0], precision=PRECISE_PRODUCT
    )
    combined_increment = (
        jnp.einsum("ytn,yne->yte", successor_slab[0], prior_slab[1], precision=PRECISE_PRODUCT)
        + successor_slab[1]
    )
    return (joined_map, combined_increment)


def local(
    kda_query,
    kda_key,
    kda_value,
    log_decay,
    write_rate,
    mla_query,
    latents,
    key_up,
    value_up,
    doc_lengths,
):
    slab_rows = latents.shape[0]
    head_count = write_rate.shape[1]
    first_row = lax.axis_index("ctx") * slab_rows
    doc_starts = jnp.cumsum(doc_lengths) - doc_lengths
    positions = first_row + jnp.arange(slab_rows, dtype=jnp.int32)
    docids = doc_of(positions, doc_starts)
    query_unit = unit_rows(kda_query.astype(jnp.float32).reshape(slab_rows, head_count, -1))
    keyvec = unit_rows(kda_key.astype(jnp.float32).reshape(slab_rows, head_count, -1))
    valvec = kda_value.astype(jnp.float32).reshape(slab_rows, head_count, -1)
    logarithm_decay = log_decay.astype(jnp.float32).reshape(slab_rows, head_count, -1)
    block_count = slab_rows // BLOCK
    prevdocs = doc_of(first_row + jnp.arange(block_count, dtype=jnp.int32) * BLOCK - 1, doc_starts)

    def shaped(values):
        return values.reshape((block_count, BLOCK) + values.shape[1:])

    block_outs = jax.vmap(block_terms)(
        shaped(query_unit),
        shaped(keyvec),
        shaped(valvec),
        shaped(logarithm_decay),
        shaped(write_rate),
        shaped(docids),
        prevdocs,
    )
    key_dim = keyvec.shape[2]
    value_dim = valvec.shape[2]
    identity_map = jnp.broadcast_to(
        jnp.eye(key_dim, dtype=jnp.float32)[None], (head_count, key_dim, key_dim)
    )
    zero_add = jnp.zeros((head_count, key_dim, value_dim), jnp.float32)

    def advance_block(prefix_pair, block_item):
        map_before, update_from_prior = prefix_pair
        local_output, query_effective, handed_operator, handed_update = block_item
        eff_now = jnp.einsum("htk,hkj->htj", query_effective, map_before, precision=PRECISE_PRODUCT)
        output_current = local_output + jnp.einsum(
            "cor,crm->com", query_effective, update_from_prior, precision=PRECISE_PRODUCT
        )
        map_after = jnp.einsum(
            "hkj,hjl->hkl", handed_operator, map_before, precision=PRECISE_PRODUCT
        )
        increment_later = (
            jnp.einsum(
                "ytn,yne->yte", handed_operator, update_from_prior, precision=PRECISE_PRODUCT
            )
            + handed_update
        )
        return ((map_after, increment_later), (eff_now, output_current))

    slab_pair, per_block = lax.scan(advance_block, (identity_map, zero_add), block_outs)
    effective_everything, output_everything = per_block
    leading_part = prefix(slab_pair, "ctx", compose, (identity_map, zero_add))
    delta_attention_complete = output_everything + jnp.einsum(
        "enzx,nxu->enzu", effective_everything, leading_part[1], precision=PRECISE_PRODUCT
    )
    kda_out = (
        jnp.transpose(delta_attention_complete, (0, 2, 1, 3))
        .reshape(slab_rows, -1)
        .astype(jnp.bfloat16)
    )
    queries = mla_query.reshape(slab_rows, head_count, NOPE + ROPE)
    query_nope = queries[:, :, :NOPE]
    query_rope = queries[:, :, NOPE:]
    score_scale = 1.0 / math.sqrt(NOPE + ROPE)
    last_place = positions[slab_rows - 1]
    first_doc_start = jnp.sum(
        jnp.where(jnp.arange(doc_starts.shape[0]) == docids[0], doc_starts, 0)
    )

    def attend_rows(softmax_state, key_rows, key_first):
        running_max, running_sum, accumulated = softmax_state
        row_count = key_rows.shape[0]
        latent_part = key_rows[:, :LATENT]
        keys_nope = (
            jnp.dot(latent_part, key_up, preferred_element_type=jnp.float32)
            .astype(jnp.bfloat16)
            .reshape(row_count, head_count, NOPE)
        )
        values = (
            jnp.dot(latent_part, value_up, preferred_element_type=jnp.float32)
            .astype(jnp.bfloat16)
            .reshape(row_count, head_count, -1)
        )
        scores = jnp.einsum(
            "thd,shd->hts", query_nope, keys_nope, preferred_element_type=jnp.float32
        )
        scores = (
            scores
            + jnp.einsum(
                "thr,sr->hts", query_rope, key_rows[:, LATENT:], preferred_element_type=jnp.float32
            )
        ) * score_scale
        key_places = key_first + jnp.arange(row_count, dtype=jnp.int32)
        key_docs = doc_of(key_places, doc_starts)
        allowed = (key_places[None, :] <= positions[:, None]) & (
            key_docs[None, :] == docids[:, None]
        )
        masked = jnp.where(allowed[None], scores, -1e30)
        new_max = jnp.maximum(running_max, jnp.max(masked, axis=2))
        weights = jnp.where(allowed[None], jnp.exp(masked - new_max[:, :, None]), 0.0)
        factor = jnp.exp(running_max - new_max)
        running_sum = running_sum * factor + jnp.sum(weights, axis=2)
        product = jnp.einsum(
            "hts,shv->thv", weights.astype(jnp.bfloat16), values, preferred_element_type=jnp.float32
        )
        accumulated = accumulated * jnp.transpose(factor)[:, :, None] + product
        return (new_max, running_sum, accumulated)

    def guarded(softmax_state, key_rows, key_first):
        row_count = key_rows.shape[0]
        needed = (key_first <= last_place) & (key_first + row_count - 1 >= first_doc_start)
        return lax.cond(
            needed, lambda: attend_rows(softmax_state, key_rows, key_first), lambda: softmax_state
        )

    value_width = value_up.shape[1] // head_count
    initial_state = (
        jnp.full((head_count, slab_rows), -1e30, jnp.float32),
        jnp.zeros((head_count, slab_rows), jnp.float32),
        jnp.zeros((slab_rows, head_count, value_width), jnp.float32),
    )
    own_state = guarded(initial_state, latents, first_row)

    def advance_window(step_index, window_pair):
        carried_state, moving = window_pair
        moving = shifted(moving, "ctx", 1)
        carried_state = guarded(carried_state, moving, first_row - (step_index + 1) * slab_rows)
        return (carried_state, moving)

    softmax_state, _ = lax.fori_loop(
        0, lax.axis_size("ctx") // 2, advance_window, (own_state, latents)
    )
    running_sum = softmax_state[1]
    accumulated = softmax_state[2]
    mla_out = (
        (accumulated / jnp.transpose(running_sum)[:, :, None])
        .astype(jnp.bfloat16)
        .reshape(slab_rows, -1)
    )
    return (kda_out, mla_out)


def solution(mesh):
    in_specs = (
        P(("batch", "ctx"), None),
        P(("batch", "ctx"), None),
        P(("batch", "ctx"), None),
        P(("batch", "ctx"), None),
        P(("batch", "ctx"), None),
        P(("batch", "ctx"), None),
        P(("batch", "ctx"), None),
        P(),
        P(),
        P("batch"),
    )
    out_specs = (P(("batch", "ctx"), None), P(("batch", "ctx"), None))
    return jax.shard_map(local, mesh=mesh, in_specs=in_specs, out_specs=out_specs, check_vma=False)
```

profile of v0, /device:TPU:31, one launch (start us, length us, event | category | flops | bytes accessed | tf_op | source)
XLA Modules:
  0.0 266.4 jit_solution(3368275443084440778)
XLA Ops:
  7.2 1.7 copy.270
  12.8 1.4 copy_exponential_fusion
  15.5 1.2 copy.151
  16.7 1.6 reduce_sum.83
  18.7 3.1 %fusion.69 = f32[2,16,64,64]{3,2,1,0:T(8,128)S(1)} fusion(f32[2,16,64]{2,1,0:T(8,128)S(1)} %get-tuple-element.952, pred[2,64,64]{2,1,0:T(8,128)(4,1)S(1)} %get-tuple-element.955, f32[2,64,16,128]{3,2,1,0:T(8,128)S(1)} %bitcast.226, f32[2,64,16]{1,2,0:T(8,128)S(1)} %copy.115, f32[2,64,16,128]{3,2,1,0:T(8,128)S(1)} %fusion.74), kind=kOutput, calls=%fused_computation.101 | convolution fusion | flops 202899456 | bytes 2646016 | tf_op jit(solution)/shard_map/vmap(thk,shk->hts)/dot_general | solution.py:79
  21.8 1.2 fusion.110
  23.0 1.2 fusion.111
  24.2 1.2 fusion.89
  25.4 1.2 fusion.112
  26.6 1.2 fusion.87
  27.8 1.2 fusion.113
  29.0 1.2 fusion.85
  30.2 1.2 convolution_add_fusion.3
  31.4 2.2 fusion.83
  36.1 1.6 reduce_sum.84
  38.2 1.4 copy.153
  40.8 1.9 fusion.79
  42.7 1.4 fusion.77
  44.2 2.9 %convolution_select_fusion = f32[2,16,64,64]{3,2,1,0:T(8,128)S(1)} fusion(pred[2,64,64]{2,1,0:T(8,128)(4,1)S(1)} %get-tuple-element.954, f32[2,64,16,128]{3,2,1,0:T(8,128)S(1)} %bitcast.231, f32[2,64,16]{1,2,0:T(8,128)S(1)} %copy.124, f32[2,64,16,128]{3,2,1,0:T(8,128)S(1)} %fusion.74, f32[2,64,16,128]{3,2,1,0:T(8,128)S(1)} %bitcast.228, ...), kind=kOutput, calls=%fused_computation.99 | convolution fusion | flops 202768384 | bytes 3694592 | tf_op jit(solution)/shard_map/vmap(thk,shk->hts)/dot_general | solution.py:90
  47.1 2.2 fusion.115
  49.3 3.0 %convolution_subtract_fusion = f32[2,16,64,128]{3,2,1,0:T(8,128)} fusion(f32[2,16,64,64]{3,2,1,0:T(8,128)S(1)} %convolution_select_fusion, f32[2,16,64,128]{3,2,1,0:T(8,128)S(1)} %fusion.79, f32[2,64]{1,0:T(2,128)S(1)} %get-tuple-element.957, f32[2,64,16]{1,2,0:T(8,128)S(1)} %copy.124, f32[2,64,16,128]{3,2,1,0:T(8,128)S(1)} %bitcast.232, ...), kind=kOutput, calls=%fused_computation.97 | convolution fusion | flops 202375168 | bytes 4727296 | tf_op jit(solution)/shard_map/vmap(hts,hsk->htk)/dot_general | solution.py:94
  53.2 5.6 %fusion.102 = f32[2,16,128,128]{3,2,1,0:T(8,128)} fusion(f32[2,16,64,128]{3,2,1,0:T(8,128)S(1)} %fusion.77, f32[2,64,16,128]{3,2,1,0:T(8,128)S(1)} %fusion.74, f32[2,64,16,128]{3,2,1,0:T(8,128)S(1)} %bitcast.229, f32[2,64]{1,0:T(2,128)S(1)} %get-tuple-element.956, f32[2,16,128]{2,1,0:T(8,128)S(1)} %slice_bitcast_fusion, f32[2,64,16]{1,2,0:T(8,128)S(1)} %copy.115), kind=kOutput, calls=%fused_computation.147 | convolution fusion | flops 403701760 | bytes 5267968 | tf_op jit(solution)/shard_map/vmap(omt,mor->mtr)/dot_general | solution.py:106
  58.8 5.9 %multiply_subtract_fusion = f32[2,16,128,128]{3,2,1,0:T(8,128)S(1)} fusion(f32[2,16,64,128]{3,2,1,0:T(8,128)S(1)} %fusion.79, f32[128,128]{1,0:T(8,128)S(1)} %fusion.103, f32[2,16,128]{2,1,0:T(8,128)S(1)} %bitcast.245, f32[2]{0:T(128)S(1)} %slice_reduce_fusion.1, f32[2,64,16,128]{3,2,1,0:T(8,128)S(1)} %fusion.74, f32[2,64,16,128]{3,2,1,0:T(8,128)} %bitcast.230, ...), kind=kOutput, calls=%fused_computation.94 | convolution fusion | flops 405274624 | bytes 5349896 | tf_op jit(solution)/shard_map/vmap(shk,hsj->hkj)/dot_general | solution.py:103
  64.8 20.9 %while.55 = (s32[]{:T(128)}, f32[16,128,128]{2,1,0:T(8,128)S(1)}, f32[16,128,128]{2,1,0:T(8,128)}, f32[2,16,64,128]{3,2,0,1:T(8,128)}, f32[2,16,64,128]{3,2,0,1:...) while((s32[]{:T(128)}, f32[16,128,128]{2,1,0:T(8,128)S(1)}, ...), condition=%wide.region_7.8_spmd.clone, body=%wide.region_6.7_spmd.clone.sunk | while | flops 1208877056 | bytes 41422084 | solution.py:185
  65.0 1.4 copy.273
  66.8 1.9 fusion.178
  68.7 2.1 convolution_add_fusion.7
  75.4 1.4 copy.273
  77.2 1.9 fusion.178
  79.1 2.1 convolution_add_fusion.7
  88.6 1.7 copy.129
  92.8 2.0 fusion.106
  96.5 14.0 %conditional.2 = (f32[16,128]{1,0:T(8,128)}, f32[16,128]{1,0:T(8,128)}, f32[128,16,128]{0,2,1:T(8,128)}) conditional(s32[]{:T(128)} %convert_element_type.143, () %tuple.66, (s32[]{:T(128)}, s32[128]{0:T(128)}, s32[8]{0:T(128)}, s32[128]{0:T(128)}, bf16[128,576]{0,1:T(8,128)(2,1)}, /*index=5*/bf16[512,2048]{1,0:T(8,128)(2,1)S(1)}, ...), branch_computations={%region_11.12_spmd, %region_12.16_spmd} | conditional | flops 708111488 | bytes 26063560 | solution.py:247
  99.0 1.4 fusion.9
  100.5 1.5 fusion.108
  102.6 1.3 convolution_convert_fusion
  103.9 2.1 copy.137
  105.9 2.4 fusion.5
  109.2 1.3 fusion.23
  110.5 76.1 %while.56 = (s32[]{:T(128)}, f32[16,128]{1,0:T(8,128)}, f32[16,128]{1,0:T(8,128)}, f32[128,16,128]{0,2,1:T(8,128)}, bf16[128,576]{0,1:T(8,128)(2,1)}, /*index=5*...) while((s32[]{:T(128)}, f32[16,128]{1,0:T(8,128)}, ...), condition=%wide.region_22.23_spmd.clone.clone, body=%wide.region_16.22_spmd.clone.clone.sunk | while | flops 708371712 | bytes 27482712 | solution.py:265
  110.5 1.3 collective-permute-start
  113.1 4.3 %collective-permute-done = bf16[128,576]{0,1:T(8,128)(2,1)S(1)} collective-permute-done((bf16[128,576]{0,1:T(8,128)(2,1)}, bf16[128,576]{0,1:T(8,128)(2,1)S(1)}, u32[]{:S(2)}, u32[]{:S(2)}) %collective-permute-start) | collective-permute-done | bytes 147488 | tf_op jit(solution)/shard_map/while/body/eval_jaxpr/ppermute | solution.py:42
  117.3 12.5 %conditional.6 = ((f32[16,128]{1,0:T(8,128)}, f32[16,128]{1,0:T(8,128)}, f32[128,16,128]{0,2,1:T(8,128)})) conditional(s32[]{:T(128)} %convert_element_type.183, (f32[16,128]{1,0:T(8,128)}, f32[16,128]{1,0:T(8,128)}, f32[128,16,128]{0,2,1:T(8,128)}) %tuple.130, (s32[]{:T(128)}, s32[]{:T(128)}, s32[8]{0:T(128)}, s32[128]{0:T(128)}, ...), branch_computations={%region_17.17_spmd, %region_18.21_spmd} | conditional | flops 708371712 | bytes 26597076 | solution.py:247
  120.2 1.4 fusion.42
  121.6 1.3 convolution_convert_fusion.2
  122.9 2.0 copy.138
  125.0 2.7 %fusion.25 = f32[128,16,128]{0,2,1:T(8,128)} fusion(bf16[128,16,128]{0,2,1:T(8,128)(2,1)} %bitcast.225, f32[128,16,128]{0,2,1:T(8,128)} %get-tuple-element.623, f32[16,128,128]{1,2,0:T(8,128)S(1)} %get-tuple-element.946, f32[128,16]{0,1:T(8,128)} %get-tuple-element.943, f32[16,128]{1,0:T(8,128)} %get-tuple-element.1141, pred[128,128]{0,1:T(8,128)(4,1)} %copy-done.9), kind=kOutput, calls=%fused_computation.39 | convolution fusion | flops 68419584 | bytes 3702784 | tf_op jit(solution)/shard_map/while/body/eval_jaxpr/cond/branch_1_fun/hts,shv->thv/dot_general | solution.py:238
  127.9 1.3 multiply_add_fusion
  130.5 1.3 collective-permute-start
  133.0 7.9 %collective-permute-done = bf16[128,576]{0,1:T(8,128)(2,1)S(1)} collective-permute-done((bf16[128,576]{0,1:T(8,128)(2,1)}, bf16[128,576]{0,1:T(8,128)(2,1)S(1)}, u32[]{:S(2)}, u32[]{:S(2)}) %collective-permute-start) | collective-permute-done | bytes 147488 | tf_op jit(solution)/shard_map/while/body/eval_jaxpr/ppermute | solution.py:42
  141.6 1.3 collective-permute-start
  144.1 20.2 %collective-permute-done = bf16[128,576]{0,1:T(8,128)(2,1)S(1)} collective-permute-done((bf16[128,576]{0,1:T(8,128)(2,1)}, bf16[128,576]{0,1:T(8,128)(2,1)S(1)}, u32[]{:S(2)}, u32[]{:S(2)}) %collective-permute-start) | collective-permute-done | bytes 147488 | tf_op jit(solution)/shard_map/while/body/eval_jaxpr/ppermute | solution.py:42
  165.0 1.3 collective-permute-start
  167.5 18.4 %collective-permute-done = bf16[128,576]{0,1:T(8,128)(2,1)S(1)} collective-permute-done((bf16[128,576]{0,1:T(8,128)(2,1)}, bf16[128,576]{0,1:T(8,128)(2,1)S(1)}, u32[]{:S(2)}, u32[]{:S(2)}) %collective-permute-start) | collective-permute-done | bytes 147488 | tf_op jit(solution)/shard_map/while/body/eval_jaxpr/ppermute | solution.py:42
  186.6 1.4 divide_convert_fusion
  189.0 53.6 %all-gather.7.cloned.1.call-done = bf16[128,128,128]{2,1,0:T(8,128)(2,1)} async-done(((bf16[16,128,128]{2,1,0:T(8,128)(2,1)}), bf16[128,128,128]{2,1,0:T(8,128)(2,1)}) %all-gather.7.cloned.1.call-update) | async-done | bytes 4194320 | tf_op jit(solution)/shard_map/all_gather | solution.py:20
  242.7 14.3 %while.54 = (s32[]{:T(128)}, f32[16,128,128]{2,1,0:T(8,128)S(1)}, s32[]{:T(128)}, bf16[8,16,128,128]{3,2,1,0:T(8,128)(2,1)}, bf16[8,16,128,128]{3,2,1,0:T(8,128)(2,1)}, /*index=5*/s32[]{:T(128)}, s32[]{:T(128)}, s32[]{:T(128)}) while((s32[]{:T(128)}, f32[16,128,128]{2,1,0:T(8,128)S(1)}, s32[]{:T(128)}, bf16[8,16,128,128]{3,2,1,0:T(8,128)(2,1)}, ...), condition=%wide.region_9.10_spmd, body=%wide.region_8.9_spmd.sunk | while | flops 403177472 | bytes 5244023 | solution.py:36
  242.8 2.0 convolution_add_fusion.6
  244.9 1.9 convolution_add_fusion.6
  246.9 1.9 convolution_add_fusion.6
  249.0 1.9 convolution_add_fusion.6
  251.0 1.9 convolution_add_fusion.6
  253.0 1.9 convolution_add_fusion.6
  255.0 1.9 convolution_add_fusion.6
  (176 shorter events, 40.4 us)
Async XLA Ops:
  7.2 3.1 %copy-start.18 = (bf16[128,2048]{1,0:T(8,128)(2,1)S(1)}, bf16[128,2048]{1,0:T(8,128)(2,1)}, u32[]{:S(2)}) copy-start(bf16[128,2048]{1,0:T(8,128)(2,1)} %param.20) | copy-start | bytes 1572868
  7.2 2.9 %copy-start.17 = (bf16[128,2048]{1,0:T(8,128)(2,1)S(1)}, bf16[128,2048]{1,0:T(8,128)(2,1)}, u32[]{:S(2)}) copy-start(bf16[128,2048]{1,0:T(8,128)(2,1)} %param.21) | copy-start | bytes 1572868
  7.2 181.8 %all-gather.5.cloned.1.call-start = ((), (), s32[]{:S(2)}) async-start(), calls=%async_computation | async-start | bytes 4718592 | tf_op jit(solution)/shard_map/all_gather | solution.py:20
  8.9 79.1 %copy-start.30 = (s32[128]{0:T(128)}, s32[128]{0:T(128)S(1)}, u32[]{:S(2)}) copy-start(s32[128]{0:T(128)S(1)} %iota_add_fusion.2) | copy-start | bytes 1540
  10.1 2.3 copy-start.24
  12.7 1.5 copy-start.31
  12.7 2.4 copy-start.29
  14.4 0.5 copy-start.32
  14.5 0.6 copy-start.28
  18.6 34.6 %copy-start.3 = (f32[16,8,16,128]{3,2,1,0:T(8,128)}, f32[16,8,16,128]{3,2,1,0:T(8,128)S(1)}, u32[]{:S(2)}) copy-start(f32[16,8,16,128]{3,2,1,0:T(8,128)S(1)} %copy.150) | copy-start | bytes 3145732
  31.4 2.2 copy-start.25
  33.6 1.3 copy-start.15
  37.8 1.9 copy-start.13
  40.8 1.9 copy-start.14
  65.0 1.5 copy-start.5
  65.0 1.8 copy-start.8
  65.0 3.7 %copy-start.6 = (f32[2,16,128,128]{3,2,1,0:T(8,128)S(1)}, f32[2,16,128,128]{3,2,1,0:T(8,128)}, u32[]{:S(2)}) copy-start(f32[2,16,128,128]{3,2,1,0:T(8,128)} %get-tuple-element.1172) | copy-start | bytes 6291460 | tf_op jit(solution)/shard_map/while
  70.8 1.2 copy-start.20
  73.1 1.1 copy-start.21
  75.3 1.5 copy-start.5
  75.4 1.8 copy-start.8
  75.4 3.7 %copy-start.6 = (f32[2,16,128,128]{3,2,1,0:T(8,128)S(1)}, f32[2,16,128,128]{3,2,1,0:T(8,128)}, u32[]{:S(2)}) copy-start(f32[2,16,128,128]{3,2,1,0:T(8,128)} %get-tuple-element.1172) | copy-start | bytes 6291460 | tf_op jit(solution)/shard_map/while
  81.2 1.2 copy-start.20
  83.5 1.1 copy-start.21
  85.7 1.4 copy-start.4
  86.6 155.9 %all-gather.7.cloned.1.call-start = ((), (), s32[]{:S(2)}) async-start(), calls=%async_computation.1 | async-start | bytes 4718592 | tf_op jit(solution)/shard_map/all_gather | solution.py:20
  88.6 7.9 %copy-start = (bf16[512,2048]{1,0:T(8,128)(2,1)S(1)}, bf16[512,2048]{1,0:T(8,128)(2,1)}, u32[]{:S(2)}) copy-start(bf16[512,2048]{1,0:T(8,128)(2,1)} %param.27) | copy-start | bytes 6291460
  90.3 0.9 copy-start.16
  96.5 3.9 %copy-start.12 = (bf16[128,16,128]{0,2,1:T(8,128)(2,1)}, bf16[128,16,128]{0,2,1:T(8,128)(2,1)S(1)}, u32[]{:S(2)}) copy-start(bf16[128,16,128]{0,2,1:T(8,128)(2,1)S(1)} %get-tuple-element.865) | copy-start | bytes 1572868 | tf_op jit(solution)/shard_map/cond
  98.0 4.0 %copy-start.26 = (pred[128,128]{0,1:T(8,128)(4,1)}, pred[128,128]{0,1:T(8,128)(4,1)S(1)}, u32[]{:S(2)}) copy-start(pred[128,128]{0,1:T(8,128)(4,1)S(1)} %compare_and_fusion) | copy-start | bytes 49156 | tf_op jit(solution)/shard_map/cond
  100.4 2.2 copy-start.1
  100.4 2.2 copy-start.19
  103.9 4.4 %copy-start.27 = (pred[128,128]{0,1:T(8,128)(4,1)S(1)}, pred[128,128]{0,1:T(8,128)(4,1)}, u32[]{:S(2)}) copy-start(pred[128,128]{0,1:T(8,128)(4,1)} %copy-done.26) | copy-start | bytes 49156 | tf_op jit(solution)/shard_map/cond
  110.5 6.8 %collective-permute-start = (bf16[128,576]{0,1:T(8,128)(2,1)}, bf16[128,576]{0,1:T(8,128)(2,1)S(1)}, u32[]{:S(2)}, u32[]{:S(2)}) collective-permute-start(bf16[128,576]{0,1:T(8,128)(2,1)} %get-tuple-element.1228), channel_id=1, source_target_pairs={{0,4},{4,8},{8,12},{12,16},{16,20},{20,24},{24,28},{1,5},{5,9},{9,... | collective-permute-start | bytes 442376 | tf_op jit(solution)/shard_map/while/body/eval_jaxpr/ppermute | solution.py:42
  117.3 2.4 copy-start.7
  118.9 1.3 copy-start.9
  119.7 1.9 copy-start.2
  125.0 2.7 %copy-start.10 = (pred[128,128]{0,1:T(8,128)(4,1)S(1)}, pred[128,128]{0,1:T(8,128)(4,1)}, u32[]{:S(2)}) copy-start(pred[128,128]{0,1:T(8,128)(4,1)} %copy-done.9) | copy-start | bytes 49156 | tf_op jit(solution)/shard_map/while/body/eval_jaxpr/cond
  125.0 2.7 %copy-start.11 = (f32[16,128]{1,0:T(8,128)S(1)}, f32[16,128]{1,0:T(8,128)}, u32[]{:S(2)}) copy-start(f32[16,128]{1,0:T(8,128)} %get-tuple-element.1141) | copy-start | bytes 24580 | tf_op jit(solution)/shard_map/while/body/eval_jaxpr/cond
  130.5 10.4 %collective-permute-start = (bf16[128,576]{0,1:T(8,128)(2,1)}, bf16[128,576]{0,1:T(8,128)(2,1)S(1)}, u32[]{:S(2)}, u32[]{:S(2)}) collective-permute-start(bf16[128,576]{0,1:T(8,128)(2,1)} %get-tuple-element.1228), channel_id=1, source_target_pairs={{0,4},{4,8},{8,12},{12,16},{16,20},{20,24},{24,28},{1,5},{5,9},{9,... | collective-permute-start | bytes 442376 | tf_op jit(solution)/shard_map/while/body/eval_jaxpr/ppermute | solution.py:42
  141.6 22.7 %collective-permute-start = (bf16[128,576]{0,1:T(8,128)(2,1)}, bf16[128,576]{0,1:T(8,128)(2,1)S(1)}, u32[]{:S(2)}, u32[]{:S(2)}) collective-permute-start(bf16[128,576]{0,1:T(8,128)(2,1)} %get-tuple-element.1228), channel_id=1, source_target_pairs={{0,4},{4,8},{8,12},{12,16},{16,20},{20,24},{24,28},{1,5},{5,9},{9,... | collective-permute-start | bytes 442376 | tf_op jit(solution)/shard_map/while/body/eval_jaxpr/ppermute | solution.py:42
  165.0 21.0 %collective-permute-start = (bf16[128,576]{0,1:T(8,128)(2,1)}, bf16[128,576]{0,1:T(8,128)(2,1)S(1)}, u32[]{:S(2)}, u32[]{:S(2)}) collective-permute-start(bf16[128,576]{0,1:T(8,128)(2,1)} %get-tuple-element.1228), channel_id=1, source_target_pairs={{0,4},{4,8},{8,12},{12,16},{16,20},{20,24},{24,28},{1,5},{5,9},{9,... | collective-permute-start | bytes 442376 | tf_op jit(solution)/shard_map/while/body/eval_jaxpr/ppermute | solution.py:42
  242.6 14.3 %copy-start.22 = (f32[2,16,64,128]{3,2,0,1:T(8,128)S(1)}, f32[2,16,64,128]{3,2,0,1:T(8,128)}, u32[]{:S(2)}) copy-start(f32[2,16,64,128]{3,2,0,1:T(8,128)} %get-tuple-element.660) | copy-start | bytes 3145732
  242.7 14.3 %copy-start.23 = (f32[2,16,64,128]{3,2,0,1:T(8,128)S(1)}, f32[2,16,64,128]{3,2,0,1:T(8,128)}, u32[]{:S(2)}) copy-start(f32[2,16,64,128]{3,2,0,1:T(8,128)} %get-tuple-element.656) | copy-start | bytes 3145732
Sparse Core Ops, SparseCore 0:
  86.8 74.6 all-gather.4
  163.6 78.9 all-gather.6
where the time goes:
time: 270 us; the launch traced here: 266 us
  waiting for transfers between devices  104 us (39%)
  matrix products  78.6 us (29%)
  local copies, waits for them, and re-layouts  34.6 us (13%)
  other arithmetic  21.4 us (8%)
  between operations  16.4 us (6%)
  loops' own time  5.77 us (2%)
  starting transfers between devices  5.2 us (2%)
    all_gather x2, waiting for transfers between devices, prefix(): lax.all_gather(a.astype(kind), axis)  53.6 us
    ppermute x4, waiting for transfers between devices, shifted(): return lax.ppermute(block, axis, route)  50.8 us
    dot_general x7, matrix products, compose(): jnp.einsum('ytn,yne->yte', successor_slab[0], prior_slab[1], precision=PR...  13.3 us
    unnamed x46, local copies, waits for them, and re-layouts  12.1 us
    while x35, local copies, waits for them, and re-layouts  11.5 us
    dot_general x5, matrix products, unit_lower_inverse(): jnp.einsum('hij,hjk->hik', result, identity + power_term, precision=PRECI...  6.97 us
    dot_general x5, matrix products, unit_lower_inverse(): jnp.einsum('hij,hjk->hik', power_term, power_term, precision=PRECISE_PROD...  5.97 us
    dot_general x1, matrix products, block_terms(): jnp.einsum('shk,hsj->hkj', key_trailing, solved_key, precision=PRECISE_PR...  5.88 us
  transfers between devices with their start and end apart: 6, of which 5 were waited for; matrix products, arithmetic and copies ran while one was open for 14% of the time, Pallas kernels for 0%

commit v1 on v0

v1 whole, which is shorter than its diff:
```python
import functools
import math

import jax
import jax.numpy as jnp
import numpy as np
from jax import lax
from jax.experimental import pallas as pl
from jax.experimental.pallas import tpu as pltpu
from jax.sharding import PartitionSpec as P

NOPE = 128
ROPE = 64
LATENT = 512
GROUP = 4
VMEM = 32 * 1024 * 1024
BF = jnp.bfloat16
F32 = jnp.float32
NEG = -1e30


def mm(a, b):
    return jnp.dot(a, b, preferred_element_type=F32)


def mm_nt(a, b):
    return lax.dot_general(a, b, (((1,), (1,)), ((), ())), preferred_element_type=F32)


def mm_tn(a, b):
    return lax.dot_general(a, b, (((0,), (0,)), ((), ())), preferred_element_type=F32)


def doc_of(places, starts_ref, base, ndocs):
    total = jnp.zeros(jnp.shape(places), jnp.int32)
    for j in range(ndocs):
        total = total + (starts_ref[base + j] <= places).astype(jnp.int32)
    return total - 1


def kda_kernel(ndocs, sc, q_ref, k_ref, v_ref, g_ref, b_ref, mu_ref, qe_ref, lo_ref):
    rows = q_ref.shape[0]
    half = rows // 2
    heads = q_ref.shape[1] // 128
    group = sc[0] + pl.program_id(0)
    first = sc[1]
    ri = lax.broadcasted_iota(jnp.int32, (rows, rows), 0)
    ci = lax.broadcasted_iota(jnp.int32, (rows, rows), 1)
    doc_r = doc_of(first + ri, sc, 2, ndocs)
    doc_c = doc_of(first + ci, sc, 2, ndocs)
    prev = doc_of(first - 1, sc, 2, ndocs)
    last = doc_of(first + rows - 1, sc, 2, ndocs)
    same = doc_r == doc_c
    strict = same & (ri > ci)
    causal = same & (ri >= ci)
    follow = (doc_r == prev).astype(F32)
    tail = (doc_r == last).astype(F32)
    keep = (last == prev).astype(F32)
    eye = (ri == ci).astype(F32)
    tri = (ri >= ci).astype(BF)
    low = ci < half
    cum_all = mm(tri, g_ref[...])
    gains = b_ref[...]
    gain_lane = lax.broadcasted_iota(jnp.int32, gains.shape, 1)

    hs = range(heads)
    lhs, km, lhs_off, km_off, rhs, kt, qg, gl, gain = [], [], [], [], [], [], [], [], []
    for h in hs:
        cols = slice(h * 128, (h + 1) * 128)
        q = q_ref[:, cols].astype(F32)
        k = k_ref[:, cols].astype(F32)
        v = v_ref[:, cols].astype(F32)
        qn = q * lax.rsqrt(jnp.sum(q * q, axis=1, keepdims=True) + 1e-06)
        kn = k * lax.rsqrt(jnp.sum(k * k, axis=1, keepdims=True) + 1e-06)
        cum = cum_all[:, cols]
        b = jnp.sum(
            jnp.where(gain_lane == group * heads + h, gains, 0.0), axis=1, keepdims=True
        )
        quarter = half // 2
        m0 = cum[quarter - 1 : quarter]
        m1 = cum[half + quarter - 1 : half + quarter]
        mid = cum[half - 1 : half]
        end = cum[rows - 1 : rows]
        c0, c1 = cum[:half], cum[half:]
        dp = jnp.concatenate([jnp.exp(c0 - m0), jnp.exp(c1 - m1)], axis=0)
        dm = jnp.concatenate([jnp.exp(m0 - c0), jnp.exp(m1 - c1)], axis=0)
        op = jnp.exp(c1 - mid)
        om = jnp.exp(jnp.minimum(mid - cum, 0.0))
        growth = jnp.exp(cum)
        trail = jnp.exp(end - cum)
        lhs.append(jnp.concatenate([(kn * dp).astype(BF), (qn * dp).astype(BF)], axis=0))
        km.append((kn * dm).astype(BF))
        lhs_off.append(
            jnp.concatenate([(kn[half:] * op).astype(BF), (qn[half:] * op).astype(BF)], axis=0)
        )
        km_off.append((kn * om).astype(BF))
        rhs.append(
            jnp.concatenate([(kn * growth * (b * follow)).astype(BF), (v * b).astype(BF)], axis=1)
        )
        kt.append((kn * trail * tail).astype(BF))
        qg.append(qn * growth * follow)
        gl.append(jnp.exp(end) * keep)
        gain.append(b)

    a, mix = [], []
    for h in hs:
        p = mm_nt(lhs[h], km[h])
        o = mm_nt(lhs_off[h], km_off[h])
        pa, pq = p[:rows], p[rows:]
        pa = jnp.concatenate([pa[:half], jnp.where(low[half:], o[:half], pa[half:])], axis=0)
        pq = jnp.concatenate([pq[:half], jnp.where(low[half:], o[half:], pq[half:])], axis=0)
        a.append(jnp.where(strict, pa, 0.0) * gain[h])
        mix.append(jnp.where(causal, pq, 0.0).astype(BF))

    t = [eye - jnp.where((ri >> 1) == (ci >> 1), a[h], 0.0) for h in hs]
    shift = 1
    while (2 << shift) <= rows:
        level = ((ri >> (shift + 1)) == (ci >> (shift + 1))) & ((ri >> shift) != (ci >> shift))
        tb = [t[h].astype(BF) for h in hs]
        x = [mm(jnp.where(level, a[h], 0.0).astype(BF), tb[h]).astype(BF) for h in hs]
        t = [t[h] - mm(tb[h], x[h]) for h in hs]
        shift += 1

    wu = [mm(t[h].astype(BF), rhs[h]).astype(BF) for h in hs]
    for h in hs:
        cols = slice(h * 128, (h + 1) * 128)
        z = mm_tn(kt[h], wu[h])
        mu_ref[h, :, :128] = (eye * gl[h] - z[:, :128]).astype(BF)
        mu_ref[h, :, 128:] = z[:, 128:].astype(BF)
        y = mm(mix[h], wu[h])
        qe_ref[:, cols] = (qg[h] - y[:, :128]).astype(BF)
        lo_ref[:, cols] = y[:, 128:]


def kda_local(scalars, q, k, v, g, b, groups, ndocs):
    rows, width = q.shape[0], GROUP * 128
    heads = b.shape[1]
    wide = pl.BlockSpec((rows, width), lambda i, sc: (0, sc[0] + i))
    out_wide = pl.BlockSpec((rows, width), lambda i, sc: (0, i))
    return pl.pallas_call(
        functools.partial(kda_kernel, ndocs),
        grid_spec=pltpu.PrefetchScalarGridSpec(
            num_scalar_prefetch=1,
            grid=(groups,),
            in_specs=[wide, wide, wide, wide, pl.BlockSpec((rows, heads), lambda i, sc: (0, 0))],
            out_specs=[
                pl.BlockSpec((GROUP, 128, 256), lambda i, sc: (i, 0, 0)),
                out_wide,
                out_wide,
            ],
        ),
        out_shape=[
            jax.ShapeDtypeStruct((groups * GROUP, 128, 256), BF),
            jax.ShapeDtypeStruct((rows, groups * width), BF),
            jax.ShapeDtypeStruct((rows, groups * width), F32),
        ],
        compiler_params=pltpu.CompilerParams(vmem_limit_bytes=VMEM),
        cost_estimate=pl.CostEstimate(
            flops=groups * GROUP * 2 * 128**3 * 22,
            bytes_accessed=groups * width * rows * 16,
            transcendentals=0,
        ),
        name="kda_slab",
    )(scalars, q, k, v, g, b)


def pair_kernel(sc, own_ref, got_ref, pm_ref, pu_ref):
    def go(first_ref, second_ref):
        for h in range(own_ref.shape[0]):
            z = mm(second_ref[h, :, :128], first_ref[h])
            pm_ref[h] = z[:, :128].astype(BF)
            pu_ref[h] = (z[:, 128:] + second_ref[h, :, 128:].astype(F32)).astype(BF)

    @pl.when(sc[0] == 0)
    def _():
        go(own_ref, got_ref)

    @pl.when(sc[0] != 0)
    def _():
        go(got_ref, own_ref)


def arrived(sc, a_ref, b_ref, h):
    x = jnp.where(sc[2] == 1, a_ref[h].astype(F32), b_ref[h].astype(F32))
    return jnp.where(sc[1] == 1, 0.0, x).astype(BF)


def step_kernel(sc, pm_ref, pu_ref, a_ref, b_ref, out_ref):
    for h in range(pm_ref.shape[0]):
        x = arrived(sc, a_ref, b_ref, h)
        out_ref[h] = (mm(pm_ref[h], x) + pu_ref[h].astype(F32)).astype(BF)


def split_kernel(sc, own_ref, got_ref, a_ref, b_ref, mine_ref, send_ref):
    def go(mu_ref, plain_ref, moved_ref):
        for h in range(own_ref.shape[0]):
            x = arrived(sc, a_ref, b_ref, h)
            plain_ref[h] = x
            moved_ref[h] = (mm(mu_ref[h, :, :128], x) + mu_ref[h, :, 128:].astype(F32)).astype(BF)

    @pl.when(sc[0] == 0)
    def _():
        go(own_ref, mine_ref, send_ref)

    @pl.when(sc[0] != 0)
    def _():
        go(got_ref, send_ref, mine_ref)


def whole_call(kernel, name, scalars, args, outs):
    def full(shape):
        return pl.BlockSpec(shape, lambda i, sc, n=len(shape): (0,) * n)

    return pl.pallas_call(
        kernel,
        grid_spec=pltpu.PrefetchScalarGridSpec(
            num_scalar_prefetch=1,
            grid=(1,),
            in_specs=[full(x.shape) for x in args],
            out_specs=[full(o) for o in outs],
        ),
        out_shape=[jax.ShapeDtypeStruct(o, BF) for o in outs],
        compiler_params=pltpu.CompilerParams(vmem_limit_bytes=VMEM),
        name=name,
    )(scalars, *args)


def final_kernel(sc, qe_ref, lo_ref, s_ref, *rest):
    out_ref = rest[-1]
    for h in range(s_ref.shape[0]):
        cols = slice(h * 128, (h + 1) * 128)
        out_ref[:, cols] = (lo_ref[:, cols] + mm(qe_ref[:, cols], s_ref[h])).astype(BF)


def final(block, qe, lo, s, heads, previous):
    rows = qe.shape[0]
    half = s.shape[0]
    wide = pl.BlockSpec((rows, half * 128), lambda i, sc: (0, 0))
    args = [qe, lo, s]
    specs = [wide, wide, pl.BlockSpec(s.shape, lambda i, sc: (0, 0, 0))]
    aliases = {}
    if previous is not None:
        args.append(previous)
        specs.append(pl.BlockSpec(memory_space=pl.ANY))
        aliases = {4: 0}
    return pl.pallas_call(
        final_kernel,
        grid_spec=pltpu.PrefetchScalarGridSpec(
            num_scalar_prefetch=1,
            grid=(1,),
            in_specs=specs,
            out_specs=pl.BlockSpec((rows, half * 128), lambda i, sc: (0, sc[0])),
        ),
        out_shape=jax.ShapeDtypeStruct((rows, heads * 128), BF),
        input_output_aliases=aliases,
        compiler_params=pltpu.CompilerParams(vmem_limit_bytes=VMEM),
        name="kda_out",
    )(block, *args)


def mla_kernel(ndocs, n, window, has_previous, sc, *refs):
    q_ref, ku_ref, vu_ref = refs[:3]
    blocks = refs[3 : 3 + n]
    out_ref, lat_ref, bias_ref = refs[3 + n + int(has_previous) :]
    rows = q_ref.shape[0]
    keys = window * rows

    @pl.when(pl.program_id(0) == 0)
    def _():
        lat_ref[...] = jnp.zeros_like(lat_ref)
        for m in range(n):
            slot = sc[1 + m]

            @pl.when(slot >= 0)
            def _():
                lat_ref[pl.ds(pl.multiple_of(slot * rows, rows), rows), :] = blocks[m][...]

        here = sc[0] + lax.broadcasted_iota(jnp.int32, (rows, 1), 0)
        there = sc[0] - keys + rows + lax.broadcasted_iota(jnp.int32, (1, keys), 1)
        doc_q = doc_of(here, sc, 1 + n, ndocs)
        doc_k = doc_of(there, sc, 1 + n, ndocs)
        bias_ref[...] = jnp.where((there <= here) & (doc_q == doc_k), 0.0, NEG)

    factor = math.log2(math.e) / math.sqrt(NOPE + ROPE)
    lat = lat_ref[:, :LATENT]
    rope = lat_ref[:, LATENT:]
    kn = mm(lat, ku_ref[...]).astype(BF)
    vals = mm(lat, vu_ref[...]).astype(BF)
    bias = bias_ref[...]
    for h in range(out_ref.shape[1] // 128):
        cols = slice(h * 128, (h + 1) * 128)
        q = q_ref[:, h * (NOPE + ROPE) : (h + 1) * (NOPE + ROPE)]
        s = mm_nt(q, jnp.concatenate([kn[:, cols], rope], axis=1)) * factor + bias
        w = jnp.exp2(s - jnp.max(s, axis=1, keepdims=True))
        total = jnp.sum(w, axis=1, keepdims=True)
        out_ref[:, cols] = (mm(w.astype(BF), vals[:, cols]) / total).astype(BF)


def mla(scalars, q, ku, vu, blocks, window, ndocs, first, groups, previous):
    rows = q.shape[0]
    n = len(blocks)
    heads = ku.shape[1] // NOPE
    qw, w = GROUP * (NOPE + ROPE), GROUP * 128
    keys = window * rows
    args = [q, ku, vu, *blocks]
    specs = [
        pl.BlockSpec((rows, qw), lambda i, sc: (0, first + i)),
        pl.BlockSpec((LATENT, w), lambda i, sc: (0, first + i)),
        pl.BlockSpec((LATENT, w), lambda i, sc: (0, first + i)),
    ] + [pl.BlockSpec(x.shape, lambda i, sc: (0, 0)) for x in blocks]
    aliases = {}
    if previous is not None:
        args.append(previous)
        specs.append(pl.BlockSpec(memory_space=pl.ANY))
        aliases = {len(args): 0}
    return pl.pallas_call(
        functools.partial(mla_kernel, ndocs, n, window, previous is not None),
        grid_spec=pltpu.PrefetchScalarGridSpec(
            num_scalar_prefetch=1,
            grid=(groups,),
            in_specs=specs,
            out_specs=pl.BlockSpec((rows, w), lambda i, sc: (0, first + i)),
            scratch_shapes=[
                pltpu.VMEM((keys, LATENT + ROPE), BF),
                pltpu.VMEM((rows, keys), F32),
            ],
        ),
        out_shape=jax.ShapeDtypeStruct((rows, heads * 128), BF),
        input_output_aliases=aliases,
        compiler_params=pltpu.CompilerParams(vmem_limit_bytes=VMEM),
        cost_estimate=pl.CostEstimate(
            flops=2 * keys * groups * w * (2 * LATENT + 3 * rows),
            bytes_accessed=groups * w * 3000,
            transcendentals=0,
        ),
        name="mla_heads",
    )(scalars, *args)


def repaired(n, wanted):
    left = [i for i in range(n) if i not in wanted]
    out = dict(wanted)
    for a, b in zip(left[::2], left[1::2]):
        out[a], out[b] = b, a
    return [out[i] for i in range(n)]


def routes(n):
    reach = n // 2
    tables = []
    for m in range(1, n):
        tables.append(repaired(n, {i: i ^ m for i in range(n) if abs(i - (i ^ m)) <= reach}))
    up = repaired(n, {i: i ^ 2 for i in range(n)})
    middle = {}
    for pair in range(1, n // 2 - 1, 2):
        for c in range(2):
            middle[2 * pair + c], middle[2 * pair + 2 + c] = 2 * pair + 2 + c, 2 * pair + c
    return tables, up, repaired(n, middle)


def swap(x, table):
    return lax.ppermute(x, "ctx", list(enumerate(table)))


def local(
    kda_query,
    kda_key,
    kda_value,
    log_decay,
    write_rate,
    mla_query,
    latents,
    key_up,
    value_up,
    doc_lengths,
):
    rows = latents.shape[0]
    heads = write_rate.shape[1]
    n = lax.axis_size("ctx")
    ndocs = doc_lengths.shape[0]
    place = lax.axis_index("ctx")
    first_row = place * rows
    starts = (jnp.cumsum(doc_lengths) - doc_lengths).astype(jnp.int32)
    tables, up, middle = routes(n)
    partner = [i ^ 1 for i in range(n)]
    reach = n // 2
    window = reach + 1
    column = place % 2
    pair = place // 2
    half_groups = heads // 2 // GROUP

    def kda_half(which):
        scalars = jnp.concatenate(
            [jnp.stack([which * half_groups, first_row]).astype(jnp.int32), starts]
        )
        return kda_local(
            scalars, kda_query, kda_key, kda_value, log_decay, write_rate, half_groups, ndocs
        )

    mu_away, qe_away, lo_away = kda_half(1 - column)
    mu_got = swap(mu_away, partner)
    moved = [swap(latents, t) for t in tables]
    mu_own, qe_own, lo_own = kda_half(column)

    slots = np.full((n, n), -1, np.int32)
    for i in range(n):
        slots[i, 0] = window - 1
        for m, t in enumerate(tables):
            if 0 < i - t[i] <= reach:
                slots[i, m + 1] = window - 1 - (i - t[i])
    mla_scalars = jnp.concatenate(
        [first_row[None].astype(jnp.int32), jnp.asarray(slots)[place], starts]
    )

    def attend(first, groups, previous):
        return mla(
            mla_scalars,
            mla_query,
            key_up,
            value_up,
            [latents, *moved],
            window,
            ndocs,
            first,
            groups,
            previous,
        )

    where = jnp.stack([column, (pair == 0).astype(jnp.int32), pair % 2]).astype(jnp.int32)
    shape = (heads // 2, 128, 128)
    pm, pu = whole_call(pair_kernel, "pair_join", where, [mu_own, mu_got], [shape, shape])
    state = pu
    rounds = -(-n // 4)
    for step in range(rounds):
        a, b = swap(state, up), swap(state, middle)
        if step < rounds - 1:
            (state,) = whole_call(step_kernel, "pair_step", where, [pm, pu, a, b], [shape])
    s_own, s_send = whole_call(
        split_kernel, "slab_states", where, [mu_own, mu_got, a, b], [shape, shape]
    )
    s_got = swap(s_send, partner)
    all_groups = heads // GROUP
    mla_out = attend(0, all_groups // 2, None)
    mla_out = attend(all_groups // 2, all_groups // 2, mla_out)
    out = final(column[None].astype(jnp.int32), qe_own, lo_own, s_own, heads, None)
    kda_out = final((1 - column)[None].astype(jnp.int32), qe_away, lo_away, s_got, heads, out)
    return (kda_out, mla_out)


def solution(mesh):
    in_specs = (
        P(("batch", "ctx"), None),
        P(("batch", "ctx"), None),
        P(("batch", "ctx"), None),
        P(("batch", "ctx"), None),
        P(("batch", "ctx"), None),
        P(("batch", "ctx"), None),
        P(("batch", "ctx"), None),
        P(),
        P(),
        P("batch"),
    )
    out_specs = (P(("batch", "ctx"), None), P(("batch", "ctx"), None))
    return jax.shard_map(local, mesh=mesh, in_specs=in_specs, out_specs=out_specs, check_vma=False)
```

time: 270 us -> 91.7 us (0.34)
  the two profiles are of different devices: /device:TPU:31 before, /device:TPU:16 now
where the time goes in v1:
time: 91.7 us; the launch traced here: 91.2 us
  Pallas kernels  32.4 us (35%)
  waiting for transfers between devices  25.8 us (28%)
  starting transfers between devices  20.5 us (22%)
  local copies, waits for them, and re-layouts  10.1 us (11%)
  other arithmetic  1.72 us (2%)
    ppermute x13, waiting for transfers between devices, swap(): return lax.ppermute(x, 'ctx', list(enumerate(table)))  25.8 us
    ppermute x13, starting transfers between devices, swap(): return lax.ppermute(x, 'ctx', list(enumerate(table)))  20.5 us
    pallas_call x2, Pallas kernels, mla(): pl.pallas_call(functools.partial(mla_kernel, ndocs, n, window, previous i...  13.9 us
    pallas_call x2, Pallas kernels, kda_local(): pl.pallas_call(functools.partial(kda_kernel, ndocs), grid_spec=pltpu.Pref...  12.5 us
    unnamed x42, local copies, waits for them, and re-layouts  9.38 us
    pallas_call x3, Pallas kernels, whole_call(): pl.pallas_call(kernel, grid_spec=pltpu.PrefetchScalarGridSpec(num_scalar_...  4.12 us
    pallas_call x2, Pallas kernels, final(): pl.pallas_call(final_kernel, grid_spec=pltpu.PrefetchScalarGridSpec(num_s...  1.85 us
  transfers between devices with their start and end apart: 13, of which 8 were waited for; matrix products, arithmetic and copies ran while one was open for 1% of the time, Pallas kernels for 25%

profile of v1, /device:TPU:16, one launch (start us, length us, event | category | flops | bytes accessed | tf_op | source)
XLA Modules:
  0.0 91.2 jit_solution(3252320333091287766)
XLA Ops:
  0.6 0.8 reduce-window.9
  1.5 0.7 bitcast_subtract_fusion
  2.1 0.8 copy.15.b_ref
  2.9 0.1 add_add_fusion.1
  3.0 1.0 %copy-done.11 = bf16[128,2048]{1,0:T(8,128)(2,1)S(1)} copy-done((bf16[128,2048]{1,0:T(8,128)(2,1)S(1)}, bf16[128,2048]{1,0:T(8,128)(2,1)}, u32[]{:S(2)}) %copy-start.11) | copy-done | bytes 524312
  4.1 1.0 %copy-done.13 = bf16[128,2048]{1,0:T(8,128)(2,1)S(1)} copy-done((bf16[128,2048]{1,0:T(8,128)(2,1)S(1)}, bf16[128,2048]{1,0:T(8,128)(2,1)}, u32[]{:S(2)}) %copy-start.13) | copy-done | bytes 524312
  5.1 1.0 %copy-done.15 = bf16[128,2048]{1,0:T(8,128)(2,1)S(1)} copy-done((bf16[128,2048]{1,0:T(8,128)(2,1)S(1)}, bf16[128,2048]{1,0:T(8,128)(2,1)}, u32[]{:S(2)}) %copy-start.15) | copy-done | bytes 524312
  6.1 1.0 %copy-done.17 = bf16[128,2048]{1,0:T(8,128)(2,1)S(1)} copy-done((bf16[128,2048]{1,0:T(8,128)(2,1)S(1)}, bf16[128,2048]{1,0:T(8,128)(2,1)}, u32[]{:S(2)}) %copy-start.17) | copy-done | bytes 524312
  7.2 6.6 %kda_slab.2 = (bf16[8,128,256]{2,1,0:T(8,128)(2,1)}, bf16[128,1024]{1,0:T(8,128)(2,1)S(1)}, f32[128,1024]{1,0:T(8,128)S(1)}) custom-call(s32[10]{0:T(128)S(1)} %get-tuple-element.23.sc, bf16[128,2048]{1,0:T(8,128)(2,1)S(1)} %copy-done.11, bf16[128,2048]{1,0:T(8,128)(2,1)S(1)} %copy-done.13, bf16[128,2048]{1,0:T(8,128)(2,1)S(1)} %copy-done.15, ...), custom_call_target="tpu_custom_call" | custom-call | flops 738197504 | bytes 2097152 | tf_op jit(solution)/shard_map/kda_slab/pallas_call | solution.py:140
  13.8 0.8 copy-done.3
  14.5 0.7 copy-done.7
  15.2 1.5 %collective-permute-start = (bf16[8,128,256]{2,1,0:T(8,128)(2,1)}, bf16[8,128,256]{2,1,0:T(8,128)(2,1)S(1)}, u32[]{:S(2)}, u32[]{:S(2)}) collective-permute-start(bf16[8,128,256]{2,1,0:T(8,128)(2,1)} %get-tuple-element.15), channel_id=1, source_target_pairs={{0,4},{4,0},{8,12},{12,8},{16,20},{20,16},{24,28},{28,24},{1,5},{5... | collective-permute-start | bytes 1572872 | tf_op jit(solution)/shard_map/ppermute | solution.py:362
  16.7 0.0 copy-done.12
  16.7 0.0 copy-done.14
  16.7 0.0 copy-done.16
  16.7 0.0 copy-done.18
  16.7 0.0 copy-start.19
  16.8 5.9 %kda_slab.3 = (bf16[8,128,256]{2,1,0:T(8,128)(2,1)S(1)}, bf16[128,1024]{1,0:T(8,128)(2,1)S(1)}, f32[128,1024]{1,0:T(8,128)S(1)}) custom-call(s32[10]{0:T(128)S(1)} %get-tuple-element.22.sc, bf16[128,2048]{1,0:T(8,128)(2,1)S(1)} %copy-done.12, bf16[128,2048]{1,0:T(8,128)(2,1)S(1)} %copy-done.14, bf16[128,2048]{1,0:T(8,128)(2,1)S(1)} %copy-done.16, ...), custom_call_target="tpu_custom_call" | custom-call | flops 738197504 | bytes 2097152 | tf_op jit(solution)/shard_map/kda_slab/pallas_call | solution.py:140
  22.7 0.0 copy-start.5
  22.7 0.0 copy-start.9
  22.7 0.1 pad_add_fusion.sc
  22.8 6.3 %collective-permute-done.got_ref = bf16[8,128,256]{2,1,0:T(8,128)(2,1)S(1)} collective-permute-done((bf16[8,128,256]{2,1,0:T(8,128)(2,1)}, bf16[8,128,256]{2,1,0:T(8,128)(2,1)S(1)}, u32[]{:S(2)}, u32[]{:S(2)}) %collective-permute-start) | collective-permute-done | bytes 524320 | tf_op jit(solution)/shard_map/ppermute | solution.py:362
  29.1 0.8 pair_join.1
  30.0 1.6 %collective-permute-start.1 = (bf16[8,128,128]{2,1,0:T(8,128)(2,1)S(1)}, bf16[8,128,128]{2,1,0:T(8,128)(2,1)S(1)}, u32[]{:S(2)}, u32[]{:S(2)}) collective-permute-start(bf16[8,128,128]{2,1,0:T(8,128)(2,1)S(1)} %get-tuple-element.17.pu_ref), channel_id=1, source_target_pairs={{0,8},{4,12},{8,0},{12,4},{16,24},{20,28},{24,16},{28,20},{1,9},{5... | collective-permute-start | bytes 786440 | tf_op jit(solution)/shard_map/ppermute | solution.py:362
  31.6 0.0 collective-permute-start.2
  31.6 5.6 %collective-permute-done.1.a_ref = bf16[8,128,128]{2,1,0:T(8,128)(2,1)S(1)} collective-permute-done((bf16[8,128,128]{2,1,0:T(8,128)(2,1)S(1)}, bf16[8,128,128]{2,1,0:T(8,128)(2,1)S(1)}, u32[]{:S(2)}, u32[]{:S(2)}) %collective-permute-start.1) | collective-permute-done | bytes 262176 | tf_op jit(solution)/shard_map/ppermute | solution.py:362
  37.2 1.3 %collective-permute-done.2.b_ref = bf16[8,128,128]{2,1,0:T(8,128)(2,1)S(1)} collective-permute-done((bf16[8,128,128]{2,1,0:T(8,128)(2,1)S(1)}, bf16[8,128,128]{2,1,0:T(8,128)(2,1)S(1)}, u32[]{:S(2)}, u32[]{:S(2)}) %collective-permute-start.2) | collective-permute-done | bytes 262176 | tf_op jit(solution)/shard_map/ppermute | solution.py:362
  38.5 1.5 %pair_step.1 = bf16[8,128,128]{2,1,0:T(8,128)(2,1)} custom-call(s32[3]{0:T(128)S(1)} %pad_add_fusion.sc, bf16[8,128,128]{2,1,0:T(8,128)(2,1)S(1)} %get-tuple-element.16.pm_ref, bf16[8,128,128]{2,1,0:T(8,128)(2,1)S(1)} %get-tuple-element.17.pu_ref, bf16[8,128,128]{2,1,0:T(8,128)(2,1)S(1)} %collective-permute-done.1.a_ref, ...), custom_call_target="tpu_custom_call" | custom-call | tf_op jit(solution)/shard_map/pair_step/pallas_call | solution.py:214
  40.0 0.5 collective-permute-start.3
  40.4 0.0 copy-done.5
  40.4 0.0 copy-done.9
  40.4 0.4 collective-permute-start.4
  40.9 0.0 copy-done.19
  40.9 0.2 copy.25.refs_3_
  41.0 1.6 %collective-permute-start.6 = (bf16[128,576]{1,0:T(8,128)(2,1)S(1)}, bf16[128,576]{1,0:T(8,128)(2,1)S(1)}, u32[]{:S(2)}, u32[]{:S(2)}) collective-permute-start(bf16[128,576]{1,0:T(8,128)(2,1)S(1)} %copy.25.refs_3_), channel_id=1, source_target_pairs={{0,4},{4,0},{8,12},{12,8},{16,20},{20,16},{24,28},{28,24},{1,5},{5... | collective-permute-start | bytes 442376 | tf_op jit(solution)/shard_map/ppermute | solution.py:362
  42.6 1.7 %collective-permute-start.7 = (bf16[128,576]{1,0:T(8,128)(2,1)S(1)}, bf16[128,576]{1,0:T(8,128)(2,1)}, u32[]{:S(2)}, u32[]{:S(2)}) collective-permute-start(bf16[128,576]{1,0:T(8,128)(2,1)S(1)} %copy.25.refs_3_), channel_id=1, source_target_pairs={{0,8},{4,12},{8,0},{12,4},{16,24},{20,28},{24,16},{28,20},{1,9},{5... | collective-permute-start | bytes 442376 | tf_op jit(solution)/shard_map/ppermute | solution.py:362
  44.2 0.9 %collective-permute-start.8 = (bf16[128,576]{1,0:T(8,128)(2,1)S(1)}, bf16[128,576]{1,0:T(8,128)(2,1)}, u32[]{:S(2)}, u32[]{:S(2)}) collective-permute-start(bf16[128,576]{1,0:T(8,128)(2,1)S(1)} %copy.25.refs_3_), channel_id=1, source_target_pairs={{0,12},{4,8},{8,4},{12,0},{16,28},{20,24},{24,20},{28,16},{1,13},{... | collective-permute-start | bytes 442376 | tf_op jit(solution)/shard_map/ppermute | solution.py:362
  45.2 1.2 %collective-permute-done.6.refs_4_ = bf16[128,576]{1,0:T(8,128)(2,1)S(1)} collective-permute-done((bf16[128,576]{1,0:T(8,128)(2,1)S(1)}, bf16[128,576]{1,0:T(8,128)(2,1)S(1)}, u32[]{:S(2)}, u32[]{:S(2)}) %collective-permute-start.6) | collective-permute-done | bytes 147488 | tf_op jit(solution)/shard_map/ppermute | solution.py:362
  46.4 8.7 %collective-permute-start.9 = (bf16[128,576]{1,0:T(8,128)(2,1)S(1)}, bf16[128,576]{1,0:T(8,128)(2,1)S(1)}, u32[]{:S(2)}, u32[]{:S(2)}) collective-permute-start(bf16[128,576]{1,0:T(8,128)(2,1)S(1)} %copy.25.refs_3_), channel_id=1, source_target_pairs={{0,16},{4,20},{8,24},{12,28},{16,0},{20,4},{24,8},{28,12},{1,17},{... | collective-permute-start | bytes 442376 | tf_op jit(solution)/shard_map/ppermute | solution.py:362
  55.1 0.0 collective-permute-done.7.refs_5_
  55.1 0.0 collective-permute-start.10
  55.1 0.0 collective-permute-done.3.a_ref
  55.1 0.6 collective-permute-start.11
  55.7 0.0 collective-permute-done.4.b_ref
  55.7 1.3 %collective-permute-start.12 = (bf16[128,576]{1,0:T(8,128)(2,1)S(1)}, bf16[128,576]{1,0:T(8,128)(2,1)S(1)}, u32[]{:S(2)}, u32[]{:S(2)}) collective-permute-start(bf16[128,576]{1,0:T(8,128)(2,1)S(1)} %copy.25.refs_3_), channel_id=1, source_target_pairs={{0,4},{4,0},{8,20},{12,16},{16,12},{20,8},{24,28},{28,24},{1,5},{5... | collective-permute-start | bytes 442376 | tf_op jit(solution)/shard_map/ppermute | solution.py:362
  57.0 0.7 dynamic-slice_bitcast_fusion
  57.7 0.1 pad_add_fusion.1.sc
  57.8 1.8 %slab_states.1 = (bf16[8,128,128]{2,1,0:T(8,128)(2,1)S(1)}, bf16[8,128,128]{2,1,0:T(8,128)(2,1)S(1)}) custom-call(s32[3]{0:T(128)S(1)} %pad_add_fusion.sc, bf16[8,128,256]{2,1,0:T(8,128)(2,1)S(1)} %get-tuple-element.14.own_ref, bf16[8,128,256]{2,1,0:T(8,128)(2,1)S(1)} %collective-permute-done.got_ref, bf16[8,128,128]{2,1,0:T(8,128)(2,1)} %collective-permute-done.3.a_ref, ...), custom_call_target="tpu_custom_call" | custom-call | tf_op jit(solution)/shard_map/slab_states/pallas_call | solution.py:214
  59.6 0.0 collective-permute-done.8.refs_6_
  59.6 1.7 %collective-permute-start.5 = (bf16[8,128,128]{2,1,0:T(8,128)(2,1)S(1)}, bf16[8,128,128]{2,1,0:T(8,128)(2,1)S(1)}, u32[]{:S(2)}, u32[]{:S(2)}) collective-permute-start(bf16[8,128,128]{2,1,0:T(8,128)(2,1)S(1)} %get-tuple-element.18), channel_id=1, source_target_pairs={{0,4},{4,0},{8,12},{12,8},{16,20},{20,16},{24,28},{28,24},{1,5},{5... | collective-permute-start | bytes 786440 | tf_op jit(solution)/shard_map/ppermute | solution.py:362
  61.3 1.5 %collective-permute-done.9.refs_7_ = bf16[128,576]{1,0:T(8,128)(2,1)S(1)} collective-permute-done((bf16[128,576]{1,0:T(8,128)(2,1)S(1)}, bf16[128,576]{1,0:T(8,128)(2,1)S(1)}, u32[]{:S(2)}, u32[]{:S(2)}) %collective-permute-start.9) | collective-permute-done | bytes 147488 | tf_op jit(solution)/shard_map/ppermute | solution.py:362
  62.8 3.4 %collective-permute-done.10.refs_8_ = bf16[128,576]{1,0:T(8,128)(2,1)S(1)} collective-permute-done((bf16[128,576]{1,0:T(8,128)(2,1)S(1)}, bf16[128,576]{1,0:T(8,128)(2,1)S(1)}, u32[]{:S(2)}, u32[]{:S(2)}) %collective-permute-start.10) | collective-permute-done | bytes 147488 | tf_op jit(solution)/shard_map/ppermute | solution.py:362
  66.2 1.8 %collective-permute-done.11.refs_9_ = bf16[128,576]{1,0:T(8,128)(2,1)S(1)} collective-permute-done((bf16[128,576]{1,0:T(8,128)(2,1)S(1)}, bf16[128,576]{1,0:T(8,128)(2,1)S(1)}, u32[]{:S(2)}, u32[]{:S(2)}) %collective-permute-start.11) | collective-permute-done | bytes 147488 | tf_op jit(solution)/shard_map/ppermute | solution.py:362
  68.0 4.7 %collective-permute-done.12.refs_10_ = bf16[128,576]{1,0:T(8,128)(2,1)S(1)} collective-permute-done((bf16[128,576]{1,0:T(8,128)(2,1)S(1)}, bf16[128,576]{1,0:T(8,128)(2,1)S(1)}, u32[]{:S(2)}, u32[]{:S(2)}) %collective-permute-start.12) | collective-permute-done | bytes 147488 | tf_op jit(solution)/shard_map/ppermute | solution.py:362
  72.7 0.0 copy-done
  72.7 1.6 %copy-done.1 = bf16[512,2048]{1,0:T(8,128)(2,1)S(1)} copy-done((bf16[512,2048]{1,0:T(8,128)(2,1)S(1)}, bf16[512,2048]{1,0:T(8,128)(2,1)}, u32[]{:S(2)}) %copy-start.1) | copy-done | bytes 2097176
  74.3 1.1 %copy-done.2 = bf16[128,3072]{1,0:T(8,128)(2,1)S(1)} copy-done((bf16[128,3072]{1,0:T(8,128)(2,1)S(1)}, bf16[128,3072]{1,0:T(8,128)(2,1)}, u32[]{:S(2)}) %copy-start.2) | copy-done | bytes 786456
  75.4 7.0 %mla_heads.2.refs_11_ = bf16[128,2048]{1,0:T(8,128)(2,1)} custom-call(s32[17]{0:T(128)S(1)} %pad_add_fusion.1.sc, bf16[128,3072]{1,0:T(8,128)(2,1)S(1)} %copy-done.2, bf16[512,2048]{1,0:T(8,128)(2,1)S(1)} %copy-done, bf16[512,2048]{1,0:T(8,128)(2,1)S(1)} %copy-done.1, bf16[128,576]{1,0:T(8,128)(2,1)S(1)} %copy.25.refs_3_, ...), custom_call_target="tpu_custom_call" | custom-call | flops 1845493760 | bytes 3072000 | tf_op jit(solution)/shard_map/mla_heads/pallas_call | solution.py:316
  82.4 7.0 %mla_heads.3 = bf16[128,2048]{1,0:T(8,128)(2,1)} custom-call(s32[17]{0:T(128)S(1)} %pad_add_fusion.1.sc, bf16[128,3072]{1,0:T(8,128)(2,1)S(1)} %copy-done.2, bf16[512,2048]{1,0:T(8,128)(2,1)S(1)} %copy-done, bf16[512,2048]{1,0:T(8,128)(2,1)S(1)} %copy-done.1, bf16[128,576]{1,0:T(8,128)(2,1)S(1)} %copy.25.refs_3_, ...), custom_call_target="tpu_custom_call", output_to_operand_aliasing={{}: (12, {})} | custom-call | flops 1845493760 | bytes 3072000 | tf_op jit(solution)/shard_map/mla_heads/pallas_call | solution.py:316
  89.3 0.0 copy-done.6
  89.3 0.9 %kda_out.2.rest_0_ = bf16[128,2048]{1,0:T(8,128)(2,1)} custom-call(s32[1]{0:T(128)} %bitcast.5.sc, bf16[128,1024]{1,0:T(8,128)(2,1)S(1)} %copy-done.10, f32[128,1024]{1,0:T(8,128)S(1)} %copy-done.6, bf16[8,128,128]{2,1,0:T(8,128)(2,1)S(1)} %get-tuple-element.21.s_ref), custom_call_target="tpu_custom_call" | custom-call | tf_op jit(solution)/shard_map/kda_out/pallas_call | solution.py:246
  90.3 0.0 collective-permute-done.5.s_ref
  90.3 0.0 copy-done.8
  90.3 0.9 %kda_out.3 = bf16[128,2048]{1,0:T(8,128)(2,1)} custom-call(s32[1]{0:T(128)} %bitcast.sc, bf16[128,1024]{1,0:T(8,128)(2,1)S(1)} %copy-done.8, f32[128,1024]{1,0:T(8,128)S(1)} %copy-done.4, bf16[8,128,128]{2,1,0:T(8,128)(2,1)S(1)} %collective-permute-done.5.s_ref, bf16[128,2048]{1,0:T(8,128)(2,1)} %kda_out.2.rest_0_), custom_call_target="tpu_custom_call", output_to_operand_aliasing={{}: (4, {})} | custom-call | tf_op jit(solution)/shard_map/kda_out/pallas_call | solution.py:246
  (19 shorter events, 0.0 us)
Async XLA Ops:
  3.0 1.0 %copy-start.11 = (bf16[128,2048]{1,0:T(8,128)(2,1)S(1)}, bf16[128,2048]{1,0:T(8,128)(2,1)}, u32[]{:S(2)}) copy-start(bf16[128,2048]{1,0:T(8,128)(2,1)} %q_ref.3) | copy-start | bytes 1572868
  4.0 1.0 %copy-start.13 = (bf16[128,2048]{1,0:T(8,128)(2,1)S(1)}, bf16[128,2048]{1,0:T(8,128)(2,1)}, u32[]{:S(2)}) copy-start(bf16[128,2048]{1,0:T(8,128)(2,1)} %k_ref.3) | copy-start | bytes 1572868
  5.1 1.0 %copy-start.15 = (bf16[128,2048]{1,0:T(8,128)(2,1)S(1)}, bf16[128,2048]{1,0:T(8,128)(2,1)}, u32[]{:S(2)}) copy-start(bf16[128,2048]{1,0:T(8,128)(2,1)} %v_ref.3) | copy-start | bytes 1572868
  6.1 1.0 %copy-start.17 = (bf16[128,2048]{1,0:T(8,128)(2,1)S(1)}, bf16[128,2048]{1,0:T(8,128)(2,1)}, u32[]{:S(2)}) copy-start(bf16[128,2048]{1,0:T(8,128)(2,1)} %g_ref.3) | copy-start | bytes 1572868
  7.2 9.6 %copy-start.12 = (bf16[128,2048]{1,0:T(8,128)(2,1)S(1)}, bf16[128,2048]{1,0:T(8,128)(2,1)}, u32[]{:S(2)}) copy-start(bf16[128,2048]{1,0:T(8,128)(2,1)} %q_ref.3) | copy-start | bytes 1572868
  7.2 9.6 %copy-start.14 = (bf16[128,2048]{1,0:T(8,128)(2,1)S(1)}, bf16[128,2048]{1,0:T(8,128)(2,1)}, u32[]{:S(2)}) copy-start(bf16[128,2048]{1,0:T(8,128)(2,1)} %k_ref.3) | copy-start | bytes 1572868
  7.2 9.6 %copy-start.16 = (bf16[128,2048]{1,0:T(8,128)(2,1)S(1)}, bf16[128,2048]{1,0:T(8,128)(2,1)}, u32[]{:S(2)}) copy-start(bf16[128,2048]{1,0:T(8,128)(2,1)} %v_ref.3) | copy-start | bytes 1572868
  7.2 9.6 %copy-start.18 = (bf16[128,2048]{1,0:T(8,128)(2,1)S(1)}, bf16[128,2048]{1,0:T(8,128)(2,1)}, u32[]{:S(2)}) copy-start(bf16[128,2048]{1,0:T(8,128)(2,1)} %g_ref.3) | copy-start | bytes 1572868
  13.8 0.8 copy-start.3
  14.5 0.7 copy-start.7
  15.2 13.9 %collective-permute-start = (bf16[8,128,256]{2,1,0:T(8,128)(2,1)}, bf16[8,128,256]{2,1,0:T(8,128)(2,1)S(1)}, u32[]{:S(2)}, u32[]{:S(2)}) collective-permute-start(bf16[8,128,256]{2,1,0:T(8,128)(2,1)} %get-tuple-element.15), channel_id=1, source_target_pairs={{0,4},{4,0},{8,12},{12,8},{16,20},{20,16},{24,28},{28,24},{1,5},{5... | collective-permute-start | bytes 1572872 | tf_op jit(solution)/shard_map/ppermute | solution.py:362
  16.7 24.1 %copy-start.19 = (bf16[128,576]{0,1:T(8,128)(2,1)S(1)}, bf16[128,576]{0,1:T(8,128)(2,1)}, u32[]{:S(2)}) copy-start(bf16[128,576]{0,1:T(8,128)(2,1)} %param.17) | copy-start | bytes 442372
  22.7 17.7 %copy-start.5 = (f32[128,1024]{1,0:T(8,128)}, f32[128,1024]{1,0:T(8,128)S(1)}, u32[]{:S(2)}) copy-start(f32[128,1024]{1,0:T(8,128)S(1)} %get-tuple-element.20.lo_ref) | copy-start | bytes 1572868
  22.7 17.7 %copy-start.9 = (bf16[128,1024]{1,0:T(8,128)(2,1)}, bf16[128,1024]{1,0:T(8,128)(2,1)S(1)}, u32[]{:S(2)}) copy-start(bf16[128,1024]{1,0:T(8,128)(2,1)S(1)} %get-tuple-element.19.qe_ref) | copy-start | bytes 786436
  29.1 43.6 %copy-start = (bf16[512,2048]{1,0:T(8,128)(2,1)S(1)}, bf16[512,2048]{1,0:T(8,128)(2,1)}, u32[]{:S(2)}) copy-start(bf16[512,2048]{1,0:T(8,128)(2,1)} %refs_1_.3) | copy-start | bytes 6291460
  30.0 7.2 %collective-permute-start.1 = (bf16[8,128,128]{2,1,0:T(8,128)(2,1)S(1)}, bf16[8,128,128]{2,1,0:T(8,128)(2,1)S(1)}, u32[]{:S(2)}, u32[]{:S(2)}) collective-permute-start(bf16[8,128,128]{2,1,0:T(8,128)(2,1)S(1)} %get-tuple-element.17.pu_ref), channel_id=1, source_target_pairs={{0,8},{4,12},{8,0},{12,4},{16,24},{20,28},{24,16},{28,20},{1,9},{5... | collective-permute-start | bytes 786440 | tf_op jit(solution)/shard_map/ppermute | solution.py:362
  31.6 6.9 %collective-permute-start.2 = (bf16[8,128,128]{2,1,0:T(8,128)(2,1)S(1)}, bf16[8,128,128]{2,1,0:T(8,128)(2,1)S(1)}, u32[]{:S(2)}, u32[]{:S(2)}) collective-permute-start(bf16[8,128,128]{2,1,0:T(8,128)(2,1)S(1)} %get-tuple-element.17.pu_ref), channel_id=1, source_target_pairs={{0,4},{4,0},{8,16},{12,20},{16,8},{20,12},{24,28},{28,24},{1,5},{5... | collective-permute-start | bytes 786440 | tf_op jit(solution)/shard_map/ppermute | solution.py:362
  40.0 15.2 %collective-permute-start.3 = (bf16[8,128,128]{2,1,0:T(8,128)(2,1)}, bf16[8,128,128]{2,1,0:T(8,128)(2,1)}, u32[]{:S(2)}, u32[]{:S(2)}) collective-permute-start(bf16[8,128,128]{2,1,0:T(8,128)(2,1)} %pair_step.1), channel_id=1, source_target_pairs={{0,8},{4,12},{8,0},{12,4},{16,24},{20,28},{24,16},{28,20},{1,9},{5... | collective-permute-start | bytes 786440 | tf_op jit(solution)/shard_map/ppermute | solution.py:362
  40.4 15.3 %collective-permute-start.4 = (bf16[8,128,128]{2,1,0:T(8,128)(2,1)}, bf16[8,128,128]{2,1,0:T(8,128)(2,1)}, u32[]{:S(2)}, u32[]{:S(2)}) collective-permute-start(bf16[8,128,128]{2,1,0:T(8,128)(2,1)} %pair_step.1), channel_id=1, source_target_pairs={{0,4},{4,0},{8,16},{12,20},{16,8},{20,12},{24,28},{28,24},{1,5},{5... | collective-permute-start | bytes 786440 | tf_op jit(solution)/shard_map/ppermute | solution.py:362
  41.0 5.4 %collective-permute-start.6 = (bf16[128,576]{1,0:T(8,128)(2,1)S(1)}, bf16[128,576]{1,0:T(8,128)(2,1)S(1)}, u32[]{:S(2)}, u32[]{:S(2)}) collective-permute-start(bf16[128,576]{1,0:T(8,128)(2,1)S(1)} %copy.25.refs_3_), channel_id=1, source_target_pairs={{0,4},{4,0},{8,12},{12,8},{16,20},{20,16},{24,28},{28,24},{1,5},{5... | collective-permute-start | bytes 442376 | tf_op jit(solution)/shard_map/ppermute | solution.py:362
  42.6 12.5 %collective-permute-start.7 = (bf16[128,576]{1,0:T(8,128)(2,1)S(1)}, bf16[128,576]{1,0:T(8,128)(2,1)}, u32[]{:S(2)}, u32[]{:S(2)}) collective-permute-start(bf16[128,576]{1,0:T(8,128)(2,1)S(1)} %copy.25.refs_3_), channel_id=1, source_target_pairs={{0,8},{4,12},{8,0},{12,4},{16,24},{20,28},{24,16},{28,20},{1,9},{5... | collective-permute-start | bytes 442376 | tf_op jit(solution)/shard_map/ppermute | solution.py:362
  44.2 15.4 %collective-permute-start.8 = (bf16[128,576]{1,0:T(8,128)(2,1)S(1)}, bf16[128,576]{1,0:T(8,128)(2,1)}, u32[]{:S(2)}, u32[]{:S(2)}) collective-permute-start(bf16[128,576]{1,0:T(8,128)(2,1)S(1)} %copy.25.refs_3_), channel_id=1, source_target_pairs={{0,12},{4,8},{8,4},{12,0},{16,28},{20,24},{24,20},{28,16},{1,13},{... | collective-permute-start | bytes 442376 | tf_op jit(solution)/shard_map/ppermute | solution.py:362
  46.4 16.4 %collective-permute-start.9 = (bf16[128,576]{1,0:T(8,128)(2,1)S(1)}, bf16[128,576]{1,0:T(8,128)(2,1)S(1)}, u32[]{:S(2)}, u32[]{:S(2)}) collective-permute-start(bf16[128,576]{1,0:T(8,128)(2,1)S(1)} %copy.25.refs_3_), channel_id=1, source_target_pairs={{0,16},{4,20},{8,24},{12,28},{16,0},{20,4},{24,8},{28,12},{1,17},{... | collective-permute-start | bytes 442376 | tf_op jit(solution)/shard_map/ppermute | solution.py:362
  55.1 11.1 %collective-permute-start.10 = (bf16[128,576]{1,0:T(8,128)(2,1)S(1)}, bf16[128,576]{1,0:T(8,128)(2,1)S(1)}, u32[]{:S(2)}, u32[]{:S(2)}) collective-permute-start(bf16[128,576]{1,0:T(8,128)(2,1)S(1)} %copy.25.refs_3_), channel_id=1, source_target_pairs={{0,8},{4,16},{8,0},{12,24},{16,4},{20,28},{24,12},{28,20},{1,9},{5... | collective-permute-start | bytes 442376 | tf_op jit(solution)/shard_map/ppermute | solution.py:362
  55.1 12.9 %collective-permute-start.11 = (bf16[128,576]{1,0:T(8,128)(2,1)S(1)}, bf16[128,576]{1,0:T(8,128)(2,1)S(1)}, u32[]{:S(2)}, u32[]{:S(2)}) collective-permute-start(bf16[128,576]{1,0:T(8,128)(2,1)S(1)} %copy.25.refs_3_), channel_id=1, source_target_pairs={{0,4},{4,0},{8,16},{12,20},{16,8},{20,12},{24,28},{28,24},{1,5},{5... | collective-permute-start | bytes 442376 | tf_op jit(solution)/shard_map/ppermute | solution.py:362
  55.7 17.0 %collective-permute-start.12 = (bf16[128,576]{1,0:T(8,128)(2,1)S(1)}, bf16[128,576]{1,0:T(8,128)(2,1)S(1)}, u32[]{:S(2)}, u32[]{:S(2)}) collective-permute-start(bf16[128,576]{1,0:T(8,128)(2,1)S(1)} %copy.25.refs_3_), channel_id=1, source_target_pairs={{0,4},{4,0},{8,20},{12,16},{16,12},{20,8},{24,28},{28,24},{1,5},{5... | collective-permute-start | bytes 442376 | tf_op jit(solution)/shard_map/ppermute | solution.py:362
  59.6 30.7 %collective-permute-start.5 = (bf16[8,128,128]{2,1,0:T(8,128)(2,1)S(1)}, bf16[8,128,128]{2,1,0:T(8,128)(2,1)S(1)}, u32[]{:S(2)}, u32[]{:S(2)}) collective-permute-start(bf16[8,128,128]{2,1,0:T(8,128)(2,1)S(1)} %get-tuple-element.18), channel_id=1, source_target_pairs={{0,4},{4,0},{8,12},{12,8},{16,20},{20,16},{24,28},{28,24},{1,5},{5... | collective-permute-start | bytes 786440 | tf_op jit(solution)/shard_map/ppermute | solution.py:362
  72.7 1.6 %copy-start.1 = (bf16[512,2048]{1,0:T(8,128)(2,1)S(1)}, bf16[512,2048]{1,0:T(8,128)(2,1)}, u32[]{:S(2)}) copy-start(bf16[512,2048]{1,0:T(8,128)(2,1)} %refs_2_.3) | copy-start | bytes 6291460
  74.3 1.1 %copy-start.2 = (bf16[128,3072]{1,0:T(8,128)(2,1)S(1)}, bf16[128,3072]{1,0:T(8,128)(2,1)}, u32[]{:S(2)}) copy-start(bf16[128,3072]{1,0:T(8,128)(2,1)} %refs_0_.3) | copy-start | bytes 2359300
  82.4 7.0 %copy-start.6 = (f32[128,1024]{1,0:T(8,128)S(1)}, f32[128,1024]{1,0:T(8,128)}, u32[]{:S(2)}) copy-start(f32[128,1024]{1,0:T(8,128)} %copy-done.5) | copy-start | bytes 1572868
  82.4 7.0 %copy-start.10 = (bf16[128,1024]{1,0:T(8,128)(2,1)S(1)}, bf16[128,1024]{1,0:T(8,128)(2,1)}, u32[]{:S(2)}) copy-start(bf16[128,1024]{1,0:T(8,128)(2,1)} %copy-done.9) | copy-start | bytes 786436
  82.4 7.9 %copy-start.4 = (f32[128,1024]{1,0:T(8,128)S(1)}, f32[128,1024]{1,0:T(8,128)}, u32[]{:S(2)}) copy-start(f32[128,1024]{1,0:T(8,128)} %copy-done.3) | copy-start | bytes 1572868
  82.4 7.9 %copy-start.8 = (bf16[128,1024]{1,0:T(8,128)(2,1)S(1)}, bf16[128,1024]{1,0:T(8,128)(2,1)}, u32[]{:S(2)}) copy-start(bf16[128,1024]{1,0:T(8,128)(2,1)} %copy-done.7) | copy-start | bytes 786436

commit v2 on v1

v2 whole, which is shorter than its diff:
```python
import functools
import math

import jax
import jax.numpy as jnp
import numpy as np
from jax import lax
from jax.experimental import pallas as pl
from jax.experimental.pallas import tpu as pltpu
from jax.sharding import PartitionSpec as P

NOPE = 128
ROPE = 64
LATENT = 512
VMEM = 20 * 1024 * 1024
WHOLE = pl.BlockSpec(memory_space=pltpu.VMEM)
SCALARS = pl.BlockSpec(memory_space=pltpu.SMEM)
FAR = pl.BlockSpec(memory_space=pltpu.HBM)
BF = jnp.bfloat16
F32 = jnp.float32
NEG = -1e30


def mm(a, b):
    return jnp.dot(a, b, preferred_element_type=F32)


def mm_nt(a, b):
    return lax.dot_general(a, b, (((1,), (1,)), ((), ())), preferred_element_type=F32)


def mm_tn(a, b):
    return lax.dot_general(a, b, (((0,), (0,)), ((), ())), preferred_element_type=F32)


def doc_of(places, lengths_ref, ndocs):
    total = jnp.full(jnp.shape(places), -1, jnp.int32)
    start = 0
    for j in range(ndocs):
        total = total + (start <= places).astype(jnp.int32)
        start = start + lengths_ref[j]
    return total


def kda_kernel(ndocs, flip, sc, *refs):
    sources, (b_ref, mu_ref, qe_ref, lo_ref), blocks, sems = refs[:4], refs[4:8], refs[8:12], refs[12]
    rows, width = blocks[0].shape
    place = lax.axis_index("ctx")
    side = (place + flip) % 2
    start = pl.multiple_of(side * width, width)
    parts = 2
    part = width // parts
    copies = [
        [
            pltpu.make_async_copy(
                source.at[:, pl.ds(start + i * part, part)],
                block.at[:, pl.ds(i * part, part)],
                sems.at[j, i],
            )
            for j, (source, block) in enumerate(zip(sources, blocks))
        ]
        for i in range(parts)
    ]
    for group in copies:
        for copy in group:
            copy.start()
    q_ref, k_ref, v_ref, g_ref = blocks
    half = rows // 2
    heads = width // 128
    base = side * heads
    first = place * rows
    ri = lax.broadcasted_iota(jnp.int32, (rows, rows), 0)
    ci = lax.broadcasted_iota(jnp.int32, (rows, rows), 1)
    doc_r = doc_of(first + ri, sc, ndocs)
    doc_c = doc_of(first + ci, sc, ndocs)
    prev = doc_of(first - 1, sc, ndocs)
    last = doc_of(first + rows - 1, sc, ndocs)
    same = doc_r == doc_c
    strict = same & (ri > ci)
    causal = same & (ri >= ci)
    follow = (doc_r == prev).astype(F32)
    tail = (doc_r == last).astype(F32)
    keep = (last == prev).astype(F32)
    eye = (ri == ci).astype(F32)
    tri = (ri >= ci).astype(BF)
    low = ci < half

    hs = range(heads)
    lhs, km, lhs_off, km_off, rhs, kt, qg, gl, gain = [], [], [], [], [], [], [], [], []
    for h in hs:
        cols = slice(h * 128, (h + 1) * 128)
        if h % (heads // parts) == 0:
            i = h // (heads // parts)
            for copy in copies[i]:
                copy.wait()
            cum_part = mm(tri, g_ref[:, i * part : (i + 1) * part])
        q = q_ref[:, cols].astype(F32)
        k = k_ref[:, cols].astype(F32)
        v = v_ref[:, cols].astype(F32)
        qn = q * lax.rsqrt(jnp.sum(q * q, axis=1, keepdims=True) + 1e-06)
        kn = k * lax.rsqrt(jnp.sum(k * k, axis=1, keepdims=True) + 1e-06)
        cum = cum_part[:, h * 128 - i * part : (h + 1) * 128 - i * part]
        b = jnp.sum(eye * b_ref[pl.ds(base + h, 1), :], axis=1, keepdims=True)
        quarter = half // 2
        m0 = cum[quarter - 1 : quarter]
        m1 = cum[half + quarter - 1 : half + quarter]
        mid = cum[half - 1 : half]
        end = cum[rows - 1 : rows]
        c0, c1 = cum[:half], cum[half:]
        dp = jnp.concatenate([jnp.exp(c0 - m0), jnp.exp(c1 - m1)], axis=0)
        dm = jnp.concatenate([jnp.exp(m0 - c0), jnp.exp(m1 - c1)], axis=0)
        op = jnp.exp(c1 - mid)
        om = jnp.exp(jnp.minimum(mid - cum, 0.0))
        growth = jnp.exp(cum)
        trail = jnp.exp(end - cum)
        lhs.append(jnp.concatenate([(kn * dp).astype(BF), (qn * dp).astype(BF)], axis=0))
        km.append((kn * dm).astype(BF))
        lhs_off.append(
            jnp.concatenate([(kn[half:] * op).astype(BF), (qn[half:] * op).astype(BF)], axis=0)
        )
        km_off.append((kn * om).astype(BF))
        rhs.append(
            jnp.concatenate([(kn * growth * (b * follow)).astype(BF), (v * b).astype(BF)], axis=1)
        )
        kt.append((kn * trail * tail).astype(BF))
        qg.append(qn * growth * follow)
        gl.append(jnp.exp(end) * keep)
        gain.append(b)

    a, mix = [], []
    for h in hs:
        p = mm_nt(lhs[h], km[h])
        o = mm_nt(lhs_off[h], km_off[h])
        pa, pq = p[:rows], p[rows:]
        pa = jnp.concatenate([pa[:half], jnp.where(low[half:], o[:half], pa[half:])], axis=0)
        pq = jnp.concatenate([pq[:half], jnp.where(low[half:], o[half:], pq[half:])], axis=0)
        a.append(jnp.where(strict, pa, 0.0) * gain[h])
        mix.append(jnp.where(causal, pq, 0.0).astype(BF))

    t = [eye - jnp.where((ri >> 1) == (ci >> 1), a[h], 0.0) for h in hs]
    shift = 1
    while (2 << shift) <= rows:
        level = ((ri >> (shift + 1)) == (ci >> (shift + 1))) & ((ri >> shift) != (ci >> shift))
        tb = [t[h].astype(BF) for h in hs]
        x = [mm(jnp.where(level, a[h], 0.0).astype(BF), tb[h]).astype(BF) for h in hs]
        t = [t[h] - mm(tb[h], x[h]) for h in hs]
        shift += 1

    wu = [mm(t[h].astype(BF), rhs[h]).astype(BF) for h in hs]
    for h in hs:
        cols = slice(h * 128, (h + 1) * 128)
        z = mm_tn(kt[h], wu[h])
        mu_ref[h, :, :128] = (eye * gl[h] - z[:, :128]).astype(BF)
        mu_ref[h, :, 128:] = z[:, 128:].astype(BF)
        y = mm(mix[h], wu[h])
        qe_ref[:, cols] = (qg[h] - y[:, :128]).astype(BF)
        lo_ref[:, cols] = y[:, 128:]


def kda_half(flip, lengths, q, k, v, g, b):
    rows, width = q.shape[0], q.shape[1] // 2
    heads, ndocs = b.shape[0], lengths.shape[0]
    return pl.pallas_call(
        functools.partial(kda_kernel, ndocs, flip),
        in_specs=[SCALARS, FAR, FAR, FAR, FAR, WHOLE],
        out_specs=[WHOLE, WHOLE, WHOLE],
        out_shape=[
            jax.ShapeDtypeStruct((heads // 2, 128, 256), BF),
            jax.ShapeDtypeStruct((rows, width), BF),
            jax.ShapeDtypeStruct((rows, width), F32),
        ],
        scratch_shapes=[pltpu.VMEM((rows, width), BF)] * 4 + [pltpu.SemaphoreType.DMA((4, 2))],
        compiler_params=pltpu.CompilerParams(vmem_limit_bytes=VMEM),
        cost_estimate=pl.CostEstimate(
            flops=heads * 2 * 128**3 * 100, bytes_accessed=width * rows * 16, transcendentals=0
        ),
        name="kda_slab",
    )(lengths, q, k, v, g, b)


def pair_kernel(own_ref, got_ref, pm_ref, pu_ref):
    place = lax.axis_index("ctx")

    def go(first_ref, second_ref):
        for h in range(own_ref.shape[0]):
            z = mm(second_ref[h, :, :128], first_ref[h])
            pm_ref[h] = z[:, :128].astype(BF)
            pu_ref[h] = (z[:, 128:] + second_ref[h, :, 128:].astype(F32)).astype(BF)

    @pl.when(place % 2 == 0)
    def _():
        go(own_ref, got_ref)

    @pl.when(place % 2 == 1)
    def _():
        go(got_ref, own_ref)


def arrived(place, a_ref, b_ref, h):
    x = jnp.where((place // 2) % 2 == 1, a_ref[h].astype(F32), b_ref[h].astype(F32))
    return jnp.where(place < 2, 0.0, x).astype(BF)


def step_kernel(pm_ref, pu_ref, a_ref, b_ref, out_ref):
    place = lax.axis_index("ctx")
    for h in range(pm_ref.shape[0]):
        x = arrived(place, a_ref, b_ref, h)
        out_ref[h] = (mm(pm_ref[h], x) + pu_ref[h].astype(F32)).astype(BF)


def split_kernel(own_ref, got_ref, a_ref, b_ref, mine_ref, send_ref):
    place = lax.axis_index("ctx")

    def go(mu_ref, plain_ref, moved_ref):
        for h in range(own_ref.shape[0]):
            x = arrived(place, a_ref, b_ref, h)
            plain_ref[h] = x
            moved_ref[h] = (mm(mu_ref[h, :, :128], x) + mu_ref[h, :, 128:].astype(F32)).astype(BF)

    @pl.when(place % 2 == 0)
    def _():
        go(own_ref, mine_ref, send_ref)

    @pl.when(place % 2 == 1)
    def _():
        go(got_ref, send_ref, mine_ref)


def whole_call(kernel, name, args, outs):
    return pl.pallas_call(
        kernel,
        in_specs=[WHOLE] * len(args),
        out_specs=[WHOLE] * len(outs),
        out_shape=[jax.ShapeDtypeStruct(o, BF) for o in outs],
        compiler_params=pltpu.CompilerParams(vmem_limit_bytes=VMEM // 2),
        name=name,
    )(*args)


def final_kernel(flip, qe_ref, lo_ref, s_ref, *rest):
    out_ref, held_ref, sem = rest[-3:]
    width = qe_ref.shape[1]
    side = (lax.axis_index("ctx") + flip) % 2
    start = pl.multiple_of(side * width, width)
    parts = 2
    part = width // parts
    copies = []
    for h in range(s_ref.shape[0]):
        cols = slice(h * 128, (h + 1) * 128)
        held_ref[:, cols] = (lo_ref[:, cols] + mm(qe_ref[:, cols], s_ref[h])).astype(BF)
        if (h + 1) * 128 % part == 0:
            i = len(copies)
            copies.append(
                pltpu.make_async_copy(
                    held_ref.at[:, pl.ds(i * part, part)],
                    out_ref.at[:, pl.ds(start + i * part, part)],
                    sem.at[i],
                )
            )
            copies[-1].start()
    for copy in copies:
        copy.wait()


def final(flip, qe, lo, s, heads, previous):
    rows, width = qe.shape
    args, specs, aliases = [qe, lo, s], [WHOLE] * 3, {}
    if previous is not None:
        args.append(previous)
        specs.append(FAR)
        aliases = {3: 0}
    return pl.pallas_call(
        functools.partial(final_kernel, flip),
        in_specs=specs,
        out_specs=FAR,
        out_shape=jax.ShapeDtypeStruct((rows, heads * 128), BF),
        scratch_shapes=[pltpu.VMEM((rows, width), BF), pltpu.SemaphoreType.DMA((2,))],
        input_output_aliases=aliases,
        compiler_params=pltpu.CompilerParams(vmem_limit_bytes=VMEM // 2),
        name="kda_out",
    )(*args)


def window_rows(place, reach, rows, own_ref, mate_ref, far, out_ref):
    def put(w, block):
        at = slice(w * rows, (w + 1) * rows)
        out_ref[at, :LATENT] = block[:LATENT].T
        out_ref[at, LATENT:] = block[LATENT:].T

    for column in range(2):
        for parity in range(2):

            @pl.when((place % 2 == column) & ((place // 2) % 2 == parity))
            def _():
                for w in range(reach + 1):
                    back = reach // 2 - (w + column) // 2
                    other = ((w + column) % 2) ^ column
                    if back == 0:
                        put(w, (mate_ref if other else own_ref)[...])
                    else:
                        put(w, far[2 * (back - 1) + 1 - parity][other])


def mla_kernel(ndocs, reach, count, first, lengths, q_ref, ku_ref, vu_ref, *refs):
    out_ref, held_ref, bias_ref, sem = refs[-4:]
    place = lax.axis_index("ctx")
    rows = q_ref.shape[0]
    keys = (reach + 1) * rows
    if count is None:
        lat_ref = refs[0]
    else:
        own_ref, mate_ref, lat_ref = refs[0], refs[1], refs[2 + count]
        window_rows(place, reach, rows, own_ref, mate_ref, refs[2 : 2 + count], lat_ref)
    here = place * rows + lax.broadcasted_iota(jnp.int32, (rows, 1), 0)
    there = (place - reach) * rows + lax.broadcasted_iota(jnp.int32, (1, keys), 1)
    doc_q = doc_of(here, lengths, ndocs)
    doc_k = doc_of(there, lengths, ndocs)
    bias_ref[...] = jnp.where((there <= here) & (doc_q == doc_k), 0.0, NEG)

    factor = math.log2(math.e) / math.sqrt(NOPE + ROPE)
    lat = lat_ref[:, :LATENT]
    rope = lat_ref[:, LATENT:]
    width = held_ref.shape[1]
    part = slice(first * 128, first * 128 + width)
    kn = mm(lat, ku_ref[:, part]).astype(BF)
    vals = mm(lat, vu_ref[:, part]).astype(BF)
    bias = bias_ref[...]
    hs = range(width // 128)
    cols = [slice(h * 128, (h + 1) * 128) for h in hs]
    wide = NOPE + ROPE
    s = [
        mm_nt(
            q_ref[:, (first + h) * wide : (first + h + 1) * wide],
            jnp.concatenate([kn[:, cols[h]], rope], axis=1),
        )
        for h in hs
    ]
    s = [x * factor + bias for x in s]
    w = [jnp.exp2(x - jnp.max(x, axis=1, keepdims=True)) for x in s]
    for h in hs:
        total = jnp.sum(w[h], axis=1, keepdims=True)
        held_ref[:, cols[h]] = (mm(w[h].astype(BF), vals[:, cols[h]]) / total).astype(BF)
    copy = pltpu.make_async_copy(held_ref, out_ref.at[:, part], sem)
    copy.start()
    copy.wait()


def mla(lengths, q, ku, vu, blocks, previous, reach, first, count):
    rows = q.shape[0]
    heads = ku.shape[1] // NOPE
    keys = (reach + 1) * rows
    args = [lengths, q, ku, vu, *blocks]
    specs = [SCALARS] + [WHOLE] * (len(args) - 1)
    out = jax.ShapeDtypeStruct((rows, heads * 128), BF)
    aliases = {}
    if previous is not None:
        aliases = {len(args): 0}
        args.append(previous)
        specs.append(FAR)
    return pl.pallas_call(
        functools.partial(
            mla_kernel,
            lengths.shape[0],
            reach,
            len(blocks) - 2 if previous is None else None,
            first,
        ),
        in_specs=specs,
        out_specs=[WHOLE, FAR] if previous is None else FAR,
        out_shape=[jax.ShapeDtypeStruct((keys, LATENT + ROPE), BF), out]
        if previous is None
        else out,
        scratch_shapes=[
            pltpu.VMEM((rows, count * 128), BF),
            pltpu.VMEM((rows, keys), F32),
            pltpu.SemaphoreType.DMA,
        ],
        input_output_aliases=aliases,
        compiler_params=pltpu.CompilerParams(vmem_limit_bytes=VMEM),
        cost_estimate=pl.CostEstimate(
            flops=6 * keys * count * 128 * (2 * LATENT + 3 * rows),
            bytes_accessed=count * 128 * 3000,
            transcendentals=0,
        ),
        name="mla_heads",
    )(*args)


def repaired(n, wanted):
    left = [i for i in range(n) if i not in wanted]
    out = dict(wanted)
    for a, b in zip(left[::2], left[1::2]):
        out[a], out[b] = b, a
    return [out[i] for i in range(n)]


def routes(n):
    mate = [i ^ 1 for i in range(n)]
    up = repaired(n, {i: i ^ 2 for i in range(n)})
    middle = {}
    for pair in range(1, n // 2 - 1, 2):
        for c in range(2):
            middle[2 * pair + c], middle[2 * pair + 2 + c] = 2 * pair + 2 + c, 2 * pair + c
    return mate, up, repaired(n, middle)


def swap(x, table):
    return lax.ppermute(x, "ctx", list(enumerate(table)))


def local(
    kda_query,
    kda_key,
    kda_value,
    log_decay,
    write_rate,
    mla_query,
    latents,
    key_up,
    value_up,
    doc_lengths,
):
    n = lax.axis_size("ctx")
    heads = write_rate.shape[1]
    reach = n // 2
    rounds = -(-n // 4)
    mate, up, middle = routes(n)
    kda_args = (doc_lengths, kda_query, kda_key, kda_value, log_decay, write_rate.T)

    lat = latents.T
    lat_mate = swap(lat, mate)
    mu_away, qe_away, lo_away = kda_half(1, *kda_args)
    mu_got = swap(mu_away, mate)
    lat_mate, _ = lax.optimization_barrier((lat_mate, mu_away))
    both = jnp.stack([lat, lat_mate])
    blocks = [lat, lat_mate]
    a = b = both
    for _ in range(rounds):
        a, b = swap(b, up), swap(a, middle)
        blocks += [a, b]
    mu_own, qe_own, lo_own = kda_half(0, *kda_args)

    def attend(latent_blocks, previous, first, count):
        return mla(
            doc_lengths,
            mla_query,
            key_up,
            value_up,
            latent_blocks,
            previous,
            reach,
            first,
            count,
        )

    shape = (heads // 2, 128, 128)
    pm, pu = whole_call(pair_kernel, "pair_join", [mu_own, mu_got], [shape, shape])
    state = pu
    for step in range(rounds):
        a, b = swap(state, up), swap(state, middle)
        if step == 0:
            window, mla_out = attend(blocks, None, 0, heads // 2)
            a, b, window = lax.optimization_barrier((a, b, window))
        if step < rounds - 1:
            (state,) = whole_call(step_kernel, "pair_step", [pm, pu, a, b], [shape])
    mla_out = attend([window], mla_out, heads // 2, heads // 2)
    a, b, mla_out = lax.optimization_barrier((a, b, mla_out))
    s_own, s_send = whole_call(split_kernel, "slab_states", [mu_own, mu_got, a, b], [shape, shape])
    s_got = swap(s_send, mate)
    out = final(0, qe_own, lo_own, s_own, heads, None)
    kda_out = final(1, qe_away, lo_away, s_got, heads, out)
    return (kda_out, mla_out)


def solution(mesh):
    in_specs = (
        P(("batch", "ctx"), None),
        P(("batch", "ctx"), None),
        P(("batch", "ctx"), None),
        P(("batch", "ctx"), None),
        P(("batch", "ctx"), None),
        P(("batch", "ctx"), None),
        P(("batch", "ctx"), None),
        P(),
        P(),
        P("batch"),
    )
    out_specs = (P(("batch", "ctx"), None), P(("batch", "ctx"), None))
    return jax.shard_map(local, mesh=mesh, in_specs=in_specs, out_specs=out_specs, check_vma=False)
```

time: 91.7 us -> 60.8 us (0.66)
  the two profiles are of different devices: /device:TPU:16 before, /device:TPU:0 now
where the time goes in v2:
time: 60.8 us; the launch traced here: 60.5 us
  waiting for transfers between devices  24.6 us (40%)
  Pallas kernels  19.8 us (33%)
  starting transfers between devices  9.47 us (16%)
  local copies, waits for them, and re-layouts  5.54 us (9%)
  between operations  0.98 us (2%)
    ppermute x11, waiting for transfers between devices, swap(): return lax.ppermute(x, 'ctx', list(enumerate(table)))  24.6 us
    ppermute x11, starting transfers between devices, swap(): return lax.ppermute(x, 'ctx', list(enumerate(table)))  9.47 us
    pallas_call x2, Pallas kernels, mla(): pl.pallas_call(functools.partial(mla_kernel, lengths.shape[0], reach, len...  8.8 us
    pallas_call x2, Pallas kernels, kda_half(): pl.pallas_call(functools.partial(kda_kernel, ndocs, flip), in_specs=[SCAL...  8.43 us
    unnamed x20, local copies, waits for them, and re-layouts  5.54 us
    pallas_call x2, Pallas kernels, final(): pl.pallas_call(functools.partial(final_kernel, flip), in_specs=specs, out...  1.8 us
  transfers between devices with their start and end apart: 11, of which 6 were waited for; matrix products, arithmetic and copies ran while one was open for 0% of the time, Pallas kernels for 30%

profile of v2, /device:TPU:0, one launch (start us, length us, event | category | flops | bytes accessed | tf_op | source)
XLA Modules:
  0.0 60.5 jit_solution(11653900596965821890)
XLA Ops:
  0.6 3.0 %collective-permute-start.3 = (bf16[576,128]{1,0:T(8,128)(2,1)}, bf16[576,128]{1,0:T(8,128)(2,1)S(1)}, u32[]{:S(2)}, u32[]{:S(2)}) collective-permute-start(bf16[576,128]{1,0:T(8,128)(2,1)} %bitcast.5), channel_id=1, source_target_pairs={{0,4},{4,0},{8,12},{12,8},{16,20},{20,16},{24,28},{28,24},{1,5},{5... | collective-permute-start | bytes 442376 | tf_op jit(solution)/shard_map/ppermute | solution.py:408
  3.6 0.0 copy-start.4
  3.6 1.0 %copy-done.4 = bf16[128,2048]{1,0:T(8,128)(2,1)S(1)} copy-done((bf16[128,2048]{1,0:T(8,128)(2,1)S(1)}, bf16[128,2048]{1,0:T(8,128)(2,1)}, u32[]{:S(2)}) %copy-start.4) | copy-done | bytes 524312
  4.7 0.0 copy-start.5
  4.7 1.0 %copy-done.5 = bf16[128,2048]{1,0:T(8,128)(2,1)S(1)} copy-done((bf16[128,2048]{1,0:T(8,128)(2,1)S(1)}, bf16[128,2048]{1,0:T(8,128)(2,1)}, u32[]{:S(2)}) %copy-start.5) | copy-done | bytes 524312
  5.7 0.0 copy-start.6
  5.7 1.0 %copy-done.6 = bf16[128,2048]{1,0:T(8,128)(2,1)S(1)} copy-done((bf16[128,2048]{1,0:T(8,128)(2,1)S(1)}, bf16[128,2048]{1,0:T(8,128)(2,1)}, u32[]{:S(2)}) %copy-start.6) | copy-done | bytes 524312
  6.8 0.0 copy-start.7
  6.8 1.0 %copy-done.7 = bf16[128,2048]{1,0:T(8,128)(2,1)S(1)} copy-done((bf16[128,2048]{1,0:T(8,128)(2,1)S(1)}, bf16[128,2048]{1,0:T(8,128)(2,1)}, u32[]{:S(2)}) %copy-start.7) | copy-done | bytes 524312
  7.8 0.0 copy-start.8
  7.8 0.7 %copy-done.8 = f32[128,16]{0,1:T(8,128)S(1)} copy-done((f32[128,16]{0,1:T(8,128)S(1)}, f32[128,16]{0,1:T(8,128)}, u32[]{:S(2)}) %copy-start.8) | copy-done | bytes 8216
  8.5 0.0 copy-start.9
  8.5 0.7 %copy-done.9 = s32[8]{0:T(128)S(1)} copy-done((s32[8]{0:T(128)S(1)}, s32[8]{0:T(128)}, u32[]{:S(2)}) %copy-start.9) | copy-done | bytes 56
  9.2 0.0 copy-start
  9.2 4.2 %kda_slab.2 = (bf16[8,128,256]{2,1,0:T(8,128)(2,1)S(1)}, bf16[128,1024]{1,0:T(8,128)(2,1)S(1)}, f32[128,1024]{1,0:T(8,128)S(1)}) custom-call(s32[8]{0:T(128)S(1)} %copy-done.9, bf16[128,2048]{1,0:T(8,128)(2,1)S(1)} %copy-done.4, bf16[128,2048]{1,0:T(8,128)(2,1)S(1)} %copy-done.5, bf16[128,2048]{1,0:T(8,128)(2,1)S(1)} %copy-done.6, ...), custom_call_target="tpu_custom_call" | custom-call | flops 6710886400 | bytes 2097152 | tf_op jit(solution)/shard_map/kda_slab/pallas_call | solution.py:163
  13.4 0.0 collective-permute-done.3.refs_1_
  13.4 0.0 copy-done
  13.4 0.0 copy-start.1
  13.5 0.0 copy-start.2
  13.5 0.0 copy-start.3
  13.5 0.1 collective-permute-start.5
  13.6 3.1 %collective-permute-start.4 = (bf16[2,576,128]{2,1,0:T(8,128)(2,1)S(1)}, bf16[2,576,128]{2,1,0:T(8,128)(2,1)S(1)}, u32[]{:S(2)}, u32[]{:S(2)}) collective-permute-start(bf16[2,576,128]{2,1,0:T(8,128)(2,1)S(1)} %pad_maximum_fusion), channel_id=1, source_target_pairs={{0,8},{4,12},{8,0},{12,4},{16,24},{20,28},{24,16},{28,20},{1,9},{5... | collective-permute-start | bytes 884744 | tf_op jit(solution)/shard_map/ppermute | solution.py:408
  16.7 0.5 collective-permute-start
  17.2 6.2 %collective-permute-done.5.refs_3_ = bf16[2,576,128]{2,1,0:T(8,128)(2,1)S(1)} collective-permute-done((bf16[2,576,128]{2,1,0:T(8,128)(2,1)S(1)}, bf16[2,576,128]{2,1,0:T(8,128)(2,1)S(1)}, u32[]{:S(2)}, u32[]{:S(2)}) %collective-permute-start.5) | collective-permute-done | bytes 294944 | tf_op jit(solution)/shard_map/ppermute | solution.py:408
  23.5 0.1 collective-permute-start.6
  23.6 0.0 collective-permute-done.4.refs_2_
  23.6 0.5 collective-permute-start.7
  24.1 4.2 %kda_slab.3 = (bf16[8,128,256]{2,1,0:T(8,128)(2,1)S(1)}, bf16[128,1024]{1,0:T(8,128)(2,1)S(1)}, f32[128,1024]{1,0:T(8,128)S(1)}) custom-call(s32[8]{0:T(128)S(1)} %copy-done.9, bf16[128,2048]{1,0:T(8,128)(2,1)S(1)} %copy-done.4, bf16[128,2048]{1,0:T(8,128)(2,1)S(1)} %copy-done.5, bf16[128,2048]{1,0:T(8,128)(2,1)S(1)} %copy-done.6, ...), custom_call_target="tpu_custom_call" | custom-call | flops 6710886400 | bytes 2097152 | tf_op jit(solution)/shard_map/kda_slab/pallas_call | solution.py:163
  28.3 6.4 %collective-permute-done.got_ref = bf16[8,128,256]{2,1,0:T(8,128)(2,1)S(1)} collective-permute-done((bf16[8,128,256]{2,1,0:T(8,128)(2,1)S(1)}, bf16[8,128,256]{2,1,0:T(8,128)(2,1)S(1)}, u32[]{:S(2)}, u32[]{:S(2)}) %collective-permute-start) | collective-permute-done | bytes 524320 | tf_op jit(solution)/shard_map/ppermute | solution.py:408
  34.7 0.3 pair_join.1
  35.0 0.1 collective-permute-start.2
  35.1 0.1 collective-permute-start.1
  35.2 0.0 collective-permute-done.6.refs_4_
  35.2 5.9 %collective-permute-done.7.refs_5_ = bf16[2,576,128]{2,1,0:T(8,128)(2,1)S(1)} collective-permute-done((bf16[2,576,128]{2,1,0:T(8,128)(2,1)S(1)}, bf16[2,576,128]{2,1,0:T(8,128)(2,1)S(1)}, u32[]{:S(2)}, u32[]{:S(2)}) %collective-permute-start.7) | collective-permute-done | bytes 294944 | tf_op jit(solution)/shard_map/ppermute | solution.py:408
  41.0 0.0 copy-done.1
  41.0 0.0 copy-done.2
  41.0 0.0 copy-done.3
  41.0 4.6 %mla_heads.2 = (bf16[640,576]{1,0:T(8,128)(2,1)S(1)}, bf16[128,2048]{1,0:T(8,128)(2,1)}) custom-call(s32[8]{0:T(128)S(1)} %copy-done.9, bf16[128,3072]{1,0:T(8,128)(2,1)S(1)} %copy-done.3, bf16[512,2048]{1,0:T(8,128)(2,1)S(1)} %copy-done.1, bf16[512,2048]{1,0:T(8,128)(2,1)S(1)} %copy-done.2, bf16[576,128]{1,0:T(8,128)(2,1)S(1)} %bitcast.7, ...), custom_call_target="tpu_custom_call" | custom-call | flops 5536481280 | bytes 3072000 | tf_op jit(solution)/shard_map/mla_heads/pallas_call | solution.py:360
  45.7 0.0 collective-permute-done.2.b_ref
  45.7 0.0 collective-permute-done.1.a_ref
  45.7 0.2 pair_step.1
  46.0 0.1 collective-permute-start.9
  46.0 0.1 collective-permute-start.8
  46.1 4.2 %mla_heads.3 = bf16[128,2048]{1,0:T(8,128)(2,1)} custom-call(s32[8]{0:T(128)S(1)} %copy-done.9, bf16[128,3072]{1,0:T(8,128)(2,1)S(1)} %copy-done.3, bf16[512,2048]{1,0:T(8,128)(2,1)S(1)} %copy-done.1, bf16[512,2048]{1,0:T(8,128)(2,1)S(1)} %copy-done.2, bf16[640,576]{1,0:T(8,128)(2,1)S(1)} %get-tuple-element.31.refs_0_, ...), custom_call_target="tpu_custom_call", output_to_operand_aliasing={{}: (5, {})} | custom-call | flops 5536481280 | bytes 3072000 | tf_op jit(solution)/shard_map/mla_heads/pallas_call | solution.py:360
  50.3 2.1 %collective-permute-done.9.b_ref = bf16[8,128,128]{2,1,0:T(8,128)(2,1)S(1)} collective-permute-done((bf16[8,128,128]{2,1,0:T(8,128)(2,1)S(1)}, bf16[8,128,128]{2,1,0:T(8,128)(2,1)S(1)}, u32[]{:S(2)}, u32[]{:S(2)}) %collective-permute-start.9) | collective-permute-done | bytes 262176 | tf_op jit(solution)/shard_map/ppermute | solution.py:408
  52.4 0.3 collective-permute-done.8.a_ref
  52.7 0.3 slab_states.1
  53.0 1.8 %collective-permute-start.10 = (bf16[8,128,128]{2,1,0:T(8,128)(2,1)S(1)}, bf16[8,128,128]{2,1,0:T(8,128)(2,1)S(1)}, u32[]{:S(2)}, u32[]{:S(2)}) collective-permute-start(bf16[8,128,128]{2,1,0:T(8,128)(2,1)S(1)} %get-tuple-element.35), channel_id=1, source_target_pairs={{0,4},{4,0},{8,12},{12,8},{16,20},{20,16},{24,28},{28,24},{1,5},{5... | collective-permute-start | bytes 786440 | tf_op jit(solution)/shard_map/ppermute | solution.py:408
  54.8 0.9 %kda_out.2.rest_0_ = bf16[128,2048]{1,0:T(8,128)(2,1)} custom-call(bf16[128,1024]{1,0:T(8,128)(2,1)S(1)} %get-tuple-element.36.qe_ref, f32[128,1024]{1,0:T(8,128)S(1)} %get-tuple-element.37.lo_ref, bf16[8,128,128]{2,1,0:T(8,128)(2,1)S(1)} %get-tuple-element.38.s_ref), custom_call_target="tpu_custom_call" | custom-call | tf_op jit(solution)/shard_map/kda_out/pallas_call | solution.py:272
  55.7 3.7 %collective-permute-done.10.s_ref = bf16[8,128,128]{2,1,0:T(8,128)(2,1)S(1)} collective-permute-done((bf16[8,128,128]{2,1,0:T(8,128)(2,1)S(1)}, bf16[8,128,128]{2,1,0:T(8,128)(2,1)S(1)}, u32[]{:S(2)}, u32[]{:S(2)}) %collective-permute-start.10) | collective-permute-done | bytes 262176 | tf_op jit(solution)/shard_map/ppermute | solution.py:408
  59.4 0.9 %kda_out.3 = bf16[128,2048]{1,0:T(8,128)(2,1)} custom-call(bf16[128,1024]{1,0:T(8,128)(2,1)S(1)} %get-tuple-element.21.qe_ref, f32[128,1024]{1,0:T(8,128)S(1)} %get-tuple-element.22.lo_ref, bf16[8,128,128]{2,1,0:T(8,128)(2,1)S(1)} %collective-permute-done.10.s_ref, bf16[128,2048]{1,0:T(8,128)(2,1)} %kda_out.2.rest_0_), custom_call_target="tpu_custom_call", output_to_operand_aliasing={{}: (3, {})} | custom-call | tf_op jit(solution)/shard_map/kda_out/pallas_call | solution.py:272
  (1 shorter events, 0.0 us)
Async XLA Ops:
  0.6 12.8 %collective-permute-start.3 = (bf16[576,128]{1,0:T(8,128)(2,1)}, bf16[576,128]{1,0:T(8,128)(2,1)S(1)}, u32[]{:S(2)}, u32[]{:S(2)}) collective-permute-start(bf16[576,128]{1,0:T(8,128)(2,1)} %bitcast.5), channel_id=1, source_target_pairs={{0,4},{4,0},{8,12},{12,8},{16,20},{20,16},{24,28},{28,24},{1,5},{5... | collective-permute-start | bytes 442376 | tf_op jit(solution)/shard_map/ppermute | solution.py:408
  3.6 1.0 %copy-start.4 = (bf16[128,2048]{1,0:T(8,128)(2,1)S(1)}, bf16[128,2048]{1,0:T(8,128)(2,1)}, u32[]{:S(2)}) copy-start(bf16[128,2048]{1,0:T(8,128)(2,1)} %refs_0_.3) | copy-start | bytes 1572868
  4.7 1.0 %copy-start.5 = (bf16[128,2048]{1,0:T(8,128)(2,1)S(1)}, bf16[128,2048]{1,0:T(8,128)(2,1)}, u32[]{:S(2)}) copy-start(bf16[128,2048]{1,0:T(8,128)(2,1)} %refs_1_.3) | copy-start | bytes 1572868
  5.7 1.0 %copy-start.6 = (bf16[128,2048]{1,0:T(8,128)(2,1)S(1)}, bf16[128,2048]{1,0:T(8,128)(2,1)}, u32[]{:S(2)}) copy-start(bf16[128,2048]{1,0:T(8,128)(2,1)} %refs_2_.3) | copy-start | bytes 1572868
  6.8 1.0 %copy-start.7 = (bf16[128,2048]{1,0:T(8,128)(2,1)S(1)}, bf16[128,2048]{1,0:T(8,128)(2,1)}, u32[]{:S(2)}) copy-start(bf16[128,2048]{1,0:T(8,128)(2,1)} %refs_3_.3) | copy-start | bytes 1572868
  7.8 0.7 %copy-start.8 = (f32[128,16]{0,1:T(8,128)S(1)}, f32[128,16]{0,1:T(8,128)}, u32[]{:S(2)}) copy-start(f32[128,16]{0,1:T(8,128)} %param.14) | copy-start | bytes 24580
  8.5 0.7 %copy-start.9 = (s32[8]{0:T(128)S(1)}, s32[8]{0:T(128)}, u32[]{:S(2)}) copy-start(s32[8]{0:T(128)} %lengths.3) | copy-start | bytes 100
  9.2 4.2 %copy-start = (bf16[128,576]{0,1:T(8,128)(2,1)S(1)}, bf16[128,576]{0,1:T(8,128)(2,1)}, u32[]{:S(2)}) copy-start(bf16[128,576]{0,1:T(8,128)(2,1)} %param.16) | copy-start | bytes 442372
  13.4 27.6 %copy-start.1 = (bf16[512,2048]{1,0:T(8,128)(2,1)S(1)}, bf16[512,2048]{1,0:T(8,128)(2,1)}, u32[]{:S(2)}) copy-start(bf16[512,2048]{1,0:T(8,128)(2,1)} %ku_ref.3) | copy-start | bytes 6291460
  13.5 27.6 %copy-start.2 = (bf16[512,2048]{1,0:T(8,128)(2,1)S(1)}, bf16[512,2048]{1,0:T(8,128)(2,1)}, u32[]{:S(2)}) copy-start(bf16[512,2048]{1,0:T(8,128)(2,1)} %vu_ref.3) | copy-start | bytes 6291460
  13.5 27.6 %copy-start.3 = (bf16[128,3072]{1,0:T(8,128)(2,1)S(1)}, bf16[128,3072]{1,0:T(8,128)(2,1)}, u32[]{:S(2)}) copy-start(bf16[128,3072]{1,0:T(8,128)(2,1)} %q_ref.3) | copy-start | bytes 2359300
  13.5 10.0 %collective-permute-start.5 = (bf16[2,576,128]{2,1,0:T(8,128)(2,1)S(1)}, bf16[2,576,128]{2,1,0:T(8,128)(2,1)S(1)}, u32[]{:S(2)}, u32[]{:S(2)}) collective-permute-start(bf16[2,576,128]{2,1,0:T(8,128)(2,1)S(1)} %pad_maximum_fusion), channel_id=1, source_target_pairs={{0,4},{4,0},{8,16},{12,20},{16,8},{20,12},{24,28},{28,24},{1,5},{5... | collective-permute-start | bytes 884744 | tf_op jit(solution)/shard_map/ppermute | solution.py:408
  13.6 10.0 %collective-permute-start.4 = (bf16[2,576,128]{2,1,0:T(8,128)(2,1)S(1)}, bf16[2,576,128]{2,1,0:T(8,128)(2,1)S(1)}, u32[]{:S(2)}, u32[]{:S(2)}) collective-permute-start(bf16[2,576,128]{2,1,0:T(8,128)(2,1)S(1)} %pad_maximum_fusion), channel_id=1, source_target_pairs={{0,8},{4,12},{8,0},{12,4},{16,24},{20,28},{24,16},{28,20},{1,9},{5... | collective-permute-start | bytes 884744 | tf_op jit(solution)/shard_map/ppermute | solution.py:408
  16.7 18.0 %collective-permute-start = (bf16[8,128,256]{2,1,0:T(8,128)(2,1)S(1)}, bf16[8,128,256]{2,1,0:T(8,128)(2,1)S(1)}, u32[]{:S(2)}, u32[]{:S(2)}) collective-permute-start(bf16[8,128,256]{2,1,0:T(8,128)(2,1)S(1)} %get-tuple-element.24), channel_id=1, source_target_pairs={{0,4},{4,0},{8,12},{12,8},{16,20},{20,16},{24,28},{28,24},{1,5},{5... | collective-permute-start | bytes 1572872 | tf_op jit(solution)/shard_map/ppermute | solution.py:408
  23.5 11.7 %collective-permute-start.6 = (bf16[2,576,128]{2,1,0:T(8,128)(2,1)S(1)}, bf16[2,576,128]{2,1,0:T(8,128)(2,1)S(1)}, u32[]{:S(2)}, u32[]{:S(2)}) collective-permute-start(bf16[2,576,128]{2,1,0:T(8,128)(2,1)S(1)} %collective-permute-done.5.refs_3_), channel_id=1, source_target_pairs={{0,8},{4,12},{8,0},{12,4},{16,24},{20,28},{24,16},{28,20},{1,9},{5... | collective-permute-start | bytes 884744 | tf_op jit(solution)/shard_map/ppermute | solution.py:408
  23.6 17.4 %collective-permute-start.7 = (bf16[2,576,128]{2,1,0:T(8,128)(2,1)S(1)}, bf16[2,576,128]{2,1,0:T(8,128)(2,1)S(1)}, u32[]{:S(2)}, u32[]{:S(2)}) collective-permute-start(bf16[2,576,128]{2,1,0:T(8,128)(2,1)S(1)} %collective-permute-done.4.refs_2_), channel_id=1, source_target_pairs={{0,4},{4,0},{8,16},{12,20},{16,8},{20,12},{24,28},{28,24},{1,5},{5... | collective-permute-start | bytes 884744 | tf_op jit(solution)/shard_map/ppermute | solution.py:408
  35.0 10.7 %collective-permute-start.2 = (bf16[8,128,128]{2,1,0:T(8,128)(2,1)S(1)}, bf16[8,128,128]{2,1,0:T(8,128)(2,1)S(1)}, u32[]{:S(2)}, u32[]{:S(2)}) collective-permute-start(bf16[8,128,128]{2,1,0:T(8,128)(2,1)S(1)} %get-tuple-element.26.pu_ref), channel_id=1, source_target_pairs={{0,4},{4,0},{8,16},{12,20},{16,8},{20,12},{24,28},{28,24},{1,5},{5... | collective-permute-start | bytes 786440 | tf_op jit(solution)/shard_map/ppermute | solution.py:408
  35.1 10.6 %collective-permute-start.1 = (bf16[8,128,128]{2,1,0:T(8,128)(2,1)S(1)}, bf16[8,128,128]{2,1,0:T(8,128)(2,1)S(1)}, u32[]{:S(2)}, u32[]{:S(2)}) collective-permute-start(bf16[8,128,128]{2,1,0:T(8,128)(2,1)S(1)} %get-tuple-element.26.pu_ref), channel_id=1, source_target_pairs={{0,8},{4,12},{8,0},{12,4},{16,24},{20,28},{24,16},{28,20},{1,9},{5... | collective-permute-start | bytes 786440 | tf_op jit(solution)/shard_map/ppermute | solution.py:408
  46.0 6.4 %collective-permute-start.9 = (bf16[8,128,128]{2,1,0:T(8,128)(2,1)S(1)}, bf16[8,128,128]{2,1,0:T(8,128)(2,1)S(1)}, u32[]{:S(2)}, u32[]{:S(2)}) collective-permute-start(bf16[8,128,128]{2,1,0:T(8,128)(2,1)S(1)} %pair_step.1), channel_id=1, source_target_pairs={{0,4},{4,0},{8,16},{12,20},{16,8},{20,12},{24,28},{28,24},{1,5},{5... | collective-permute-start | bytes 786440 | tf_op jit(solution)/shard_map/ppermute | solution.py:408
  46.0 6.6 %collective-permute-start.8 = (bf16[8,128,128]{2,1,0:T(8,128)(2,1)S(1)}, bf16[8,128,128]{2,1,0:T(8,128)(2,1)S(1)}, u32[]{:S(2)}, u32[]{:S(2)}) collective-permute-start(bf16[8,128,128]{2,1,0:T(8,128)(2,1)S(1)} %pair_step.1), channel_id=1, source_target_pairs={{0,8},{4,12},{8,0},{12,4},{16,24},{20,28},{24,16},{28,20},{1,9},{5... | collective-permute-start | bytes 786440 | tf_op jit(solution)/shard_map/ppermute | solution.py:408
  53.0 6.4 %collective-permute-start.10 = (bf16[8,128,128]{2,1,0:T(8,128)(2,1)S(1)}, bf16[8,128,128]{2,1,0:T(8,128)(2,1)S(1)}, u32[]{:S(2)}, u32[]{:S(2)}) collective-permute-start(bf16[8,128,128]{2,1,0:T(8,128)(2,1)S(1)} %get-tuple-element.35), channel_id=1, source_target_pairs={{0,4},{4,0},{8,12},{12,8},{16,20},{20,16},{24,28},{28,24},{1,5},{5... | collective-permute-start | bytes 786440 | tf_op jit(solution)/shard_map/ppermute | solution.py:408

commit v3 on v2

--- a/solution.py
+++ b/solution.py
@@ -13,6 +13,7 @@
 ROPE = 64
 LATENT = 512
 VMEM = 20 * 1024 * 1024
+ALL_VMEM = 56 * 1024 * 1024
 WHOLE = pl.BlockSpec(memory_space=pltpu.VMEM)
 SCALARS = pl.BlockSpec(memory_space=pltpu.SMEM)
 FAR = pl.BlockSpec(memory_space=pltpu.HBM)
@@ -42,14 +43,20 @@
     return total
 
 
-def kda_kernel(ndocs, flip, sc, *refs):
-    sources, (b_ref, mu_ref, qe_ref, lo_ref), blocks, sems = refs[:4], refs[4:8], refs[8:12], refs[12]
+def kda_kernel(ndocs, flip, *refs):
+    sources, small = refs[:4], refs[4:6]
+    mu_ref, qe_ref, lo_ref = refs[6:9]
+    blocks, (b_ref, sc, sems, small_sems) = refs[9:13], refs[13:]
     rows, width = blocks[0].shape
     place = lax.axis_index("ctx")
     side = (place + flip) % 2
     start = pl.multiple_of(side * width, width)
-    parts = 2
+    parts = sems.shape[1]
     part = width // parts
+    small_copies = [
+        pltpu.make_async_copy(source, block, small_sems.at[j])
+        for j, (source, block) in enumerate(zip(small, (sc, b_ref)))
+    ]
     copies = [
         [
             pltpu.make_async_copy(
@@ -61,6 +68,8 @@
         ]
         for i in range(parts)
     ]
+    for copy in small_copies:
+        copy.start()
     for group in copies:
         for copy in group:
             copy.start()
@@ -71,22 +80,12 @@
     first = place * rows
     ri = lax.broadcasted_iota(jnp.int32, (rows, rows), 0)
     ci = lax.broadcasted_iota(jnp.int32, (rows, rows), 1)
-    doc_r = doc_of(first + ri, sc, ndocs)
-    doc_c = doc_of(first + ci, sc, ndocs)
-    prev = doc_of(first - 1, sc, ndocs)
-    last = doc_of(first + rows - 1, sc, ndocs)
-    same = doc_r == doc_c
-    strict = same & (ri > ci)
-    causal = same & (ri >= ci)
-    follow = (doc_r == prev).astype(F32)
-    tail = (doc_r == last).astype(F32)
-    keep = (last == prev).astype(F32)
-    eye = (ri == ci).astype(F32)
     tri = (ri >= ci).astype(BF)
     low = ci < half
+    eye = (ri == ci).astype(F32)
 
     hs = range(heads)
-    lhs, km, lhs_off, km_off, rhs, kt, qg, gl, gain = [], [], [], [], [], [], [], [], []
+    kept, lhs, km, lhs_off, km_off = [], [], [], [], []
     for h in hs:
         cols = slice(h * 128, (h + 1) * 128)
         if h % (heads // parts) == 0:
@@ -96,11 +95,9 @@
             cum_part = mm(tri, g_ref[:, i * part : (i + 1) * part])
         q = q_ref[:, cols].astype(F32)
         k = k_ref[:, cols].astype(F32)
-        v = v_ref[:, cols].astype(F32)
         qn = q * lax.rsqrt(jnp.sum(q * q, axis=1, keepdims=True) + 1e-06)
         kn = k * lax.rsqrt(jnp.sum(k * k, axis=1, keepdims=True) + 1e-06)
         cum = cum_part[:, h * 128 - i * part : (h + 1) * 128 - i * part]
-        b = jnp.sum(eye * b_ref[pl.ds(base + h, 1), :], axis=1, keepdims=True)
         quarter = half // 2
         m0 = cum[quarter - 1 : quarter]
         m1 = cum[half + quarter - 1 : half + quarter]
@@ -119,12 +116,31 @@
             jnp.concatenate([(kn[half:] * op).astype(BF), (qn[half:] * op).astype(BF)], axis=0)
         )
         km_off.append((kn * om).astype(BF))
+        kept.append((kn * growth, kn * trail, qn * growth, jnp.exp(end)))
+
+    for copy in small_copies:
+        copy.wait()
+    doc_r = doc_of(first + ri, sc, ndocs)
+    doc_c = doc_of(first + ci, sc, ndocs)
+    prev = doc_of(first - 1, sc, ndocs)
+    last = doc_of(first + rows - 1, sc, ndocs)
+    same = doc_r == doc_c
+    strict = same & (ri > ci)
+    causal = same & (ri >= ci)
+    follow = (doc_r == prev).astype(F32)
+    tail = (doc_r == last).astype(F32)
+    keep = (last == prev).astype(F32)
+    rhs, kt, qg, gl, gain = [], [], [], [], []
+    for h in hs:
+        grown, trailed, queried, ended = kept[h]
+        b = jnp.sum(eye * b_ref[pl.ds(base + h, 1), :], axis=1, keepdims=True)
+        v = v_ref[:, h * 128 : (h + 1) * 128].astype(F32)
         rhs.append(
-            jnp.concatenate([(kn * growth * (b * follow)).astype(BF), (v * b).astype(BF)], axis=1)
+            jnp.concatenate([(grown * (b * follow)).astype(BF), (v * b).astype(BF)], axis=1)
         )
-        kt.append((kn * trail * tail).astype(BF))
-        qg.append(qn * growth * follow)
-        gl.append(jnp.exp(end) * keep)
+        kt.append((trailed * tail).astype(BF))
+        qg.append(queried * follow)
+        gl.append(ended * keep)
         gain.append(b)
 
     a, mix = [], []
@@ -162,20 +178,26 @@
     heads, ndocs = b.shape[0], lengths.shape[0]
     return pl.pallas_call(
         functools.partial(kda_kernel, ndocs, flip),
-        in_specs=[SCALARS, FAR, FAR, FAR, FAR, WHOLE],
+        in_specs=[FAR] * 6,
         out_specs=[WHOLE, WHOLE, WHOLE],
         out_shape=[
             jax.ShapeDtypeStruct((heads // 2, 128, 256), BF),
             jax.ShapeDtypeStruct((rows, width), BF),
             jax.ShapeDtypeStruct((rows, width), F32),
         ],
-        scratch_shapes=[pltpu.VMEM((rows, width), BF)] * 4 + [pltpu.SemaphoreType.DMA((4, 2))],
-        compiler_params=pltpu.CompilerParams(vmem_limit_bytes=VMEM),
+        scratch_shapes=[pltpu.VMEM((rows, width), BF)] * 4
+        + [
+            pltpu.VMEM(b.shape, F32),
+            pltpu.SMEM(lengths.shape, jnp.int32),
+            pltpu.SemaphoreType.DMA((4, 4)),
+            pltpu.SemaphoreType.DMA((2,)),
+        ],
+        compiler_params=pltpu.CompilerParams(vmem_limit_bytes=ALL_VMEM if flip else VMEM),
         cost_estimate=pl.CostEstimate(
             flops=heads * 2 * 128**3 * 100, bytes_accessed=width * rows * 16, transcendentals=0
         ),
         name="kda_slab",
-    )(lengths, q, k, v, g, b)
+    )(q, k, v, g, lengths, b)
 
 
 def pair_kernel(own_ref, got_ref, pm_ref, pu_ref):
@@ -281,41 +303,60 @@
     )(*args)
 
 
-def window_rows(place, reach, rows, own_ref, mate_ref, far, out_ref):
-    def put(w, block):
-        at = slice(w * rows, (w + 1) * rows)
-        out_ref[at, :LATENT] = block[:LATENT].T
-        out_ref[at, LATENT:] = block[LATENT:].T
-
+def window_rows(place, reach, rows, own_ref, mate_ref, out_ref):
     for column in range(2):
-        for parity in range(2):
-
-            @pl.when((place % 2 == column) & ((place // 2) % 2 == parity))
+
+        @pl.when(place % 2 == column)
+        def _():
+            for w in range(reach + 1):
+                back = reach // 2 - (w + column) // 2
+                block = (mate_ref if (w + column) % 2 != column else own_ref)[back]
+                at = slice(w * rows, (w + 1) * rows)
+                out_ref[at, :LATENT] = block[:LATENT].T
+                out_ref[at, LATENT:] = block[LATENT:].T
+
+
+def pick_kernel(own_ref, *refs):
+    out_ref = refs[-1]
+    out_ref[0] = own_ref[...]
+    parity = (lax.axis_index("ctx") // 2) % 2
+    for back in range(out_ref.shape[0] - 1):
+        for kind in range(2):
+
+            @pl.when(parity == 1 - kind)
             def _():
-                for w in range(reach + 1):
-                    back = reach // 2 - (w + column) // 2
-                    other = ((w + column) % 2) ^ column
-                    if back == 0:
-                        put(w, (mate_ref if other else own_ref)[...])
-                    else:
-                        put(w, far[2 * (back - 1) + 1 - parity][other])
-
-
-def mla_kernel(ndocs, reach, count, first, lengths, q_ref, ku_ref, vu_ref, *refs):
-    out_ref, held_ref, bias_ref, sem = refs[-4:]
+                out_ref[back + 1] = refs[2 * back + kind][...]
+
+
+def mask_kernel(ndocs, lengths, bias_ref):
+    rows, keys = bias_ref.shape
     place = lax.axis_index("ctx")
-    rows = q_ref.shape[0]
-    keys = (reach + 1) * rows
-    if count is None:
-        lat_ref = refs[0]
-    else:
-        own_ref, mate_ref, lat_ref = refs[0], refs[1], refs[2 + count]
-        window_rows(place, reach, rows, own_ref, mate_ref, refs[2 : 2 + count], lat_ref)
     here = place * rows + lax.broadcasted_iota(jnp.int32, (rows, 1), 0)
-    there = (place - reach) * rows + lax.broadcasted_iota(jnp.int32, (1, keys), 1)
+    there = (place + 1) * rows - keys + lax.broadcasted_iota(jnp.int32, (1, keys), 1)
     doc_q = doc_of(here, lengths, ndocs)
     doc_k = doc_of(there, lengths, ndocs)
     bias_ref[...] = jnp.where((there <= here) & (doc_q == doc_k), 0.0, NEG)
+
+
+def mask(lengths, rows, keys):
+    return pl.pallas_call(
+        functools.partial(mask_kernel, lengths.shape[0]),
+        in_specs=[SCALARS],
+        out_specs=WHOLE,
+        out_shape=jax.ShapeDtypeStruct((rows, keys), F32),
+        compiler_params=pltpu.CompilerParams(vmem_limit_bytes=VMEM // 2),
+        name="window_mask",
+    )(lengths)
+
+
+def mla_kernel(reach, fresh, first, bias_ref, q_ref, ku_ref, vu_ref, *refs):
+    out_ref, held_ref, sem = refs[-3:]
+    rows = q_ref.shape[0]
+    if not fresh:
+        lat_ref = refs[0]
+    else:
+        lat_ref = refs[2]
+        window_rows(lax.axis_index("ctx"), reach, rows, *refs[:2], lat_ref)
 
     factor = math.log2(math.e) / math.sqrt(NOPE + ROPE)
     lat = lat_ref[:, :LATENT]
@@ -345,12 +386,12 @@
     copy.wait()
 
 
-def mla(lengths, q, ku, vu, blocks, previous, reach, first, count):
+def mla(bias, q, ku, vu, blocks, previous, reach, first, count):
     rows = q.shape[0]
     heads = ku.shape[1] // NOPE
     keys = (reach + 1) * rows
-    args = [lengths, q, ku, vu, *blocks]
-    specs = [SCALARS] + [WHOLE] * (len(args) - 1)
+    args = [bias, q, ku, vu, *blocks]
+    specs = [WHOLE] * len(args)
     out = jax.ShapeDtypeStruct((rows, heads * 128), BF)
     aliases = {}
     if previous is not None:
@@ -360,9 +401,8 @@
     return pl.pallas_call(
         functools.partial(
             mla_kernel,
-            lengths.shape[0],
             reach,
-            len(blocks) - 2 if previous is None else None,
+            previous is None,
             first,
         ),
         in_specs=specs,
@@ -372,7 +412,6 @@
         else out,
         scratch_shapes=[
             pltpu.VMEM((rows, count * 128), BF),
-            pltpu.VMEM((rows, keys), F32),
             pltpu.SemaphoreType.DMA,
         ],
         input_output_aliases=aliases,
@@ -386,26 +425,25 @@
     )(*args)
 
 
-def repaired(n, wanted):
-    left = [i for i in range(n) if i not in wanted]
-    out = dict(wanted)
-    for a, b in zip(left[::2], left[1::2]):
-        out[a], out[b] = b, a
-    return [out[i] for i in range(n)]
-
-
 def routes(n):
     mate = [i ^ 1 for i in range(n)]
-    up = repaired(n, {i: i ^ 2 for i in range(n)})
+    up = [i ^ 2 for i in range(n)]
     middle = {}
     for pair in range(1, n // 2 - 1, 2):
         for c in range(2):
             middle[2 * pair + c], middle[2 * pair + 2 + c] = 2 * pair + 2 + c, 2 * pair + c
-    return mate, up, repaired(n, middle)
+    return mate, up, middle
 
 
 def swap(x, table):
-    return lax.ppermute(x, "ctx", list(enumerate(table)))
+    n, m = lax.axis_size("ctx"), lax.axis_size("batch")
+    if isinstance(table, list):
+        return lax.ppermute(x, "ctx", list(enumerate(table)))
+    pairs = []
+    for i in range(n):
+        for j in range(m):
+            pairs.append((i * m + j, table[i] * m + j if i in table else i * m + (j ^ 1)))
+    return lax.ppermute(x, ("ctx", "batch"), pairs)
 
 
 def local(
@@ -428,21 +466,30 @@
     kda_args = (doc_lengths, kda_query, kda_key, kda_value, log_decay, write_rate.T)
 
     lat = latents.T
-    lat_mate = swap(lat, mate)
+    shape = (heads // 2, 128, 128)
     mu_away, qe_away, lo_away = kda_half(1, *kda_args)
     mu_got = swap(mu_away, mate)
-    lat_mate, _ = lax.optimization_barrier((lat_mate, mu_away))
-    both = jnp.stack([lat, lat_mate])
-    blocks = [lat, lat_mate]
-    a = b = both
-    for _ in range(rounds):
-        a, b = swap(b, up), swap(a, middle)
-        blocks += [a, b]
     mu_own, qe_own, lo_own = kda_half(0, *kda_args)
+    early, _ = lax.optimization_barrier((lat, mu_away))
+    moved = [(swap(early, up), swap(early, middle))]
+    mu_own, *moved[0] = lax.optimization_barrier((mu_own, *moved[0]))
+    for _ in range(rounds - 1):
+        a, b = moved[-1]
+        moved.append((swap(b, up), swap(a, middle)))
+    (lat_own,) = whole_call(
+        pick_kernel,
+        "pick_latents",
+        [lat, *[x for ab in moved for x in ab]],
+        [(rounds + 1, *lat.shape)],
+    )
+    lat_mate = swap(lat_own, mate)
+    pm, pu = whole_call(pair_kernel, "pair_join", [mu_own, mu_got], [shape, shape])
+    later, _ = lax.optimization_barrier((doc_lengths, mu_own))
+    bias = mask(later, latents.shape[0], (reach + 1) * latents.shape[0])
 
     def attend(latent_blocks, previous, first, count):
         return mla(
-            doc_lengths,
+            bias,
             mla_query,
             key_up,
             value_up,
@@ -453,21 +500,20 @@
             count,
         )
 
-    shape = (heads // 2, 128, 128)
-    pm, pu = whole_call(pair_kernel, "pair_join", [mu_own, mu_got], [shape, shape])
     state = pu
     for step in range(rounds):
         a, b = swap(state, up), swap(state, middle)
-        if step == 0:
-            window, mla_out = attend(blocks, None, 0, heads // 2)
-            a, b, window = lax.optimization_barrier((a, b, window))
         if step < rounds - 1:
             (state,) = whole_call(step_kernel, "pair_step", [pm, pu, a, b], [shape])
-    mla_out = attend([window], mla_out, heads // 2, heads // 2)
-    a, b, mla_out = lax.optimization_barrier((a, b, mla_out))
+    lat_own, _ = lax.optimization_barrier((lat_own, state))
+    window, mla_out = attend([lat_own, lat_mate], None, 0, heads // 2)
+    a, b, window = lax.optimization_barrier((a, b, window))
     s_own, s_send = whole_call(split_kernel, "slab_states", [mu_own, mu_got, a, b], [shape, shape])
     s_got = swap(s_send, mate)
+    window, _ = lax.optimization_barrier((window, s_send))
+    mla_out = attend([window], mla_out, heads // 2, heads // 2)
     out = final(0, qe_own, lo_own, s_own, heads, None)
+    s_got, mla_out = lax.optimization_barrier((s_got, mla_out))
     kda_out = final(1, qe_away, lo_away, s_got, heads, out)
     return (kda_out, mla_out)
 

time: 60.8 us -> 49.5 us (0.81)
  waiting for transfers between devices: 24.6 us -> 12.2 us
  local copies, waits for them, and re-layouts: 5.54 us -> 0.06 us
  starting transfers between devices: 9.47 us -> 14.7 us
  Pallas kernels: 19.8 us -> 21.2 us
    ppermute x11 -> x7, waiting for transfers between devices: 24.6 us -> 12.2 us  [swap(): return lax.ppermute(x, 'ctx', list(enumerate(table)))]
    unnamed x20 -> x24, local copies, waits for them, and re-layouts: 5.54 us -> 0.06 us
    ppermute x11 -> x7, starting transfers between devices: 9.47 us -> 14.7 us  [swap(): return lax.ppermute(x, 'ctx', list(enumerate(table)))]
    pallas_call x4 -> x5, Pallas kernels: 17.2 us -> 18.4 us  [the longest x2 10.3 us: kda_half(): pl.pallas_call(functools.partial(kda_kernel, ndocs, flip), in_specs=[FAR]...]
  transfers between devices with their start and end apart: 11 -> 11, of which waited for: 6 -> 5; matrix products, arithmetic and copies ran while one was open for 0% -> 0% of each run, Pallas kernels for 30% -> 28%
where the time goes in v3:
time: 49.5 us; the launch traced here: 49.3 us
  Pallas kernels  21.2 us (43%)
  starting transfers between devices  14.7 us (30%)
  waiting for transfers between devices  12.2 us (25%)
  between operations  1.04 us (2%)
    ppermute x7, starting transfers between devices, swap(): return lax.ppermute(x, 'ctx', list(enumerate(table)))  14.7 us
    ppermute x7, waiting for transfers between devices, swap(): return lax.ppermute(x, 'ctx', list(enumerate(table)))  12.2 us
    pallas_call x2, Pallas kernels, kda_half(): pl.pallas_call(functools.partial(kda_kernel, ndocs, flip), in_specs=[FAR]...  10.3 us
    pallas_call x2, Pallas kernels, mla(): pl.pallas_call(functools.partial(mla_kernel, reach, previous is None, fir...  7.48 us
    pallas_call x2, Pallas kernels, final(): pl.pallas_call(functools.partial(final_kernel, flip), in_specs=specs, out...  1.8 us
    pallas_call x4, Pallas kernels, whole_call(): pl.pallas_call(kernel, in_specs=[WHOLE] * len(args), out_specs=[WHOLE] *...  1.01 us
  transfers between devices with their start and end apart: 11, of which 5 were waited for; matrix products, arithmetic and copies ran while one was open for 0% of the time, Pallas kernels for 28%

profile of v3, /device:TPU:0, one launch (start us, length us, event | category | flops | bytes accessed | tf_op | source)
XLA Modules:
  0.0 49.3 jit_solution(10857005699961619465)
XLA Ops:
  0.6 0.0 copy-start.2
  0.6 0.0 copy-start.3
  0.7 0.0 copy-start.7
  0.7 0.0 copy-start.8
  0.7 0.0 copy-start.9
  0.7 0.0 copy-start.10
  0.7 0.0 copy-start.11
  0.7 6.1 %kda_slab.2 = (bf16[8,128,256]{2,1,0:T(8,128)(2,1)}, bf16[128,1024]{1,0:T(8,128)(2,1)}, f32[128,1024]{1,0:T(8,128)}) custom-call(bf16[128,2048]{1,0:T(8,128)(2,1)} %refs_0_.3, bf16[128,2048]{1,0:T(8,128)(2,1)} %refs_1_.3, bf16[128,2048]{1,0:T(8,128)(2,1)} %refs_2_.3, bf16[128,2048]{1,0:T(8,128)(2,1)} %refs_3_.3, s32[8]{0:T(128)} %lengths, f32[16,128]{1,0:T(8,128)} %bitcast.5), custom_call_target="tpu_custom_call" | custom-call | flops 6710886400 | bytes 2097152 | tf_op jit(solution)/shard_map/kda_slab/pallas_call | solution.py:179
  6.8 0.0 copy-done.2
  6.8 3.1 %collective-permute-start = (bf16[576,128]{1,0:T(8,128)(2,1)S(1)}, bf16[576,128]{1,0:T(8,128)(2,1)S(1)}, u32[]{:S(2)}, u32[]{:S(2)}) collective-permute-start(bf16[576,128]{1,0:T(8,128)(2,1)S(1)} %bitcast.2), channel_id=1, source_target_pairs={{0,8},{4,12},{8,0},{12,4},{16,24},{20,28},{24,16},{28,20},{1,9},{5... | collective-permute-start | bytes 442376 | tf_op jit(solution)/shard_map/ppermute | solution.py:441
  9.9 0.0 collective-permute-start.1
  9.9 1.5 %collective-permute-start.2 = (bf16[8,128,256]{2,1,0:T(8,128)(2,1)}, bf16[8,128,256]{2,1,0:T(8,128)(2,1)S(1)}, u32[]{:S(2)}, u32[]{:S(2)}) collective-permute-start(bf16[8,128,256]{2,1,0:T(8,128)(2,1)} %get-tuple-element.29), channel_id=1, source_target_pairs={{0,4},{4,0},{8,12},{12,8},{16,20},{20,16},{24,28},{28,24},{1,5},{5... | collective-permute-start | bytes 1572872 | tf_op jit(solution)/shard_map/ppermute | solution.py:441
  11.4 0.0 copy-done.3
  11.4 0.0 copy-done.7
  11.4 0.0 copy-done.8
  11.4 0.0 copy-done.9
  11.4 0.0 copy-done.10
  11.4 0.0 copy-done.11
  11.4 0.0 copy-start.5
  11.5 4.2 %kda_slab.3 = (bf16[8,128,256]{2,1,0:T(8,128)(2,1)S(1)}, bf16[128,1024]{1,0:T(8,128)(2,1)S(1)}, f32[128,1024]{1,0:T(8,128)S(1)}) custom-call(bf16[128,2048]{1,0:T(8,128)(2,1)S(1)} %copy-done.7, bf16[128,2048]{1,0:T(8,128)(2,1)S(1)} %copy-done.8, bf16[128,2048]{1,0:T(8,128)(2,1)S(1)} %copy-done.9, bf16[128,2048]{1,0:T(8,128)(2,1)S(1)} %copy-done.10, ...), custom_call_target="tpu_custom_call" | custom-call | flops 6710886400 | bytes 2097152 | tf_op jit(solution)/shard_map/kda_slab/pallas_call | solution.py:179
  15.6 0.0 copy-start.4
  15.6 0.0 copy-start.6
  15.7 0.0 collective-permute-done.refs_0_
  15.7 0.0 collective-permute-done.1.refs_1_
  15.7 3.2 %collective-permute-start.7 = (bf16[576,128]{1,0:T(8,128)(2,1)S(1)}, bf16[576,128]{1,0:T(8,128)(2,1)S(1)}, u32[]{:S(2)}, u32[]{:S(2)}) collective-permute-start(bf16[576,128]{1,0:T(8,128)(2,1)S(1)} %collective-permute-done.1.refs_1_), channel_id=1, source_target_pairs={{0,8},{4,12},{8,0},{12,4},{16,24},{20,28},{24,16},{28,20},{1,9},{5... | collective-permute-start | bytes 442376 | tf_op jit(solution)/shard_map/ppermute | solution.py:441
  18.9 0.0 collective-permute-start.8
  18.9 3.1 %collective-permute-done.7.refs_2_ = bf16[576,128]{1,0:T(8,128)(2,1)S(1)} collective-permute-done((bf16[576,128]{1,0:T(8,128)(2,1)S(1)}, bf16[576,128]{1,0:T(8,128)(2,1)S(1)}, u32[]{:S(2)}, u32[]{:S(2)}) %collective-permute-start.7) | collective-permute-done | bytes 147488 | tf_op jit(solution)/shard_map/ppermute | solution.py:441
  22.0 0.0 collective-permute-done.8.refs_3_
  22.1 0.6 %collective-permute-start.9 = (bf16[3,576,128]{2,1,0:T(8,128)(2,1)S(1)}, bf16[3,576,128]{2,1,0:T(8,128)(2,1)S(1)}, u32[]{:S(2)}, u32[]{:S(2)}) collective-permute-start(bf16[3,576,128]{2,1,0:T(8,128)(2,1)S(1)} %pick_latents.1.refs_0_), channel_id=1, source_target_pairs={{0,4},{4,0},{8,12},{12,8},{16,20},{20,16},{24,28},{28,24},{1,5},{5... | collective-permute-start | bytes 1327112 | tf_op jit(solution)/shard_map/ppermute | solution.py:441
  22.7 2.2 %collective-permute-done.2.got_ref = bf16[8,128,256]{2,1,0:T(8,128)(2,1)S(1)} collective-permute-done((bf16[8,128,256]{2,1,0:T(8,128)(2,1)}, bf16[8,128,256]{2,1,0:T(8,128)(2,1)S(1)}, u32[]{:S(2)}, u32[]{:S(2)}) %collective-permute-start.2) | collective-permute-done | bytes 524320 | tf_op jit(solution)/shard_map/ppermute | solution.py:441
  24.9 0.3 pair_join.1
  25.1 2.9 %collective-permute-start.3 = (bf16[8,128,128]{2,1,0:T(8,128)(2,1)S(1)}, bf16[8,128,128]{2,1,0:T(8,128)(2,1)S(1)}, u32[]{:S(2)}, u32[]{:S(2)}) collective-permute-start(bf16[8,128,128]{2,1,0:T(8,128)(2,1)S(1)} %get-tuple-element.33.pu_ref), channel_id=1, source_target_pairs={{0,8},{4,12},{8,0},{12,4},{16,24},{20,28},{24,16},{28,20},{1,9},{5... | collective-permute-start | bytes 786440 | tf_op jit(solution)/shard_map/ppermute | solution.py:441
  28.1 0.0 collective-permute-start.4
  28.1 0.7 %window_mask.1.bias_ref = f32[128,640]{1,0:T(8,128)S(1)} custom-call(s32[8]{0:T(128)S(1)} %copy-done.3), custom_call_target="tpu_custom_call" | custom-call | tf_op jit(solution)/shard_map/window_mask/pallas_call | solution.py:342
  28.8 4.0 %collective-permute-done.3.a_ref = bf16[8,128,128]{2,1,0:T(8,128)(2,1)S(1)} collective-permute-done((bf16[8,128,128]{2,1,0:T(8,128)(2,1)S(1)}, bf16[8,128,128]{2,1,0:T(8,128)(2,1)S(1)}, u32[]{:S(2)}, u32[]{:S(2)}) %collective-permute-start.3) | collective-permute-done | bytes 262176 | tf_op jit(solution)/shard_map/ppermute | solution.py:441
  32.8 0.0 collective-permute-done.4.b_ref
  32.8 0.2 pair_step.1
  33.0 1.8 %collective-permute-start.5 = (bf16[8,128,128]{2,1,0:T(8,128)(2,1)S(1)}, bf16[8,128,128]{2,1,0:T(8,128)(2,1)S(1)}, u32[]{:S(2)}, u32[]{:S(2)}) collective-permute-start(bf16[8,128,128]{2,1,0:T(8,128)(2,1)S(1)} %pair_step.1), channel_id=1, source_target_pairs={{0,8},{4,12},{8,0},{12,4},{16,24},{20,28},{24,16},{28,20},{1,9},{5... | collective-permute-start | bytes 786440 | tf_op jit(solution)/shard_map/ppermute | solution.py:441
  34.8 0.0 collective-permute-start.6
  34.8 0.0 collective-permute-done.9.refs_1_
  34.9 0.0 copy-done.5
  34.9 0.0 copy-done.4
  34.9 0.0 copy-done.6
  34.9 3.9 %mla_heads.2 = (bf16[640,576]{1,0:T(8,128)(2,1)S(1)}, bf16[128,2048]{1,0:T(8,128)(2,1)}) custom-call(f32[128,640]{1,0:T(8,128)S(1)} %window_mask.1.bias_ref, bf16[128,3072]{1,0:T(8,128)(2,1)S(1)} %copy-done.6, bf16[512,2048]{1,0:T(8,128)(2,1)S(1)} %copy-done.4, bf16[512,2048]{1,0:T(8,128)(2,1)S(1)} %copy-done.5, ...), custom_call_target="tpu_custom_call" | custom-call | flops 5536481280 | bytes 3072000 | tf_op jit(solution)/shard_map/mla_heads/pallas_call | solution.py:401
  38.8 0.7 %collective-permute-done.5.a_ref = bf16[8,128,128]{2,1,0:T(8,128)(2,1)S(1)} collective-permute-done((bf16[8,128,128]{2,1,0:T(8,128)(2,1)S(1)}, bf16[8,128,128]{2,1,0:T(8,128)(2,1)S(1)}, u32[]{:S(2)}, u32[]{:S(2)}) %collective-permute-start.5) | collective-permute-done | bytes 262176 | tf_op jit(solution)/shard_map/ppermute | solution.py:441
  39.5 0.0 collective-permute-done.6.b_ref
  39.5 0.4 slab_states.1
  39.9 1.6 %collective-permute-start.10 = (bf16[8,128,128]{2,1,0:T(8,128)(2,1)S(1)}, bf16[8,128,128]{2,1,0:T(8,128)(2,1)S(1)}, u32[]{:S(2)}, u32[]{:S(2)}) collective-permute-start(bf16[8,128,128]{2,1,0:T(8,128)(2,1)S(1)} %get-tuple-element.41), channel_id=1, source_target_pairs={{0,4},{4,0},{8,12},{12,8},{16,20},{20,16},{24,28},{28,24},{1,5},{5... | collective-permute-start | bytes 786440 | tf_op jit(solution)/shard_map/ppermute | solution.py:441
  41.5 0.9 %kda_out.2.rest_0_ = bf16[128,2048]{1,0:T(8,128)(2,1)} custom-call(bf16[128,1024]{1,0:T(8,128)(2,1)S(1)} %get-tuple-element.46.qe_ref, f32[128,1024]{1,0:T(8,128)S(1)} %get-tuple-element.47.lo_ref, bf16[8,128,128]{2,1,0:T(8,128)(2,1)S(1)} %get-tuple-element.48.s_ref), custom_call_target="tpu_custom_call" | custom-call | tf_op jit(solution)/shard_map/kda_out/pallas_call | solution.py:294
  42.4 0.0 copy-start
  42.4 0.0 copy-start.1
  42.4 3.6 %mla_heads.3 = bf16[128,2048]{1,0:T(8,128)(2,1)} custom-call(f32[128,640]{1,0:T(8,128)S(1)} %window_mask.1.bias_ref, bf16[128,3072]{1,0:T(8,128)(2,1)S(1)} %copy-done.6, bf16[512,2048]{1,0:T(8,128)(2,1)S(1)} %copy-done.4, bf16[512,2048]{1,0:T(8,128)(2,1)S(1)} %copy-done.5, ...), custom_call_target="tpu_custom_call", output_to_operand_aliasing={{}: (5, {})} | custom-call | flops 5536481280 | bytes 3072000 | tf_op jit(solution)/shard_map/mla_heads/pallas_call | solution.py:401
  46.0 2.2 %collective-permute-done.10.s_ref = bf16[8,128,128]{2,1,0:T(8,128)(2,1)S(1)} collective-permute-done((bf16[8,128,128]{2,1,0:T(8,128)(2,1)S(1)}, bf16[8,128,128]{2,1,0:T(8,128)(2,1)S(1)}, u32[]{:S(2)}, u32[]{:S(2)}) %collective-permute-start.10) | collective-permute-done | bytes 262176 | tf_op jit(solution)/shard_map/ppermute | solution.py:441
  48.2 0.0 copy-done
  48.2 0.0 copy-done.1
  48.2 0.9 %kda_out.3 = bf16[128,2048]{1,0:T(8,128)(2,1)} custom-call(bf16[128,1024]{1,0:T(8,128)(2,1)S(1)} %copy-done.1, f32[128,1024]{1,0:T(8,128)S(1)} %copy-done, bf16[8,128,128]{2,1,0:T(8,128)(2,1)S(1)} %collective-permute-done.10.s_ref, bf16[128,2048]{1,0:T(8,128)(2,1)} %kda_out.2.rest_0_), custom_call_target="tpu_custom_call", output_to_operand_aliasing={{}: (3, {})} | custom-call | tf_op jit(solution)/shard_map/kda_out/pallas_call | solution.py:294
  (1 shorter events, 0.0 us)
Async XLA Ops:
  0.6 6.2 %copy-start.2 = (bf16[128,576]{0,1:T(8,128)(2,1)S(1)}, bf16[128,576]{0,1:T(8,128)(2,1)}, u32[]{:S(2)}) copy-start(bf16[128,576]{0,1:T(8,128)(2,1)} %param.16) | copy-start | bytes 442372
  0.6 10.8 %copy-start.3 = (s32[8]{0:T(128)S(1)}, s32[8]{0:T(128)}, u32[]{:S(2)}) copy-start(s32[8]{0:T(128)} %lengths) | copy-start | bytes 100
  0.7 10.8 %copy-start.7 = (bf16[128,2048]{1,0:T(8,128)(2,1)S(1)}, bf16[128,2048]{1,0:T(8,128)(2,1)}, u32[]{:S(2)}) copy-start(bf16[128,2048]{1,0:T(8,128)(2,1)} %refs_0_.3) | copy-start | bytes 1572868
  0.7 10.8 %copy-start.8 = (bf16[128,2048]{1,0:T(8,128)(2,1)S(1)}, bf16[128,2048]{1,0:T(8,128)(2,1)}, u32[]{:S(2)}) copy-start(bf16[128,2048]{1,0:T(8,128)(2,1)} %refs_1_.3) | copy-start | bytes 1572868
  0.7 10.8 %copy-start.9 = (bf16[128,2048]{1,0:T(8,128)(2,1)S(1)}, bf16[128,2048]{1,0:T(8,128)(2,1)}, u32[]{:S(2)}) copy-start(bf16[128,2048]{1,0:T(8,128)(2,1)} %refs_2_.3) | copy-start | bytes 1572868
  0.7 10.7 %copy-start.10 = (bf16[128,2048]{1,0:T(8,128)(2,1)S(1)}, bf16[128,2048]{1,0:T(8,128)(2,1)}, u32[]{:S(2)}) copy-start(bf16[128,2048]{1,0:T(8,128)(2,1)} %refs_3_.3) | copy-start | bytes 1572868
  0.7 10.7 %copy-start.11 = (f32[128,16]{0,1:T(8,128)S(1)}, f32[128,16]{0,1:T(8,128)}, u32[]{:S(2)}) copy-start(f32[128,16]{0,1:T(8,128)} %param.14) | copy-start | bytes 24580
  6.8 8.8 %collective-permute-start = (bf16[576,128]{1,0:T(8,128)(2,1)S(1)}, bf16[576,128]{1,0:T(8,128)(2,1)S(1)}, u32[]{:S(2)}, u32[]{:S(2)}) collective-permute-start(bf16[576,128]{1,0:T(8,128)(2,1)S(1)} %bitcast.2), channel_id=1, source_target_pairs={{0,8},{4,12},{8,0},{12,4},{16,24},{20,28},{24,16},{28,20},{1,9},{5... | collective-permute-start | bytes 442376 | tf_op jit(solution)/shard_map/ppermute | solution.py:441
  9.9 5.7 %collective-permute-start.1 = (bf16[576,128]{1,0:T(8,128)(2,1)S(1)}, bf16[576,128]{1,0:T(8,128)(2,1)S(1)}, u32[]{:S(2)}, u32[]{:S(2)}) collective-permute-start(bf16[576,128]{1,0:T(8,128)(2,1)S(1)} %bitcast.3), channel_id=1, source_target_pairs={{0,1},{1,0},{2,3},{3,2},{4,5},{5,4},{6,7},{7,6},{8,16},{9,17},{10,... | collective-permute-start | bytes 442376 | tf_op jit(solution)/shard_map/ppermute | solution.py:446
  9.9 14.9 %collective-permute-start.2 = (bf16[8,128,256]{2,1,0:T(8,128)(2,1)}, bf16[8,128,256]{2,1,0:T(8,128)(2,1)S(1)}, u32[]{:S(2)}, u32[]{:S(2)}) collective-permute-start(bf16[8,128,256]{2,1,0:T(8,128)(2,1)} %get-tuple-element.29), channel_id=1, source_target_pairs={{0,4},{4,0},{8,12},{12,8},{16,20},{20,16},{24,28},{28,24},{1,5},{5... | collective-permute-start | bytes 1572872 | tf_op jit(solution)/shard_map/ppermute | solution.py:441
  11.4 23.4 %copy-start.5 = (bf16[512,2048]{1,0:T(8,128)(2,1)S(1)}, bf16[512,2048]{1,0:T(8,128)(2,1)}, u32[]{:S(2)}) copy-start(bf16[512,2048]{1,0:T(8,128)(2,1)} %vu_ref.3) | copy-start | bytes 6291460
  15.6 19.2 %copy-start.4 = (bf16[512,2048]{1,0:T(8,128)(2,1)S(1)}, bf16[512,2048]{1,0:T(8,128)(2,1)}, u32[]{:S(2)}) copy-start(bf16[512,2048]{1,0:T(8,128)(2,1)} %ku_ref.3) | copy-start | bytes 6291460
  15.6 19.2 %copy-start.6 = (bf16[128,3072]{1,0:T(8,128)(2,1)S(1)}, bf16[128,3072]{1,0:T(8,128)(2,1)}, u32[]{:S(2)}) copy-start(bf16[128,3072]{1,0:T(8,128)(2,1)} %q_ref.3) | copy-start | bytes 2359300
  15.7 6.3 %collective-permute-start.7 = (bf16[576,128]{1,0:T(8,128)(2,1)S(1)}, bf16[576,128]{1,0:T(8,128)(2,1)S(1)}, u32[]{:S(2)}, u32[]{:S(2)}) collective-permute-start(bf16[576,128]{1,0:T(8,128)(2,1)S(1)} %collective-permute-done.1.refs_1_), channel_id=1, source_target_pairs={{0,8},{4,12},{8,0},{12,4},{16,24},{20,28},{24,16},{28,20},{1,9},{5... | collective-permute-start | bytes 442376 | tf_op jit(solution)/shard_map/ppermute | solution.py:441
  18.9 3.1 %collective-permute-start.8 = (bf16[576,128]{1,0:T(8,128)(2,1)S(1)}, bf16[576,128]{1,0:T(8,128)(2,1)S(1)}, u32[]{:S(2)}, u32[]{:S(2)}) collective-permute-start(bf16[576,128]{1,0:T(8,128)(2,1)S(1)} %collective-permute-done.refs_0_), channel_id=1, source_target_pairs={{0,1},{1,0},{2,3},{3,2},{4,5},{5,4},{6,7},{7,6},{8,16},{9,17},{10,... | collective-permute-start | bytes 442376 | tf_op jit(solution)/shard_map/ppermute | solution.py:446
  22.1 12.8 %collective-permute-start.9 = (bf16[3,576,128]{2,1,0:T(8,128)(2,1)S(1)}, bf16[3,576,128]{2,1,0:T(8,128)(2,1)S(1)}, u32[]{:S(2)}, u32[]{:S(2)}) collective-permute-start(bf16[3,576,128]{2,1,0:T(8,128)(2,1)S(1)} %pick_latents.1.refs_0_), channel_id=1, source_target_pairs={{0,4},{4,0},{8,12},{12,8},{16,20},{20,16},{24,28},{28,24},{1,5},{5... | collective-permute-start | bytes 1327112 | tf_op jit(solution)/shard_map/ppermute | solution.py:441
  25.1 7.6 %collective-permute-start.3 = (bf16[8,128,128]{2,1,0:T(8,128)(2,1)S(1)}, bf16[8,128,128]{2,1,0:T(8,128)(2,1)S(1)}, u32[]{:S(2)}, u32[]{:S(2)}) collective-permute-start(bf16[8,128,128]{2,1,0:T(8,128)(2,1)S(1)} %get-tuple-element.33.pu_ref), channel_id=1, source_target_pairs={{0,8},{4,12},{8,0},{12,4},{16,24},{20,28},{24,16},{28,20},{1,9},{5... | collective-permute-start | bytes 786440 | tf_op jit(solution)/shard_map/ppermute | solution.py:441
  28.1 4.7 %collective-permute-start.4 = (bf16[8,128,128]{2,1,0:T(8,128)(2,1)S(1)}, bf16[8,128,128]{2,1,0:T(8,128)(2,1)S(1)}, u32[]{:S(2)}, u32[]{:S(2)}) collective-permute-start(bf16[8,128,128]{2,1,0:T(8,128)(2,1)S(1)} %get-tuple-element.33.pu_ref), channel_id=1, source_target_pairs={{0,1},{1,0},{2,3},{3,2},{4,5},{5,4},{6,7},{7,6},{8,16},{9,17},{10,... | collective-permute-start | bytes 786440 | tf_op jit(solution)/shard_map/ppermute | solution.py:446
  33.0 6.4 %collective-permute-start.5 = (bf16[8,128,128]{2,1,0:T(8,128)(2,1)S(1)}, bf16[8,128,128]{2,1,0:T(8,128)(2,1)S(1)}, u32[]{:S(2)}, u32[]{:S(2)}) collective-permute-start(bf16[8,128,128]{2,1,0:T(8,128)(2,1)S(1)} %pair_step.1), channel_id=1, source_target_pairs={{0,8},{4,12},{8,0},{12,4},{16,24},{20,28},{24,16},{28,20},{1,9},{5... | collective-permute-start | bytes 786440 | tf_op jit(solution)/shard_map/ppermute | solution.py:441
  34.8 4.6 %collective-permute-start.6 = (bf16[8,128,128]{2,1,0:T(8,128)(2,1)S(1)}, bf16[8,128,128]{2,1,0:T(8,128)(2,1)S(1)}, u32[]{:S(2)}, u32[]{:S(2)}) collective-permute-start(bf16[8,128,128]{2,1,0:T(8,128)(2,1)S(1)} %pair_step.1), channel_id=1, source_target_pairs={{0,1},{1,0},{2,3},{3,2},{4,5},{5,4},{6,7},{7,6},{8,16},{9,17},{10,... | collective-permute-start | bytes 786440 | tf_op jit(solution)/shard_map/ppermute | solution.py:446
  39.9 8.3 %collective-permute-start.10 = (bf16[8,128,128]{2,1,0:T(8,128)(2,1)S(1)}, bf16[8,128,128]{2,1,0:T(8,128)(2,1)S(1)}, u32[]{:S(2)}, u32[]{:S(2)}) collective-permute-start(bf16[8,128,128]{2,1,0:T(8,128)(2,1)S(1)} %get-tuple-element.41), channel_id=1, source_target_pairs={{0,4},{4,0},{8,12},{12,8},{16,20},{20,16},{24,28},{28,24},{1,5},{5... | collective-permute-start | bytes 786440 | tf_op jit(solution)/shard_map/ppermute | solution.py:441
  42.4 5.9 %copy-start = (f32[128,1024]{1,0:T(8,128)S(1)}, f32[128,1024]{1,0:T(8,128)}, u32[]{:S(2)}) copy-start(f32[128,1024]{1,0:T(8,128)} %get-tuple-element.27.lo_ref) | copy-start | bytes 1572868
  42.4 5.9 %copy-start.1 = (bf16[128,1024]{1,0:T(8,128)(2,1)S(1)}, bf16[128,1024]{1,0:T(8,128)(2,1)}, u32[]{:S(2)}) copy-start(bf16[128,1024]{1,0:T(8,128)(2,1)} %get-tuple-element.26.qe_ref) | copy-start | bytes 786436

commit v4 on v3

--- a/solution.py
+++ b/solution.py
@@ -17,6 +17,7 @@
 WHOLE = pl.BlockSpec(memory_space=pltpu.VMEM)
 SCALARS = pl.BlockSpec(memory_space=pltpu.SMEM)
 FAR = pl.BlockSpec(memory_space=pltpu.HBM)
+CHEAP = pl.CostEstimate(flops=0, bytes_accessed=0, transcendentals=0)
 BF = jnp.bfloat16
 F32 = jnp.float32
 NEG = -1e30
@@ -43,37 +44,29 @@
     return total
 
 
-def kda_kernel(ndocs, flip, *refs):
-    sources, small = refs[:4], refs[4:6]
-    mu_ref, qe_ref, lo_ref = refs[6:9]
-    blocks, (b_ref, sc, sems, small_sems) = refs[9:13], refs[13:]
+def kda_kernel(ndocs, flip, states, outputs, *refs):
+    names = [name for name in "gkqv" if name != "q" or outputs]
+    sources, small = refs[: len(names)], refs[len(names) : len(names) + 2]
+    refs = refs[len(names) + 2 :]
+    if states:
+        mu_ref, refs = refs[0], refs[1:]
+    if outputs:
+        qe_ref, lo_ref, refs = refs[0], refs[1], refs[2:]
+    blocks, (b_ref, sc, sems, small_sems) = refs[: len(names)], refs[len(names) :]
+    block = dict(zip(names, blocks))
     rows, width = blocks[0].shape
     place = lax.axis_index("ctx")
     side = (place + flip) % 2
     start = pl.multiple_of(side * width, width)
-    parts = sems.shape[1]
-    part = width // parts
-    small_copies = [
-        pltpu.make_async_copy(source, block, small_sems.at[j])
-        for j, (source, block) in enumerate(zip(small, (sc, b_ref)))
+    copies = [
+        pltpu.make_async_copy(source.at[:, pl.ds(start, width)], to, sems.at[j])
+        for j, (source, to) in enumerate(zip(sources, blocks))
+    ] + [
+        pltpu.make_async_copy(source, to, small_sems.at[j])
+        for j, (source, to) in enumerate(zip(small, (sc, b_ref)))
     ]
-    copies = [
-        [
-            pltpu.make_async_copy(
-                source.at[:, pl.ds(start + i * part, part)],
-                block.at[:, pl.ds(i * part, part)],
-                sems.at[j, i],
-            )
-            for j, (source, block) in enumerate(zip(sources, blocks))
-        ]
-        for i in range(parts)
-    ]
-    for copy in small_copies:
+    for copy in copies:
         copy.start()
-    for group in copies:
-        for copy in group:
-            copy.start()
-    q_ref, k_ref, v_ref, g_ref = blocks
     half = rows // 2
     heads = width // 128
     base = side * heads
@@ -83,42 +76,52 @@
     tri = (ri >= ci).astype(BF)
     low = ci < half
     eye = (ri == ci).astype(F32)
+    zeros = jnp.zeros((half, 128), BF)
+    for copy in copies[: len(names) - 1]:
+        copy.wait()
+    cum_all = mm(tri, block["g"][...])
+
+    def halves(top, bottom):
+        return jnp.concatenate(
+            [jnp.broadcast_to(top, (half, 128)), jnp.broadcast_to(bottom, (half, 128))], axis=0
+        )
 
     hs = range(heads)
     kept, lhs, km, lhs_off, km_off = [], [], [], [], []
     for h in hs:
         cols = slice(h * 128, (h + 1) * 128)
-        if h % (heads // parts) == 0:
-            i = h // (heads // parts)
-            for copy in copies[i]:
-                copy.wait()
-            cum_part = mm(tri, g_ref[:, i * part : (i + 1) * part])
-        q = q_ref[:, cols].astype(F32)
-        k = k_ref[:, cols].astype(F32)
-        qn = q * lax.rsqrt(jnp.sum(q * q, axis=1, keepdims=True) + 1e-06)
+        k = block["k"][:, cols].astype(F32)
         kn = k * lax.rsqrt(jnp.sum(k * k, axis=1, keepdims=True) + 1e-06)
-        cum = cum_part[:, h * 128 - i * part : (h + 1) * 128 - i * part]
+        cum = cum_all[:, cols]
         quarter = half // 2
         m0 = cum[quarter - 1 : quarter]
         m1 = cum[half + quarter - 1 : half + quarter]
         mid = cum[half - 1 : half]
         end = cum[rows - 1 : rows]
-        c0, c1 = cum[:half], cum[half:]
-        dp = jnp.concatenate([jnp.exp(c0 - m0), jnp.exp(c1 - m1)], axis=0)
-        dm = jnp.concatenate([jnp.exp(m0 - c0), jnp.exp(m1 - c1)], axis=0)
-        op = jnp.exp(c1 - mid)
-        om = jnp.exp(jnp.minimum(mid - cum, 0.0))
-        growth = jnp.exp(cum)
-        trail = jnp.exp(end - cum)
-        lhs.append(jnp.concatenate([(kn * dp).astype(BF), (qn * dp).astype(BF)], axis=0))
-        km.append((kn * dm).astype(BF))
-        lhs_off.append(
-            jnp.concatenate([(kn[half:] * op).astype(BF), (qn[half:] * op).astype(BF)], axis=0)
+        about = cum - halves(m0, m1)
+        dp = jnp.exp(about)
+        kd = kn * dp
+        ku = kn * jnp.exp(-about)
+        late = jnp.exp(m1 - mid)
+        grow = halves(jnp.exp(m0 * 0.5), jnp.exp(m1 * 0.5))
+        wane = halves(jnp.exp((end - m0) * 0.5), jnp.exp((end - m1) * 0.5))
+        left, left_off = [kd.astype(BF)], [(kd[half:] * late).astype(BF)]
+        queried = None
+        if outputs:
+            q = block["q"][:, cols].astype(F32)
+            qd = q * lax.rsqrt(jnp.sum(q * q, axis=1, keepdims=True) + 1e-06) * dp
+            left.append(qd.astype(BF))
+            left_off.append((qd[half:] * late).astype(BF))
+            queried = qd * grow * grow
+        lhs.append(jnp.concatenate(left, axis=0))
+        lhs_off.append(jnp.concatenate(left_off, axis=0))
+        km.append(ku.astype(BF))
+        km_off.append(
+            jnp.concatenate([(ku[:half] * jnp.exp(mid - m0)).astype(BF), zeros], axis=0)
         )
-        km_off.append((kn * om).astype(BF))
-        kept.append((kn * growth, kn * trail, qn * growth, jnp.exp(end)))
-
-    for copy in small_copies:
+        kept.append((kd * grow * grow, ku * wane * wane, queried, jnp.exp(end)))
+
+    for copy in copies[len(names) - 1 :]:
         copy.wait()
     doc_r = doc_of(first + ri, sc, ndocs)
     doc_c = doc_of(first + ci, sc, ndocs)
@@ -130,74 +133,83 @@
     follow = (doc_r == prev).astype(F32)
     tail = (doc_r == last).astype(F32)
     keep = (last == prev).astype(F32)
-    rhs, kt, qg, gl, gain = [], [], [], [], []
-    for h in hs:
-        grown, trailed, queried, ended = kept[h]
-        b = jnp.sum(eye * b_ref[pl.ds(base + h, 1), :], axis=1, keepdims=True)
-        v = v_ref[:, h * 128 : (h + 1) * 128].astype(F32)
-        rhs.append(
-            jnp.concatenate([(grown * (b * follow)).astype(BF), (v * b).astype(BF)], axis=1)
-        )
-        kt.append((trailed * tail).astype(BF))
-        qg.append(queried * follow)
-        gl.append(ended * keep)
-        gain.append(b)
-
-    a, mix = [], []
+    a, mix, rhs = [], [], []
     for h in hs:
         p = mm_nt(lhs[h], km[h])
         o = mm_nt(lhs_off[h], km_off[h])
-        pa, pq = p[:rows], p[rows:]
-        pa = jnp.concatenate([pa[:half], jnp.where(low[half:], o[:half], pa[half:])], axis=0)
-        pq = jnp.concatenate([pq[:half], jnp.where(low[half:], o[half:], pq[half:])], axis=0)
-        a.append(jnp.where(strict, pa, 0.0) * gain[h])
-        mix.append(jnp.where(causal, pq, 0.0).astype(BF))
-
-    t = [eye - jnp.where((ri >> 1) == (ci >> 1), a[h], 0.0) for h in hs]
-    shift = 1
-    while (2 << shift) <= rows:
-        level = ((ri >> (shift + 1)) == (ci >> (shift + 1))) & ((ri >> shift) != (ci >> shift))
-        tb = [t[h].astype(BF) for h in hs]
-        x = [mm(jnp.where(level, a[h], 0.0).astype(BF), tb[h]).astype(BF) for h in hs]
-        t = [t[h] - mm(tb[h], x[h]) for h in hs]
-        shift += 1
-
-    wu = [mm(t[h].astype(BF), rhs[h]).astype(BF) for h in hs]
+        b = jnp.sum(eye * b_ref[pl.ds(base + h, 1), :], axis=1, keepdims=True)
+        pa = jnp.concatenate([p[:half], jnp.where(low[half:], o[:half], p[half:rows])], axis=0)
+        a.append(jnp.where(strict, pa * b, 0.0))
+        if outputs:
+            pq = p[rows:]
+            pq = jnp.concatenate([pq[:half], jnp.where(low[half:], o[half:], pq[half:])], axis=0)
+            mix.append(jnp.where(causal, pq, 0.0).astype(BF))
+        v = block["v"][:, h * 128 : (h + 1) * 128].astype(F32)
+        rhs.append(
+            jnp.concatenate([(kept[h][0] * (b * follow)).astype(BF), (v * b).astype(BF)], axis=1)
+        )
+
+    t = [(eye - jnp.where((ri >> 1) == (ci >> 1), a[h], 0.0)).astype(BF) for h in hs]
+    a = [a[h].astype(BF) for h in hs]
+    bits, low_bit = rows.bit_length() - 1, 1
+    while low_bit < bits:
+        up_bit = min(low_bit + 3, bits)
+        rest = ((ri >> up_bit) == (ci >> up_bit)) & ((ri >> low_bit) != (ci >> low_bit))
+        rest = rest.astype(BF)
+        w = [mm(a[h] * rest, t[h]).astype(BF) for h in hs]
+        left = t
+        for step in range(up_bit - low_bit):
+            if step + 1 < up_bit - low_bit:
+                z = [mm(jnp.concatenate([left[h], w[h]], axis=0), w[h]) for h in hs]
+                w = [z[h][rows:].astype(BF) for h in hs]
+                z = [z[h][:rows] for h in hs]
+            else:
+                z = [mm(left[h], w[h]) for h in hs]
+            t = [t[h] - z[h] if step == 0 else t[h] + z[h] for h in hs]
+            left = [t[h].astype(BF) for h in hs]
+        t = left
+        low_bit = up_bit
+
+    wu = [mm(t[h], rhs[h]).astype(BF) for h in hs]
     for h in hs:
         cols = slice(h * 128, (h + 1) * 128)
-        z = mm_tn(kt[h], wu[h])
-        mu_ref[h, :, :128] = (eye * gl[h] - z[:, :128]).astype(BF)
-        mu_ref[h, :, 128:] = z[:, 128:].astype(BF)
-        y = mm(mix[h], wu[h])
-        qe_ref[:, cols] = (qg[h] - y[:, :128]).astype(BF)
-        lo_ref[:, cols] = y[:, 128:]
-
-
-def kda_half(flip, lengths, q, k, v, g, b):
+        if states:
+            z = mm_tn((kept[h][1] * tail).astype(BF), wu[h])
+            mu_ref[h, :, :128] = (eye * (kept[h][3] * keep) - z[:, :128]).astype(BF)
+            mu_ref[h, :, 128:] = z[:, 128:].astype(BF)
+        if outputs:
+            y = mm(mix[h], wu[h])
+            qe_ref[:, cols] = (kept[h][2] * follow - y[:, :128]).astype(BF)
+            lo_ref[:, cols] = y[:, 128:]
+
+
+def kda_half(flip, lengths, q, k, v, g, b, states=True, outputs=True, limit=VMEM):
     rows, width = q.shape[0], q.shape[1] // 2
     heads, ndocs = b.shape[0], lengths.shape[0]
-    return pl.pallas_call(
-        functools.partial(kda_kernel, ndocs, flip),
-        in_specs=[FAR] * 6,
-        out_specs=[WHOLE, WHOLE, WHOLE],
-        out_shape=[
-            jax.ShapeDtypeStruct((heads // 2, 128, 256), BF),
+    args = [g, k] + ([q] if outputs else []) + [v, lengths, b]
+    wide = len(args) - 2
+    shapes = [jax.ShapeDtypeStruct((heads // 2, 128, 256), BF)] if states else []
+    if outputs:
+        shapes += [
             jax.ShapeDtypeStruct((rows, width), BF),
             jax.ShapeDtypeStruct((rows, width), F32),
-        ],
-        scratch_shapes=[pltpu.VMEM((rows, width), BF)] * 4
+        ]
+    return pl.pallas_call(
+        functools.partial(kda_kernel, ndocs, flip, states, outputs),
+        in_specs=[FAR] * len(args),
+        out_specs=[WHOLE] * len(shapes),
+        out_shape=shapes,
+        scratch_shapes=[pltpu.VMEM((rows, width), BF)] * wide
         + [
             pltpu.VMEM(b.shape, F32),
             pltpu.SMEM(lengths.shape, jnp.int32),
-            pltpu.SemaphoreType.DMA((4, 4)),
+            pltpu.SemaphoreType.DMA((wide,)),
             pltpu.SemaphoreType.DMA((2,)),
         ],
-        compiler_params=pltpu.CompilerParams(vmem_limit_bytes=ALL_VMEM if flip else VMEM),
-        cost_estimate=pl.CostEstimate(
-            flops=heads * 2 * 128**3 * 100, bytes_accessed=width * rows * 16, transcendentals=0
-        ),
+        compiler_params=pltpu.CompilerParams(vmem_limit_bytes=limit),
+        cost_estimate=CHEAP,
         name="kda_slab",
-    )(q, k, v, g, lengths, b)
+    )(*args)
 
 
 def pair_kernel(own_ref, got_ref, pm_ref, pu_ref):
@@ -254,6 +266,7 @@
         in_specs=[WHOLE] * len(args),
         out_specs=[WHOLE] * len(outs),
         out_shape=[jax.ShapeDtypeStruct(o, BF) for o in outs],
+        cost_estimate=CHEAP,
         compiler_params=pltpu.CompilerParams(vmem_limit_bytes=VMEM // 2),
         name=name,
     )(*args)
@@ -298,6 +311,7 @@
         out_shape=jax.ShapeDtypeStruct((rows, heads * 128), BF),
         scratch_shapes=[pltpu.VMEM((rows, width), BF), pltpu.SemaphoreType.DMA((2,))],
         input_output_aliases=aliases,
+        cost_estimate=CHEAP,
         compiler_params=pltpu.CompilerParams(vmem_limit_bytes=VMEM // 2),
         name="kda_out",
     )(*args)
@@ -310,22 +324,32 @@
         def _():
             for w in range(reach + 1):
                 back = reach // 2 - (w + column) // 2
-                block = (mate_ref if (w + column) % 2 != column else own_ref)[back]
+                if (w + column) % 2 == column:
+                    block = own_ref[back]
+                else:
+                    block = mate_ref[back - 1 + column]
                 at = slice(w * rows, (w + 1) * rows)
                 out_ref[at, :LATENT] = block[:LATENT].T
                 out_ref[at, LATENT:] = block[LATENT:].T
 
 
 def pick_kernel(own_ref, *refs):
-    out_ref = refs[-1]
+    out_ref, send_ref = refs[-2:]
+    place = lax.axis_index("ctx")
+    rounds = send_ref.shape[0]
     out_ref[0] = own_ref[...]
-    parity = (lax.axis_index("ctx") // 2) % 2
-    for back in range(out_ref.shape[0] - 1):
+    for back in range(rounds):
         for kind in range(2):
 
-            @pl.when(parity == 1 - kind)
+            @pl.when((place // 2) % 2 == 1 - kind)
             def _():
                 out_ref[back + 1] = refs[2 * back + kind][...]
+
+    for column in range(2):
+
+        @pl.when(place % 2 == column)
+        def _():
+            send_ref[...] = out_ref[column : column + rounds]
 
 
 def mask_kernel(ndocs, lengths, bias_ref):
@@ -344,6 +368,7 @@
         in_specs=[SCALARS],
         out_specs=WHOLE,
         out_shape=jax.ShapeDtypeStruct((rows, keys), F32),
+        cost_estimate=CHEAP,
         compiler_params=pltpu.CompilerParams(vmem_limit_bytes=VMEM // 2),
         name="window_mask",
     )(lengths)
@@ -416,11 +441,7 @@
         ],
         input_output_aliases=aliases,
         compiler_params=pltpu.CompilerParams(vmem_limit_bytes=VMEM),
-        cost_estimate=pl.CostEstimate(
-            flops=6 * keys * count * 128 * (2 * LATENT + 3 * rows),
-            bytes_accessed=count * 128 * 3000,
-            transcendentals=0,
-        ),
+        cost_estimate=CHEAP,
         name="mla_heads",
     )(*args)
 
@@ -467,25 +488,31 @@
 
     lat = latents.T
     shape = (heads // 2, 128, 128)
-    mu_away, qe_away, lo_away = kda_half(1, *kda_args)
+    def after(x, *others):
+        return lax.optimization_barrier((x, others))[0]
+
+    (mu_away,) = kda_half(1, *kda_args, outputs=False, limit=ALL_VMEM)
     mu_got = swap(mu_away, mate)
-    mu_own, qe_own, lo_own = kda_half(0, *kda_args)
-    early, _ = lax.optimization_barrier((lat, mu_away))
+    args = after(kda_args, mu_away)
+    early = after(lat, mu_away)
     moved = [(swap(early, up), swap(early, middle))]
-    mu_own, *moved[0] = lax.optimization_barrier((mu_own, *moved[0]))
+    mu_own, qe_own, lo_own = kda_half(0, *args)
+    moved[0] = after(moved[0], mu_own)
+    args = after(args, mu_own, moved[0])
+    qe_away, lo_away = kda_half(1, *args, states=False)
     for _ in range(rounds - 1):
         a, b = moved[-1]
         moved.append((swap(b, up), swap(a, middle)))
-    (lat_own,) = whole_call(
+    bias = mask(after(doc_lengths, qe_away), latents.shape[0], (reach + 1) * latents.shape[0])
+    lat_own, lat_send = whole_call(
         pick_kernel,
         "pick_latents",
-        [lat, *[x for ab in moved for x in ab]],
-        [(rounds + 1, *lat.shape)],
+        [after(lat, qe_away), *[x for ab in moved for x in ab]],
+        [(rounds + 1, *lat.shape), (rounds, *lat.shape)],
     )
-    lat_mate = swap(lat_own, mate)
+    lat_mate = swap(lat_send, mate)
+    mu_got = after(mu_got, bias, lat_own)
     pm, pu = whole_call(pair_kernel, "pair_join", [mu_own, mu_got], [shape, shape])
-    later, _ = lax.optimization_barrier((doc_lengths, mu_own))
-    bias = mask(later, latents.shape[0], (reach + 1) * latents.shape[0])
 
     def attend(latent_blocks, previous, first, count):
         return mla(

time: 49.5 us -> 45.6 us (0.921)
  waiting for transfers between devices: 12.2 us -> 10 us
  starting transfers between devices: 14.7 us -> 13.3 us
    ppermute x7, waiting for transfers between devices: 12.2 us -> 10 us  [swap(): return lax.ppermute(x, 'ctx', list(enumerate(table)))]
    ppermute x7, starting transfers between devices: 14.7 us -> 13.3 us  [swap(): return lax.ppermute(x, 'ctx', list(enumerate(table)))]
    pallas_call x2 -> x3, Pallas kernels: 10.3 us -> 10 us  [kda_half(): pl.pallas_call(functools.partial(kda_kernel, ndocs, flip, states, outputs...]
  transfers between devices with their start and end apart: 11 -> 11, of which waited for: 5 -> 6; matrix products, arithmetic and copies ran while one was open for 0% -> 0% of each run, Pallas kernels for 28% -> 33%
where the time goes in v4:
time: 45.6 us; the launch traced here: 45.4 us
  Pallas kernels  21 us (46%)
  starting transfers between devices  13.3 us (29%)
  waiting for transfers between devices  10 us (22%)
  between operations  1.02 us (2%)
    ppermute x7, starting transfers between devices, swap(): return lax.ppermute(x, 'ctx', list(enumerate(table)))  13.3 us
    pallas_call x3, Pallas kernels, kda_half(): pl.pallas_call(functools.partial(kda_kernel, ndocs, flip, states, outputs...  10 us
    ppermute x7, waiting for transfers between devices, swap(): return lax.ppermute(x, 'ctx', list(enumerate(table)))  10 us
    pallas_call x2, Pallas kernels, mla(): pl.pallas_call(functools.partial(mla_kernel, reach, previous is None, fir...  7.65 us
    pallas_call x2, Pallas kernels, final(): pl.pallas_call(functools.partial(final_kernel, flip), in_specs=specs, out...  1.8 us
  transfers between devices with their start and end apart: 11, of which 6 were waited for; matrix products, arithmetic and copies ran while one was open for 0% of the time, Pallas kernels for 33%

profile of v4, /device:TPU:0, one launch (start us, length us, event | category | flops | bytes accessed | tf_op | source)
XLA Modules:
  0.0 45.4 jit_solution(5320169603854719512)
XLA Ops:
  0.6 0.0 copy-start.8
  0.6 0.0 copy-start.3
  0.7 0.0 copy-start.4
  0.7 0.0 copy-start.2
  0.7 0.0 copy-start.9
  0.7 0.0 copy-start.6
  0.7 4.5 %kda_slab.3 = bf16[8,128,256]{2,1,0:T(8,128)(2,1)} custom-call(bf16[128,2048]{1,0:T(8,128)(2,1)} %refs_0_.3, bf16[128,2048]{1,0:T(8,128)(2,1)} %refs_1_.3, bf16[128,2048]{1,0:T(8,128)(2,1)} %refs_3_.3, s32[8]{0:T(128)} %lengths, f32[16,128]{1,0:T(8,128)} %bitcast.5), custom_call_target="tpu_custom_call" | custom-call | tf_op jit(solution)/shard_map/kda_slab/pallas_call | solution.py:197
  5.2 3.0 %collective-permute-start.2 = (bf16[8,128,256]{2,1,0:T(8,128)(2,1)}, bf16[8,128,256]{2,1,0:T(8,128)(2,1)S(1)}, u32[]{:S(2)}, u32[]{:S(2)}) collective-permute-start(bf16[8,128,256]{2,1,0:T(8,128)(2,1)} %kda_slab.3), channel_id=1, source_target_pairs={{0,4},{4,0},{8,12},{12,8},{16,20},{20,16},{24,28},{28,24},{1,5},{5... | collective-permute-start | bytes 1572872 | tf_op jit(solution)/shard_map/ppermute | solution.py:462
  8.2 0.0 copy-start.7
  8.2 1.6 %collective-permute-start = (bf16[576,128]{1,0:T(8,128)(2,1)}, bf16[576,128]{1,0:T(8,128)(2,1)S(1)}, u32[]{:S(2)}, u32[]{:S(2)}) collective-permute-start(bf16[576,128]{1,0:T(8,128)(2,1)} %bitcast.2), channel_id=1, source_target_pairs={{0,8},{4,12},{8,0},{12,4},{16,24},{20,28},{24,16},{28,20},{1,9},{5... | collective-permute-start | bytes 442376 | tf_op jit(solution)/shard_map/ppermute | solution.py:462
  9.8 0.0 collective-permute-start.1
  9.8 0.0 copy-done.8
  9.8 0.0 copy-done.3
  9.8 0.0 copy-done.4
  9.8 0.0 copy-done.2
  9.8 0.0 copy-done.9
  9.8 0.0 copy-done.6
  9.8 2.9 %kda_slab.4 = (bf16[8,128,256]{2,1,0:T(8,128)(2,1)S(1)}, bf16[128,1024]{1,0:T(8,128)(2,1)S(1)}, f32[128,1024]{1,0:T(8,128)S(1)}) custom-call(bf16[128,2048]{1,0:T(8,128)(2,1)S(1)} %copy-done.2, bf16[128,2048]{1,0:T(8,128)(2,1)S(1)} %copy-done.3, bf16[128,2048]{1,0:T(8,128)(2,1)S(1)} %copy-done.6, bf16[128,2048]{1,0:T(8,128)(2,1)S(1)} %copy-done.4, ...), custom_call_target="tpu_custom_call" | custom-call | tf_op jit(solution)/shard_map/kda_slab/pallas_call | solution.py:197
  12.7 1.0 %collective-permute-done.refs_0_ = bf16[576,128]{1,0:T(8,128)(2,1)S(1)} collective-permute-done((bf16[576,128]{1,0:T(8,128)(2,1)}, bf16[576,128]{1,0:T(8,128)(2,1)S(1)}, u32[]{:S(2)}, u32[]{:S(2)}) %collective-permute-start) | collective-permute-done | bytes 147488 | tf_op jit(solution)/shard_map/ppermute | solution.py:462
  13.7 0.0 collective-permute-done.1.refs_1_
  13.7 2.7 %collective-permute-start.3 = (bf16[576,128]{1,0:T(8,128)(2,1)S(1)}, bf16[576,128]{1,0:T(8,128)(2,1)S(1)}, u32[]{:S(2)}, u32[]{:S(2)}) collective-permute-start(bf16[576,128]{1,0:T(8,128)(2,1)S(1)} %collective-permute-done.1.refs_1_), channel_id=1, source_target_pairs={{0,8},{4,12},{8,0},{12,4},{16,24},{20,28},{24,16},{28,20},{1,9},{5... | collective-permute-start | bytes 442376 | tf_op jit(solution)/shard_map/ppermute | solution.py:462
  16.5 0.0 collective-permute-start.4
  16.5 0.0 copy-start.1
  16.5 2.7 %kda_slab.5 = (bf16[128,1024]{1,0:T(8,128)(2,1)S(1)}, f32[128,1024]{1,0:T(8,128)S(1)}) custom-call(bf16[128,2048]{1,0:T(8,128)(2,1)S(1)} %copy-done.2, bf16[128,2048]{1,0:T(8,128)(2,1)S(1)} %copy-done.3, bf16[128,2048]{1,0:T(8,128)(2,1)S(1)} %copy-done.6, bf16[128,2048]{1,0:T(8,128)(2,1)S(1)} %copy-done.4, s32[8]{0:T(128)S(1)} %copy-done.9, ...), custom_call_target="tpu_custom_call" | custom-call | tf_op jit(solution)/shard_map/kda_slab/pallas_call | solution.py:197
  19.1 0.0 copy-start
  19.1 0.0 copy-start.5
  19.2 0.7 %window_mask.1.bias_ref = f32[128,640]{1,0:T(8,128)S(1)} custom-call(s32[8]{0:T(128)S(1)} %copy-done.9), custom_call_target="tpu_custom_call" | custom-call | tf_op jit(solution)/shard_map/window_mask/pallas_call | solution.py:366
  19.8 0.0 collective-permute-done.3.refs_2_
  19.8 0.0 collective-permute-done.4.refs_3_
  19.9 0.0 copy-done.7
  19.9 0.1 pick_latents.1
  20.0 0.4 collective-permute-done.2.got_ref
  20.3 0.3 pair_join.1
  20.6 1.9 %collective-permute-start.5 = (bf16[8,128,128]{2,1,0:T(8,128)(2,1)S(1)}, bf16[8,128,128]{2,1,0:T(8,128)(2,1)S(1)}, u32[]{:S(2)}, u32[]{:S(2)}) collective-permute-start(bf16[8,128,128]{2,1,0:T(8,128)(2,1)S(1)} %get-tuple-element.63.pu_ref), channel_id=1, source_target_pairs={{0,8},{4,12},{8,0},{12,4},{16,24},{20,28},{24,16},{28,20},{1,9},{5... | collective-permute-start | bytes 786440 | tf_op jit(solution)/shard_map/ppermute | solution.py:462
  22.5 0.0 collective-permute-start.6
  22.5 1.5 %collective-permute-start.9 = (bf16[2,576,128]{2,1,0:T(8,128)(2,1)S(1)}, bf16[2,576,128]{2,1,0:T(8,128)(2,1)S(1)}, u32[]{:S(2)}, u32[]{:S(2)}) collective-permute-start(bf16[2,576,128]{2,1,0:T(8,128)(2,1)S(1)} %get-tuple-element.65), channel_id=1, source_target_pairs={{0,4},{4,0},{8,12},{12,8},{16,20},{20,16},{24,28},{28,24},{1,5},{5... | collective-permute-start | bytes 884744 | tf_op jit(solution)/shard_map/ppermute | solution.py:462
  24.0 5.0 %collective-permute-done.5.a_ref = bf16[8,128,128]{2,1,0:T(8,128)(2,1)S(1)} collective-permute-done((bf16[8,128,128]{2,1,0:T(8,128)(2,1)S(1)}, bf16[8,128,128]{2,1,0:T(8,128)(2,1)S(1)}, u32[]{:S(2)}, u32[]{:S(2)}) %collective-permute-start.5) | collective-permute-done | bytes 262176 | tf_op jit(solution)/shard_map/ppermute | solution.py:462
  29.1 0.0 collective-permute-done.6.b_ref
  29.1 0.2 pair_step.1
  29.3 1.9 %collective-permute-start.7 = (bf16[8,128,128]{2,1,0:T(8,128)(2,1)S(1)}, bf16[8,128,128]{2,1,0:T(8,128)(2,1)S(1)}, u32[]{:S(2)}, u32[]{:S(2)}) collective-permute-start(bf16[8,128,128]{2,1,0:T(8,128)(2,1)S(1)} %pair_step.1), channel_id=1, source_target_pairs={{0,8},{4,12},{8,0},{12,4},{16,24},{20,28},{24,16},{28,20},{1,9},{5... | collective-permute-start | bytes 786440 | tf_op jit(solution)/shard_map/ppermute | solution.py:462
  31.2 0.0 collective-permute-start.8
  31.2 0.8 %collective-permute-done.9.refs_1_ = bf16[2,576,128]{2,1,0:T(8,128)(2,1)S(1)} collective-permute-done((bf16[2,576,128]{2,1,0:T(8,128)(2,1)S(1)}, bf16[2,576,128]{2,1,0:T(8,128)(2,1)S(1)}, u32[]{:S(2)}, u32[]{:S(2)}) %collective-permute-start.9) | collective-permute-done | bytes 294944 | tf_op jit(solution)/shard_map/ppermute | solution.py:462
  32.0 0.0 copy-done.1
  32.0 0.0 copy-done
  32.0 0.0 copy-done.5
  32.0 4.1 %mla_heads.2 = (bf16[640,576]{1,0:T(8,128)(2,1)S(1)}, bf16[128,2048]{1,0:T(8,128)(2,1)}) custom-call(f32[128,640]{1,0:T(8,128)S(1)} %window_mask.1.bias_ref, bf16[128,3072]{1,0:T(8,128)(2,1)S(1)} %copy-done.5, bf16[512,2048]{1,0:T(8,128)(2,1)S(1)} %copy-done, bf16[512,2048]{1,0:T(8,128)(2,1)S(1)} %copy-done.1, ...), custom_call_target="tpu_custom_call" | custom-call | tf_op jit(solution)/shard_map/mla_heads/pallas_call | solution.py:426
  36.0 0.8 %collective-permute-done.7.a_ref = bf16[8,128,128]{2,1,0:T(8,128)(2,1)S(1)} collective-permute-done((bf16[8,128,128]{2,1,0:T(8,128)(2,1)S(1)}, bf16[8,128,128]{2,1,0:T(8,128)(2,1)S(1)}, u32[]{:S(2)}, u32[]{:S(2)}) %collective-permute-start.7) | collective-permute-done | bytes 262176 | tf_op jit(solution)/shard_map/ppermute | solution.py:462
  36.9 0.0 collective-permute-done.8.b_ref
  36.9 0.3 slab_states.1
  37.1 0.7 %collective-permute-start.10 = (bf16[8,128,128]{2,1,0:T(8,128)(2,1)S(1)}, bf16[8,128,128]{2,1,0:T(8,128)(2,1)S(1)}, u32[]{:S(2)}, u32[]{:S(2)}) collective-permute-start(bf16[8,128,128]{2,1,0:T(8,128)(2,1)S(1)} %get-tuple-element.69), channel_id=1, source_target_pairs={{0,4},{4,0},{8,12},{12,8},{16,20},{20,16},{24,28},{28,24},{1,5},{5... | collective-permute-start | bytes 786440 | tf_op jit(solution)/shard_map/ppermute | solution.py:462
  37.9 3.6 %mla_heads.3 = bf16[128,2048]{1,0:T(8,128)(2,1)} custom-call(f32[128,640]{1,0:T(8,128)S(1)} %window_mask.1.bias_ref, bf16[128,3072]{1,0:T(8,128)(2,1)S(1)} %copy-done.5, bf16[512,2048]{1,0:T(8,128)(2,1)S(1)} %copy-done, bf16[512,2048]{1,0:T(8,128)(2,1)S(1)} %copy-done.1, ...), custom_call_target="tpu_custom_call", output_to_operand_aliasing={{}: (5, {})} | custom-call | tf_op jit(solution)/shard_map/mla_heads/pallas_call | solution.py:426
  41.5 0.9 %kda_out.2.rest_0_ = bf16[128,2048]{1,0:T(8,128)(2,1)} custom-call(bf16[128,1024]{1,0:T(8,128)(2,1)S(1)} %get-tuple-element.74.qe_ref, f32[128,1024]{1,0:T(8,128)S(1)} %get-tuple-element.75.lo_ref, bf16[8,128,128]{2,1,0:T(8,128)(2,1)S(1)} %get-tuple-element.76.s_ref), custom_call_target="tpu_custom_call" | custom-call | tf_op jit(solution)/shard_map/kda_out/pallas_call | solution.py:307
  42.4 2.0 %collective-permute-done.10.s_ref = bf16[8,128,128]{2,1,0:T(8,128)(2,1)S(1)} collective-permute-done((bf16[8,128,128]{2,1,0:T(8,128)(2,1)S(1)}, bf16[8,128,128]{2,1,0:T(8,128)(2,1)S(1)}, u32[]{:S(2)}, u32[]{:S(2)}) %collective-permute-start.10) | collective-permute-done | bytes 262176 | tf_op jit(solution)/shard_map/ppermute | solution.py:462
  44.4 0.9 %kda_out.3 = bf16[128,2048]{1,0:T(8,128)(2,1)} custom-call(bf16[128,1024]{1,0:T(8,128)(2,1)S(1)} %get-tuple-element.56.qe_ref, f32[128,1024]{1,0:T(8,128)S(1)} %get-tuple-element.57.lo_ref, bf16[8,128,128]{2,1,0:T(8,128)(2,1)S(1)} %collective-permute-done.10.s_ref, bf16[128,2048]{1,0:T(8,128)(2,1)} %kda_out.2.rest_0_), custom_call_target="tpu_custom_call", output_to_operand_aliasing={{}: (3, {})} | custom-call | tf_op jit(solution)/shard_map/kda_out/pallas_call | solution.py:307
Async XLA Ops:
  0.6 9.2 %copy-start.8 = (f32[128,16]{0,1:T(8,128)S(1)}, f32[128,16]{0,1:T(8,128)}, u32[]{:S(2)}) copy-start(f32[128,16]{0,1:T(8,128)} %param.14) | copy-start | bytes 24580
  0.6 9.2 %copy-start.3 = (bf16[128,2048]{1,0:T(8,128)(2,1)S(1)}, bf16[128,2048]{1,0:T(8,128)(2,1)}, u32[]{:S(2)}) copy-start(bf16[128,2048]{1,0:T(8,128)(2,1)} %refs_1_.3) | copy-start | bytes 1572868
  0.7 9.1 %copy-start.4 = (bf16[128,2048]{1,0:T(8,128)(2,1)S(1)}, bf16[128,2048]{1,0:T(8,128)(2,1)}, u32[]{:S(2)}) copy-start(bf16[128,2048]{1,0:T(8,128)(2,1)} %refs_3_.3) | copy-start | bytes 1572868
  0.7 9.1 %copy-start.2 = (bf16[128,2048]{1,0:T(8,128)(2,1)S(1)}, bf16[128,2048]{1,0:T(8,128)(2,1)}, u32[]{:S(2)}) copy-start(bf16[128,2048]{1,0:T(8,128)(2,1)} %refs_0_.3) | copy-start | bytes 1572868
  0.7 9.1 %copy-start.9 = (s32[8]{0:T(128)S(1)}, s32[8]{0:T(128)}, u32[]{:S(2)}) copy-start(s32[8]{0:T(128)} %lengths) | copy-start | bytes 100
  0.7 9.1 %copy-start.6 = (bf16[128,2048]{1,0:T(8,128)(2,1)S(1)}, bf16[128,2048]{1,0:T(8,128)(2,1)}, u32[]{:S(2)}) copy-start(bf16[128,2048]{1,0:T(8,128)(2,1)} %refs_2_.3) | copy-start | bytes 1572868
  5.2 15.1 %collective-permute-start.2 = (bf16[8,128,256]{2,1,0:T(8,128)(2,1)}, bf16[8,128,256]{2,1,0:T(8,128)(2,1)S(1)}, u32[]{:S(2)}, u32[]{:S(2)}) collective-permute-start(bf16[8,128,256]{2,1,0:T(8,128)(2,1)} %kda_slab.3), channel_id=1, source_target_pairs={{0,4},{4,0},{8,12},{12,8},{16,20},{20,16},{24,28},{28,24},{1,5},{5... | collective-permute-start | bytes 1572872 | tf_op jit(solution)/shard_map/ppermute | solution.py:462
  8.2 11.7 %copy-start.7 = (bf16[128,576]{0,1:T(8,128)(2,1)S(1)}, bf16[128,576]{0,1:T(8,128)(2,1)}, u32[]{:S(2)}) copy-start(bf16[128,576]{0,1:T(8,128)(2,1)} %param.16) | copy-start | bytes 442372
  8.2 5.5 %collective-permute-start = (bf16[576,128]{1,0:T(8,128)(2,1)}, bf16[576,128]{1,0:T(8,128)(2,1)S(1)}, u32[]{:S(2)}, u32[]{:S(2)}) collective-permute-start(bf16[576,128]{1,0:T(8,128)(2,1)} %bitcast.2), channel_id=1, source_target_pairs={{0,8},{4,12},{8,0},{12,4},{16,24},{20,28},{24,16},{28,20},{1,9},{5... | collective-permute-start | bytes 442376 | tf_op jit(solution)/shard_map/ppermute | solution.py:462
  9.8 3.9 %collective-permute-start.1 = (bf16[576,128]{1,0:T(8,128)(2,1)}, bf16[576,128]{1,0:T(8,128)(2,1)S(1)}, u32[]{:S(2)}, u32[]{:S(2)}) collective-permute-start(bf16[576,128]{1,0:T(8,128)(2,1)} %bitcast.3), channel_id=1, source_target_pairs={{0,1},{1,0},{2,3},{3,2},{4,5},{5,4},{6,7},{7,6},{8,16},{9,17},{10,... | collective-permute-start | bytes 442376 | tf_op jit(solution)/shard_map/ppermute | solution.py:467
  13.7 6.1 %collective-permute-start.3 = (bf16[576,128]{1,0:T(8,128)(2,1)S(1)}, bf16[576,128]{1,0:T(8,128)(2,1)S(1)}, u32[]{:S(2)}, u32[]{:S(2)}) collective-permute-start(bf16[576,128]{1,0:T(8,128)(2,1)S(1)} %collective-permute-done.1.refs_1_), channel_id=1, source_target_pairs={{0,8},{4,12},{8,0},{12,4},{16,24},{20,28},{24,16},{28,20},{1,9},{5... | collective-permute-start | bytes 442376 | tf_op jit(solution)/shard_map/ppermute | solution.py:462
  16.5 3.4 %collective-permute-start.4 = (bf16[576,128]{1,0:T(8,128)(2,1)S(1)}, bf16[576,128]{1,0:T(8,128)(2,1)S(1)}, u32[]{:S(2)}, u32[]{:S(2)}) collective-permute-start(bf16[576,128]{1,0:T(8,128)(2,1)S(1)} %collective-permute-done.refs_0_), channel_id=1, source_target_pairs={{0,1},{1,0},{2,3},{3,2},{4,5},{5,4},{6,7},{7,6},{8,16},{9,17},{10,... | collective-permute-start | bytes 442376 | tf_op jit(solution)/shard_map/ppermute | solution.py:467
  16.5 15.5 %copy-start.1 = (bf16[512,2048]{1,0:T(8,128)(2,1)S(1)}, bf16[512,2048]{1,0:T(8,128)(2,1)}, u32[]{:S(2)}) copy-start(bf16[512,2048]{1,0:T(8,128)(2,1)} %vu_ref.3) | copy-start | bytes 6291460
  19.1 12.8 %copy-start = (bf16[512,2048]{1,0:T(8,128)(2,1)S(1)}, bf16[512,2048]{1,0:T(8,128)(2,1)}, u32[]{:S(2)}) copy-start(bf16[512,2048]{1,0:T(8,128)(2,1)} %ku_ref.3) | copy-start | bytes 6291460
  19.1 12.8 %copy-start.5 = (bf16[128,3072]{1,0:T(8,128)(2,1)S(1)}, bf16[128,3072]{1,0:T(8,128)(2,1)}, u32[]{:S(2)}) copy-start(bf16[128,3072]{1,0:T(8,128)(2,1)} %q_ref.3) | copy-start | bytes 2359300
  20.6 8.4 %collective-permute-start.5 = (bf16[8,128,128]{2,1,0:T(8,128)(2,1)S(1)}, bf16[8,128,128]{2,1,0:T(8,128)(2,1)S(1)}, u32[]{:S(2)}, u32[]{:S(2)}) collective-permute-start(bf16[8,128,128]{2,1,0:T(8,128)(2,1)S(1)} %get-tuple-element.63.pu_ref), channel_id=1, source_target_pairs={{0,8},{4,12},{8,0},{12,4},{16,24},{20,28},{24,16},{28,20},{1,9},{5... | collective-permute-start | bytes 786440 | tf_op jit(solution)/shard_map/ppermute | solution.py:462
  22.5 6.5 %collective-permute-start.6 = (bf16[8,128,128]{2,1,0:T(8,128)(2,1)S(1)}, bf16[8,128,128]{2,1,0:T(8,128)(2,1)S(1)}, u32[]{:S(2)}, u32[]{:S(2)}) collective-permute-start(bf16[8,128,128]{2,1,0:T(8,128)(2,1)S(1)} %get-tuple-element.63.pu_ref), channel_id=1, source_target_pairs={{0,1},{1,0},{2,3},{3,2},{4,5},{5,4},{6,7},{7,6},{8,16},{9,17},{10,... | collective-permute-start | bytes 786440 | tf_op jit(solution)/shard_map/ppermute | solution.py:467
  22.5 9.4 %collective-permute-start.9 = (bf16[2,576,128]{2,1,0:T(8,128)(2,1)S(1)}, bf16[2,576,128]{2,1,0:T(8,128)(2,1)S(1)}, u32[]{:S(2)}, u32[]{:S(2)}) collective-permute-start(bf16[2,576,128]{2,1,0:T(8,128)(2,1)S(1)} %get-tuple-element.65), channel_id=1, source_target_pairs={{0,4},{4,0},{8,12},{12,8},{16,20},{20,16},{24,28},{28,24},{1,5},{5... | collective-permute-start | bytes 884744 | tf_op jit(solution)/shard_map/ppermute | solution.py:462
  29.3 7.6 %collective-permute-start.7 = (bf16[8,128,128]{2,1,0:T(8,128)(2,1)S(1)}, bf16[8,128,128]{2,1,0:T(8,128)(2,1)S(1)}, u32[]{:S(2)}, u32[]{:S(2)}) collective-permute-start(bf16[8,128,128]{2,1,0:T(8,128)(2,1)S(1)} %pair_step.1), channel_id=1, source_target_pairs={{0,8},{4,12},{8,0},{12,4},{16,24},{20,28},{24,16},{28,20},{1,9},{5... | collective-permute-start | bytes 786440 | tf_op jit(solution)/shard_map/ppermute | solution.py:462
  31.2 5.7 %collective-permute-start.8 = (bf16[8,128,128]{2,1,0:T(8,128)(2,1)S(1)}, bf16[8,128,128]{2,1,0:T(8,128)(2,1)S(1)}, u32[]{:S(2)}, u32[]{:S(2)}) collective-permute-start(bf16[8,128,128]{2,1,0:T(8,128)(2,1)S(1)} %pair_step.1), channel_id=1, source_target_pairs={{0,1},{1,0},{2,3},{3,2},{4,5},{5,4},{6,7},{7,6},{8,16},{9,17},{10,... | collective-permute-start | bytes 786440 | tf_op jit(solution)/shard_map/ppermute | solution.py:467
  37.1 7.2 %collective-permute-start.10 = (bf16[8,128,128]{2,1,0:T(8,128)(2,1)S(1)}, bf16[8,128,128]{2,1,0:T(8,128)(2,1)S(1)}, u32[]{:S(2)}, u32[]{:S(2)}) collective-permute-start(bf16[8,128,128]{2,1,0:T(8,128)(2,1)S(1)} %get-tuple-element.69), channel_id=1, source_target_pairs={{0,4},{4,0},{8,12},{12,8},{16,20},{20,16},{24,28},{28,24},{1,5},{5... | collective-permute-start | bytes 786440 | tf_op jit(solution)/shard_map/ppermute | solution.py:462

commit v5 on v4

--- a/solution.py
+++ b/solution.py
@@ -13,7 +13,7 @@
 ROPE = 64
 LATENT = 512
 VMEM = 20 * 1024 * 1024
-ALL_VMEM = 56 * 1024 * 1024
+ALL_VMEM = 20 * 1024 * 1024
 WHOLE = pl.BlockSpec(memory_space=pltpu.VMEM)
 SCALARS = pl.BlockSpec(memory_space=pltpu.SMEM)
 FAR = pl.BlockSpec(memory_space=pltpu.HBM)
@@ -44,29 +44,43 @@
     return total
 
 
-def kda_kernel(ndocs, flip, states, outputs, *refs):
-    names = [name for name in "gkqv" if name != "q" or outputs]
-    sources, small = refs[: len(names)], refs[len(names) : len(names) + 2]
-    refs = refs[len(names) + 2 :]
+def kda_kernel(ndocs, flip, fetch, states, outputs, *refs):
+    place = lax.axis_index("ctx")
+    side = (place + flip) % 2
+    later = []
+    if fetch:
+        far, far_lengths, far_b = refs[:4], refs[4], refs[5]
+        held, other, b_ref, refs = refs[6:10], refs[10:14], refs[14], refs[15:]
+        lengths, sems = refs[-2:]
+        rows, width = held[0].shape
+
+        def copies(blocks, which, first):
+            start = pl.multiple_of(which * width, width)
+            return [
+                pltpu.make_async_copy(source.at[:, pl.ds(start, width)], to, sems.at[first + j])
+                for j, (source, to) in enumerate(zip(far, blocks))
+            ]
+
+        now = copies(held, side, 0)
+        small = [
+            pltpu.make_async_copy(far_lengths, lengths, sems.at[8]),
+            pltpu.make_async_copy(far_b, b_ref, sems.at[9]),
+        ]
+        later = copies(other, 1 - side, 4)
+        if not outputs:
+            later, now = [now[3], *later], now[:3]
+        for copy in [*now, *small, *later]:
+            copy.start()
+    else:
+        held, lengths, b_ref, refs = refs[:4], refs[4], refs[5], refs[6:]
+        rows, width = held[0].shape
+        now, small = [], []
+    sc = lengths
+    block = dict(zip("gkvq", held))
     if states:
         mu_ref, refs = refs[0], refs[1:]
     if outputs:
-        qe_ref, lo_ref, refs = refs[0], refs[1], refs[2:]
-    blocks, (b_ref, sc, sems, small_sems) = refs[: len(names)], refs[len(names) :]
-    block = dict(zip(names, blocks))
-    rows, width = blocks[0].shape
-    place = lax.axis_index("ctx")
-    side = (place + flip) % 2
-    start = pl.multiple_of(side * width, width)
-    copies = [
-        pltpu.make_async_copy(source.at[:, pl.ds(start, width)], to, sems.at[j])
-        for j, (source, to) in enumerate(zip(sources, blocks))
-    ] + [
-        pltpu.make_async_copy(source, to, small_sems.at[j])
-        for j, (source, to) in enumerate(zip(small, (sc, b_ref)))
-    ]
-    for copy in copies:
-        copy.start()
+        qe_ref, lo_ref = refs[:2]
     half = rows // 2
     heads = width // 128
     base = side * heads
@@ -77,7 +91,7 @@
     low = ci < half
     eye = (ri == ci).astype(F32)
     zeros = jnp.zeros((half, 128), BF)
-    for copy in copies[: len(names) - 1]:
+    for copy in now[:2]:
         copy.wait()
     cum_all = mm(tri, block["g"][...])
 
@@ -121,7 +135,7 @@
         )
         kept.append((kd * grow * grow, ku * wane * wane, queried, jnp.exp(end)))
 
-    for copy in copies[len(names) - 1 :]:
+    for copy in [*now[2:], *small]:
         copy.wait()
     doc_r = doc_of(first + ri, sc, ndocs)
     doc_c = doc_of(first + ci, sc, ndocs)
@@ -181,35 +195,53 @@
             y = mm(mix[h], wu[h])
             qe_ref[:, cols] = (kept[h][2] * follow - y[:, :128]).astype(BF)
             lo_ref[:, cols] = y[:, 128:]
-
-
-def kda_half(flip, lengths, q, k, v, g, b, states=True, outputs=True, limit=VMEM):
-    rows, width = q.shape[0], q.shape[1] // 2
-    heads, ndocs = b.shape[0], lengths.shape[0]
-    args = [g, k] + ([q] if outputs else []) + [v, lengths, b]
-    wide = len(args) - 2
-    shapes = [jax.ShapeDtypeStruct((heads // 2, 128, 256), BF)] if states else []
-    if outputs:
-        shapes += [
-            jax.ShapeDtypeStruct((rows, width), BF),
-            jax.ShapeDtypeStruct((rows, width), F32),
-        ]
+    for copy in later:
+        copy.wait()
+
+
+def kda_call(kernel, in_specs, shapes, scratch, limit, args):
     return pl.pallas_call(
-        functools.partial(kda_kernel, ndocs, flip, states, outputs),
-        in_specs=[FAR] * len(args),
+        kernel,
+        in_specs=in_specs,
         out_specs=[WHOLE] * len(shapes),
         out_shape=shapes,
-        scratch_shapes=[pltpu.VMEM((rows, width), BF)] * wide
-        + [
-            pltpu.VMEM(b.shape, F32),
-            pltpu.SMEM(lengths.shape, jnp.int32),
-            pltpu.SemaphoreType.DMA((wide,)),
-            pltpu.SemaphoreType.DMA((2,)),
-        ],
+        scratch_shapes=scratch,
+        cost_estimate=CHEAP,
         compiler_params=pltpu.CompilerParams(vmem_limit_bytes=limit),
-        cost_estimate=CHEAP,
         name="kda_slab",
     )(*args)
+
+
+def kda_first(lengths, q, k, v, g, b):
+    rows, width, heads = q.shape[0], q.shape[1] // 2, b.shape[0]
+    block = jax.ShapeDtypeStruct((rows, width), BF)
+    outs = kda_call(
+        functools.partial(kda_kernel, lengths.shape[0], 1, True, True, False),
+        [FAR] * 6,
+        [block] * 8
+        + [
+            jax.ShapeDtypeStruct(b.shape, F32),
+            jax.ShapeDtypeStruct((heads // 2, 128, 256), BF),
+        ],
+        [pltpu.SMEM(lengths.shape, jnp.int32), pltpu.SemaphoreType.DMA((10,))],
+        ALL_VMEM,
+        [pltpu.with_memory_space_constraint(x, pltpu.HBM) for x in (g, k, v, q, lengths, b)],
+    )
+    return outs[9], outs[:4], outs[4:8], outs[8]
+
+
+def kda_half(flip, blocks, lengths, b, states):
+    rows, width = blocks[0].shape
+    shapes = [jax.ShapeDtypeStruct((b.shape[0] // 2, 128, 256), BF)] if states else []
+    shapes += [jax.ShapeDtypeStruct((rows, width), BF), jax.ShapeDtypeStruct((rows, width), F32)]
+    return kda_call(
+        functools.partial(kda_kernel, lengths.shape[0], flip, False, states, True),
+        [WHOLE] * 4 + [SCALARS, WHOLE],
+        shapes,
+        [],
+        VMEM,
+        [*blocks, lengths, b],
+    )
 
 
 def pair_kernel(own_ref, got_ref, pm_ref, pu_ref):
@@ -484,22 +516,21 @@
     reach = n // 2
     rounds = -(-n // 4)
     mate, up, middle = routes(n)
-    kda_args = (doc_lengths, kda_query, kda_key, kda_value, log_decay, write_rate.T)
-
     lat = latents.T
     shape = (heads // 2, 128, 128)
     def after(x, *others):
         return lax.optimization_barrier((x, others))[0]
 
-    (mu_away,) = kda_half(1, *kda_args, outputs=False, limit=ALL_VMEM)
+    mu_away, away, own, rates = kda_first(
+        doc_lengths, kda_query, kda_key, kda_value, log_decay, write_rate.T
+    )
     mu_got = swap(mu_away, mate)
-    args = after(kda_args, mu_away)
     early = after(lat, mu_away)
     moved = [(swap(early, up), swap(early, middle))]
-    mu_own, qe_own, lo_own = kda_half(0, *args)
+    mu_own, qe_own, lo_own = kda_half(0, own, doc_lengths, rates, True)
     moved[0] = after(moved[0], mu_own)
-    args = after(args, mu_own, moved[0])
-    qe_away, lo_away = kda_half(1, *args, states=False)
+    away = after(away, mu_own, moved[0])
+    qe_away, lo_away = kda_half(1, away, doc_lengths, rates, False)
     for _ in range(rounds - 1):
         a, b = moved[-1]
         moved.append((swap(b, up), swap(a, middle)))

time: 45.6 us -> 44.7 us (0.980)
  Pallas kernels: 21 us -> 20.5 us
  transfers between devices with their start and end apart: 11 -> 11, of which waited for: 6 -> 6; matrix products, arithmetic and copies ran while one was open for 0% -> 0% of each run, Pallas kernels for 33% -> 34%
where the time goes in v5:
time: 44.7 us; the launch traced here: 44.6 us
  Pallas kernels  20.5 us (46%)
  starting transfers between devices  13.1 us (29%)
  waiting for transfers between devices  10 us (22%)
  between operations  0.93 us (2%)
    ppermute x7, starting transfers between devices, swap(): return lax.ppermute(x, 'ctx', list(enumerate(table)))  13 us
    ppermute x7, waiting for transfers between devices, swap(): return lax.ppermute(x, 'ctx', list(enumerate(table)))  10 us
    pallas_call x3, Pallas kernels, kda_call(): pl.pallas_call(kernel, in_specs=in_specs, out_specs=[WHOLE] * len(shapes)...  9.71 us
    pallas_call x2, Pallas kernels, mla(): pl.pallas_call(functools.partial(mla_kernel, reach, previous is None, fir...  7.5 us
    pallas_call x2, Pallas kernels, final(): pl.pallas_call(functools.partial(final_kernel, flip), in_specs=specs, out...  1.8 us
  transfers between devices with their start and end apart: 11, of which 6 were waited for; matrix products, arithmetic and copies ran while one was open for 0% of the time, Pallas kernels for 34%

profile of v5, /device:TPU:0, one launch (start us, length us, event | category | flops | bytes accessed | tf_op | source)
XLA Modules:
  0.0 44.6 jit_solution(8168514359924642068)
XLA Ops:
  0.6 0.0 copy-start.4
  0.6 0.0 copy-start.3
  0.7 3.7 %kda_slab.3 = (bf16[128,1024]{1,0:T(8,128)(2,1)S(1)}, bf16[128,1024]{1,0:T(8,128)(2,1)S(1)}, bf16[128,1024]{1,0:T(8,128)(2,1)S(1)}, bf16[128,1024]{1,0:T(8,128)(...) custom-call(bf16[128,2048]{1,0:T(8,128)(2,1)} %refs_0_.1, ...), custom_call_target="tpu_custom_call" | custom-call | tf_op jit(solution)/shard_map/kda_slab/pallas_call | solution.py:203
  4.4 3.0 %collective-permute-start.2 = (bf16[8,128,256]{2,1,0:T(8,128)(2,1)S(1)}, bf16[8,128,256]{2,1,0:T(8,128)(2,1)S(1)}, u32[]{:S(2)}, u32[]{:S(2)}) collective-permute-start(bf16[8,128,256]{2,1,0:T(8,128)(2,1)S(1)} %get-tuple-element.52), channel_id=1, source_target_pairs={{0,4},{4,0},{8,12},{12,8},{16,20},{20,16},{24,28},{28,24},{1,5},{5... | collective-permute-start | bytes 1572872 | tf_op jit(solution)/shard_map/ppermute | solution.py:494
  7.4 0.0 copy-done.3
  7.4 1.6 %collective-permute-start = (bf16[576,128]{1,0:T(8,128)(2,1)S(1)}, bf16[576,128]{1,0:T(8,128)(2,1)S(1)}, u32[]{:S(2)}, u32[]{:S(2)}) collective-permute-start(bf16[576,128]{1,0:T(8,128)(2,1)S(1)} %bitcast.2), channel_id=1, source_target_pairs={{0,8},{4,12},{8,0},{12,4},{16,24},{20,28},{24,16},{28,20},{1,9},{5... | collective-permute-start | bytes 442376 | tf_op jit(solution)/shard_map/ppermute | solution.py:494
  9.0 0.0 collective-permute-start.1
  9.0 0.0 copy-done.4
  9.0 0.0 copy-start.2
  9.0 3.1 %kda_slab.4 = (bf16[8,128,256]{2,1,0:T(8,128)(2,1)S(1)}, bf16[128,1024]{1,0:T(8,128)(2,1)S(1)}, f32[128,1024]{1,0:T(8,128)S(1)}) custom-call(bf16[128,1024]{1,0:T(8,128)(2,1)S(1)} %get-tuple-element.46.refs_0_, bf16[128,1024]{1,0:T(8,128)(2,1)S(1)} %get-tuple-element.47.refs_1_, bf16[128,1024]{1,0:T(8,128)(2,1)S(1)} %get-tuple-element.48.refs_2_, ...), custom_call_target="tpu_custom_call" | custom-call | tf_op jit(solution)/shard_map/kda_slab/pallas_call | solution.py:203
  12.1 0.6 %collective-permute-done.refs_0_ = bf16[576,128]{1,0:T(8,128)(2,1)S(1)} collective-permute-done((bf16[576,128]{1,0:T(8,128)(2,1)S(1)}, bf16[576,128]{1,0:T(8,128)(2,1)S(1)}, u32[]{:S(2)}, u32[]{:S(2)}) %collective-permute-start) | collective-permute-done | bytes 147488 | tf_op jit(solution)/shard_map/ppermute | solution.py:494
  12.7 0.0 collective-permute-done.1.refs_1_
  12.7 2.7 %collective-permute-start.3 = (bf16[576,128]{1,0:T(8,128)(2,1)S(1)}, bf16[576,128]{1,0:T(8,128)(2,1)S(1)}, u32[]{:S(2)}, u32[]{:S(2)}) collective-permute-start(bf16[576,128]{1,0:T(8,128)(2,1)S(1)} %collective-permute-done.1.refs_1_), channel_id=1, source_target_pairs={{0,8},{4,12},{8,0},{12,4},{16,24},{20,28},{24,16},{28,20},{1,9},{5... | collective-permute-start | bytes 442376 | tf_op jit(solution)/shard_map/ppermute | solution.py:494
  15.4 0.0 collective-permute-start.4
  15.4 0.0 copy-start
  15.4 0.0 copy-start.1
  15.4 2.9 %kda_slab.5 = (bf16[128,1024]{1,0:T(8,128)(2,1)S(1)}, f32[128,1024]{1,0:T(8,128)S(1)}) custom-call(bf16[128,1024]{1,0:T(8,128)(2,1)S(1)} %get-tuple-element.56.refs_0_, bf16[128,1024]{1,0:T(8,128)(2,1)S(1)} %get-tuple-element.57.refs_1_, bf16[128,1024]{1,0:T(8,128)(2,1)S(1)} %get-tuple-element.58.refs_2_, bf16[128,1024]{1,0:T(8,128)(2,1)S(1)} %get-tuple-element.59.refs_3_, ...), custom_call_target="tpu_custom_call" | custom-call | tf_op jit(solution)/shard_map/kda_slab/pallas_call | solution.py:203
  18.3 0.7 %window_mask.1.bias_ref = f32[128,640]{1,0:T(8,128)S(1)} custom-call(s32[8]{0:T(128)S(1)} %copy-done.4), custom_call_target="tpu_custom_call" | custom-call | tf_op jit(solution)/shard_map/window_mask/pallas_call | solution.py:398
  18.9 0.0 collective-permute-done.3.refs_2_
  19.0 0.0 collective-permute-done.4.refs_3_
  19.0 0.1 pick_latents.1
  19.0 0.3 collective-permute-done.2.got_ref
  19.3 0.3 pair_join.1
  19.6 1.9 %collective-permute-start.5 = (bf16[8,128,128]{2,1,0:T(8,128)(2,1)S(1)}, bf16[8,128,128]{2,1,0:T(8,128)(2,1)S(1)}, u32[]{:S(2)}, u32[]{:S(2)}) collective-permute-start(bf16[8,128,128]{2,1,0:T(8,128)(2,1)S(1)} %get-tuple-element.67.pu_ref), channel_id=1, source_target_pairs={{0,8},{4,12},{8,0},{12,4},{16,24},{20,28},{24,16},{28,20},{1,9},{5... | collective-permute-start | bytes 786440 | tf_op jit(solution)/shard_map/ppermute | solution.py:494
  21.5 0.0 collective-permute-start.6
  21.5 1.5 %collective-permute-start.9 = (bf16[2,576,128]{2,1,0:T(8,128)(2,1)S(1)}, bf16[2,576,128]{2,1,0:T(8,128)(2,1)S(1)}, u32[]{:S(2)}, u32[]{:S(2)}) collective-permute-start(bf16[2,576,128]{2,1,0:T(8,128)(2,1)S(1)} %get-tuple-element.69), channel_id=1, source_target_pairs={{0,4},{4,0},{8,12},{12,8},{16,20},{20,16},{24,28},{28,24},{1,5},{5... | collective-permute-start | bytes 884744 | tf_op jit(solution)/shard_map/ppermute | solution.py:494
  23.0 5.2 %collective-permute-done.5.a_ref = bf16[8,128,128]{2,1,0:T(8,128)(2,1)S(1)} collective-permute-done((bf16[8,128,128]{2,1,0:T(8,128)(2,1)S(1)}, bf16[8,128,128]{2,1,0:T(8,128)(2,1)S(1)}, u32[]{:S(2)}, u32[]{:S(2)}) %collective-permute-start.5) | collective-permute-done | bytes 262176 | tf_op jit(solution)/shard_map/ppermute | solution.py:494
  28.2 0.0 collective-permute-done.6.b_ref
  28.2 0.2 pair_step.1
  28.4 1.9 %collective-permute-start.7 = (bf16[8,128,128]{2,1,0:T(8,128)(2,1)S(1)}, bf16[8,128,128]{2,1,0:T(8,128)(2,1)S(1)}, u32[]{:S(2)}, u32[]{:S(2)}) collective-permute-start(bf16[8,128,128]{2,1,0:T(8,128)(2,1)S(1)} %pair_step.1), channel_id=1, source_target_pairs={{0,8},{4,12},{8,0},{12,4},{16,24},{20,28},{24,16},{28,20},{1,9},{5... | collective-permute-start | bytes 786440 | tf_op jit(solution)/shard_map/ppermute | solution.py:494
  30.3 0.0 collective-permute-start.8
  30.3 0.6 %collective-permute-done.9.refs_1_ = bf16[2,576,128]{2,1,0:T(8,128)(2,1)S(1)} collective-permute-done((bf16[2,576,128]{2,1,0:T(8,128)(2,1)S(1)}, bf16[2,576,128]{2,1,0:T(8,128)(2,1)S(1)}, u32[]{:S(2)}, u32[]{:S(2)}) %collective-permute-start.9) | collective-permute-done | bytes 294944 | tf_op jit(solution)/shard_map/ppermute | solution.py:494
  30.9 0.0 copy-done.2
  30.9 0.0 copy-done
  30.9 0.0 copy-done.1
  30.9 3.9 %mla_heads.2 = (bf16[640,576]{1,0:T(8,128)(2,1)S(1)}, bf16[128,2048]{1,0:T(8,128)(2,1)}) custom-call(f32[128,640]{1,0:T(8,128)S(1)} %window_mask.1.bias_ref, bf16[128,3072]{1,0:T(8,128)(2,1)S(1)} %copy-done.2, bf16[512,2048]{1,0:T(8,128)(2,1)S(1)} %copy-done, bf16[512,2048]{1,0:T(8,128)(2,1)S(1)} %copy-done.1, ...), custom_call_target="tpu_custom_call" | custom-call | tf_op jit(solution)/shard_map/mla_heads/pallas_call | solution.py:458
  34.8 1.3 %collective-permute-done.7.a_ref = bf16[8,128,128]{2,1,0:T(8,128)(2,1)S(1)} collective-permute-done((bf16[8,128,128]{2,1,0:T(8,128)(2,1)S(1)}, bf16[8,128,128]{2,1,0:T(8,128)(2,1)S(1)}, u32[]{:S(2)}, u32[]{:S(2)}) %collective-permute-start.7) | collective-permute-done | bytes 262176 | tf_op jit(solution)/shard_map/ppermute | solution.py:494
  36.1 0.0 collective-permute-done.8.b_ref
  36.1 0.3 slab_states.1
  36.4 0.5 %collective-permute-start.10 = (bf16[8,128,128]{2,1,0:T(8,128)(2,1)S(1)}, bf16[8,128,128]{2,1,0:T(8,128)(2,1)S(1)}, u32[]{:S(2)}, u32[]{:S(2)}) collective-permute-start(bf16[8,128,128]{2,1,0:T(8,128)(2,1)S(1)} %get-tuple-element.73), channel_id=1, source_target_pairs={{0,4},{4,0},{8,12},{12,8},{16,20},{20,16},{24,28},{28,24},{1,5},{5... | collective-permute-start | bytes 786440 | tf_op jit(solution)/shard_map/ppermute | solution.py:494
  36.9 3.6 %mla_heads.3 = bf16[128,2048]{1,0:T(8,128)(2,1)} custom-call(f32[128,640]{1,0:T(8,128)S(1)} %window_mask.1.bias_ref, bf16[128,3072]{1,0:T(8,128)(2,1)S(1)} %copy-done.2, bf16[512,2048]{1,0:T(8,128)(2,1)S(1)} %copy-done, bf16[512,2048]{1,0:T(8,128)(2,1)S(1)} %copy-done.1, ...), custom_call_target="tpu_custom_call", output_to_operand_aliasing={{}: (5, {})} | custom-call | tf_op jit(solution)/shard_map/mla_heads/pallas_call | solution.py:458
  40.5 0.9 %kda_out.2.rest_0_ = bf16[128,2048]{1,0:T(8,128)(2,1)} custom-call(bf16[128,1024]{1,0:T(8,128)(2,1)S(1)} %get-tuple-element.78.qe_ref, f32[128,1024]{1,0:T(8,128)S(1)} %get-tuple-element.79.lo_ref, bf16[8,128,128]{2,1,0:T(8,128)(2,1)S(1)} %get-tuple-element.80.s_ref), custom_call_target="tpu_custom_call" | custom-call | tf_op jit(solution)/shard_map/kda_out/pallas_call | solution.py:339
  41.4 2.1 %collective-permute-done.10.s_ref = bf16[8,128,128]{2,1,0:T(8,128)(2,1)S(1)} collective-permute-done((bf16[8,128,128]{2,1,0:T(8,128)(2,1)S(1)}, bf16[8,128,128]{2,1,0:T(8,128)(2,1)S(1)}, u32[]{:S(2)}, u32[]{:S(2)}) %collective-permute-start.10) | collective-permute-done | bytes 262176 | tf_op jit(solution)/shard_map/ppermute | solution.py:494
  43.5 0.9 %kda_out.3 = bf16[128,2048]{1,0:T(8,128)(2,1)} custom-call(bf16[128,1024]{1,0:T(8,128)(2,1)S(1)} %get-tuple-element.60.qe_ref, f32[128,1024]{1,0:T(8,128)S(1)} %get-tuple-element.61.lo_ref, bf16[8,128,128]{2,1,0:T(8,128)(2,1)S(1)} %collective-permute-done.10.s_ref, bf16[128,2048]{1,0:T(8,128)(2,1)} %kda_out.2.rest_0_), custom_call_target="tpu_custom_call", output_to_operand_aliasing={{}: (3, {})} | custom-call | tf_op jit(solution)/shard_map/kda_out/pallas_call | solution.py:339
Async XLA Ops:
  0.6 8.3 %copy-start.4 = (s32[8]{0:T(128)S(1)}, s32[8]{0:T(128)}, u32[]{:S(2)}) copy-start(s32[8]{0:T(128)} %lengths) | copy-start | bytes 100
  0.6 6.7 %copy-start.3 = (bf16[128,576]{0,1:T(8,128)(2,1)S(1)}, bf16[128,576]{0,1:T(8,128)(2,1)}, u32[]{:S(2)}) copy-start(bf16[128,576]{0,1:T(8,128)(2,1)} %param.16) | copy-start | bytes 442372
  4.4 14.9 %collective-permute-start.2 = (bf16[8,128,256]{2,1,0:T(8,128)(2,1)S(1)}, bf16[8,128,256]{2,1,0:T(8,128)(2,1)S(1)}, u32[]{:S(2)}, u32[]{:S(2)}) collective-permute-start(bf16[8,128,256]{2,1,0:T(8,128)(2,1)S(1)} %get-tuple-element.52), channel_id=1, source_target_pairs={{0,4},{4,0},{8,12},{12,8},{16,20},{20,16},{24,28},{28,24},{1,5},{5... | collective-permute-start | bytes 1572872 | tf_op jit(solution)/shard_map/ppermute | solution.py:494
  7.4 5.3 %collective-permute-start = (bf16[576,128]{1,0:T(8,128)(2,1)S(1)}, bf16[576,128]{1,0:T(8,128)(2,1)S(1)}, u32[]{:S(2)}, u32[]{:S(2)}) collective-permute-start(bf16[576,128]{1,0:T(8,128)(2,1)S(1)} %bitcast.2), channel_id=1, source_target_pairs={{0,8},{4,12},{8,0},{12,4},{16,24},{20,28},{24,16},{28,20},{1,9},{5... | collective-permute-start | bytes 442376 | tf_op jit(solution)/shard_map/ppermute | solution.py:494
  9.0 3.7 %collective-permute-start.1 = (bf16[576,128]{1,0:T(8,128)(2,1)S(1)}, bf16[576,128]{1,0:T(8,128)(2,1)S(1)}, u32[]{:S(2)}, u32[]{:S(2)}) collective-permute-start(bf16[576,128]{1,0:T(8,128)(2,1)S(1)} %bitcast.3), channel_id=1, source_target_pairs={{0,1},{1,0},{2,3},{3,2},{4,5},{5,4},{6,7},{7,6},{8,16},{9,17},{10,... | collective-permute-start | bytes 442376 | tf_op jit(solution)/shard_map/ppermute | solution.py:499
  9.0 21.9 %copy-start.2 = (bf16[128,3072]{1,0:T(8,128)(2,1)S(1)}, bf16[128,3072]{1,0:T(8,128)(2,1)}, u32[]{:S(2)}) copy-start(bf16[128,3072]{1,0:T(8,128)(2,1)} %q_ref.3) | copy-start | bytes 2359300
  12.7 6.2 %collective-permute-start.3 = (bf16[576,128]{1,0:T(8,128)(2,1)S(1)}, bf16[576,128]{1,0:T(8,128)(2,1)S(1)}, u32[]{:S(2)}, u32[]{:S(2)}) collective-permute-start(bf16[576,128]{1,0:T(8,128)(2,1)S(1)} %collective-permute-done.1.refs_1_), channel_id=1, source_target_pairs={{0,8},{4,12},{8,0},{12,4},{16,24},{20,28},{24,16},{28,20},{1,9},{5... | collective-permute-start | bytes 442376 | tf_op jit(solution)/shard_map/ppermute | solution.py:494
  15.4 3.6 %collective-permute-start.4 = (bf16[576,128]{1,0:T(8,128)(2,1)S(1)}, bf16[576,128]{1,0:T(8,128)(2,1)S(1)}, u32[]{:S(2)}, u32[]{:S(2)}) collective-permute-start(bf16[576,128]{1,0:T(8,128)(2,1)S(1)} %collective-permute-done.refs_0_), channel_id=1, source_target_pairs={{0,1},{1,0},{2,3},{3,2},{4,5},{5,4},{6,7},{7,6},{8,16},{9,17},{10,... | collective-permute-start | bytes 442376 | tf_op jit(solution)/shard_map/ppermute | solution.py:499
  15.4 15.5 %copy-start = (bf16[512,2048]{1,0:T(8,128)(2,1)S(1)}, bf16[512,2048]{1,0:T(8,128)(2,1)}, u32[]{:S(2)}) copy-start(bf16[512,2048]{1,0:T(8,128)(2,1)} %ku_ref.3) | copy-start | bytes 6291460
  15.4 15.5 %copy-start.1 = (bf16[512,2048]{1,0:T(8,128)(2,1)S(1)}, bf16[512,2048]{1,0:T(8,128)(2,1)}, u32[]{:S(2)}) copy-start(bf16[512,2048]{1,0:T(8,128)(2,1)} %vu_ref.3) | copy-start | bytes 6291460
  19.6 8.6 %collective-permute-start.5 = (bf16[8,128,128]{2,1,0:T(8,128)(2,1)S(1)}, bf16[8,128,128]{2,1,0:T(8,128)(2,1)S(1)}, u32[]{:S(2)}, u32[]{:S(2)}) collective-permute-start(bf16[8,128,128]{2,1,0:T(8,128)(2,1)S(1)} %get-tuple-element.67.pu_ref), channel_id=1, source_target_pairs={{0,8},{4,12},{8,0},{12,4},{16,24},{20,28},{24,16},{28,20},{1,9},{5... | collective-permute-start | bytes 786440 | tf_op jit(solution)/shard_map/ppermute | solution.py:494
  21.5 6.7 %collective-permute-start.6 = (bf16[8,128,128]{2,1,0:T(8,128)(2,1)S(1)}, bf16[8,128,128]{2,1,0:T(8,128)(2,1)S(1)}, u32[]{:S(2)}, u32[]{:S(2)}) collective-permute-start(bf16[8,128,128]{2,1,0:T(8,128)(2,1)S(1)} %get-tuple-element.67.pu_ref), channel_id=1, source_target_pairs={{0,1},{1,0},{2,3},{3,2},{4,5},{5,4},{6,7},{7,6},{8,16},{9,17},{10,... | collective-permute-start | bytes 786440 | tf_op jit(solution)/shard_map/ppermute | solution.py:499
  21.5 9.4 %collective-permute-start.9 = (bf16[2,576,128]{2,1,0:T(8,128)(2,1)S(1)}, bf16[2,576,128]{2,1,0:T(8,128)(2,1)S(1)}, u32[]{:S(2)}, u32[]{:S(2)}) collective-permute-start(bf16[2,576,128]{2,1,0:T(8,128)(2,1)S(1)} %get-tuple-element.69), channel_id=1, source_target_pairs={{0,4},{4,0},{8,12},{12,8},{16,20},{20,16},{24,28},{28,24},{1,5},{5... | collective-permute-start | bytes 884744 | tf_op jit(solution)/shard_map/ppermute | solution.py:494
  28.4 7.7 %collective-permute-start.7 = (bf16[8,128,128]{2,1,0:T(8,128)(2,1)S(1)}, bf16[8,128,128]{2,1,0:T(8,128)(2,1)S(1)}, u32[]{:S(2)}, u32[]{:S(2)}) collective-permute-start(bf16[8,128,128]{2,1,0:T(8,128)(2,1)S(1)} %pair_step.1), channel_id=1, source_target_pairs={{0,8},{4,12},{8,0},{12,4},{16,24},{20,28},{24,16},{28,20},{1,9},{5... | collective-permute-start | bytes 786440 | tf_op jit(solution)/shard_map/ppermute | solution.py:494
  30.3 5.8 %collective-permute-start.8 = (bf16[8,128,128]{2,1,0:T(8,128)(2,1)S(1)}, bf16[8,128,128]{2,1,0:T(8,128)(2,1)S(1)}, u32[]{:S(2)}, u32[]{:S(2)}) collective-permute-start(bf16[8,128,128]{2,1,0:T(8,128)(2,1)S(1)} %pair_step.1), channel_id=1, source_target_pairs={{0,1},{1,0},{2,3},{3,2},{4,5},{5,4},{6,7},{7,6},{8,16},{9,17},{10,... | collective-permute-start | bytes 786440 | tf_op jit(solution)/shard_map/ppermute | solution.py:499
  36.4 7.1 %collective-permute-start.10 = (bf16[8,128,128]{2,1,0:T(8,128)(2,1)S(1)}, bf16[8,128,128]{2,1,0:T(8,128)(2,1)S(1)}, u32[]{:S(2)}, u32[]{:S(2)}) collective-permute-start(bf16[8,128,128]{2,1,0:T(8,128)(2,1)S(1)} %get-tuple-element.73), channel_id=1, source_target_pairs={{0,4},{4,0},{8,12},{12,8},{16,20},{20,16},{24,28},{28,24},{1,5},{5... | collective-permute-start | bytes 786440 | tf_op jit(solution)/shard_map/ppermute | solution.py:494

commit v6 on v5

--- a/solution.py
+++ b/solution.py
@@ -304,45 +304,40 @@
     )(*args)
 
 
-def final_kernel(flip, qe_ref, lo_ref, s_ref, *rest):
-    out_ref, held_ref, sem = rest[-3:]
+def final_kernel(qe_ref, lo_ref, s_ref, *refs):
+    held_ref, copies = refs[0], []
     width = qe_ref.shape[1]
-    side = (lax.axis_index("ctx") + flip) % 2
-    start = pl.multiple_of(side * width, width)
-    parts = 2
-    part = width // parts
-    copies = []
+    if len(refs) > 1:
+        own_ref, out_ref, held_ref, sems = refs
+        side = lax.axis_index("ctx") % 2
+
+        def copy_out(source, which, sem):
+            start = pl.multiple_of(which * width, width)
+            copies.append(
+                pltpu.make_async_copy(source, out_ref.at[:, pl.ds(start, width)], sems.at[sem])
+            )
+            copies[-1].start()
+
+        copy_out(own_ref, side, 0)
     for h in range(s_ref.shape[0]):
         cols = slice(h * 128, (h + 1) * 128)
         held_ref[:, cols] = (lo_ref[:, cols] + mm(qe_ref[:, cols], s_ref[h])).astype(BF)
-        if (h + 1) * 128 % part == 0:
-            i = len(copies)
-            copies.append(
-                pltpu.make_async_copy(
-                    held_ref.at[:, pl.ds(i * part, part)],
-                    out_ref.at[:, pl.ds(start + i * part, part)],
-                    sem.at[i],
-                )
-            )
-            copies[-1].start()
+    if len(refs) > 1:
+        copy_out(held_ref, 1 - side, 1)
     for copy in copies:
         copy.wait()
 
 
-def final(flip, qe, lo, s, heads, previous):
+def final(qe, lo, s, own=None):
     rows, width = qe.shape
-    args, specs, aliases = [qe, lo, s], [WHOLE] * 3, {}
-    if previous is not None:
-        args.append(previous)
-        specs.append(FAR)
-        aliases = {3: 0}
+    args = [qe, lo, s] + ([] if own is None else [own])
+    scratch = [] if own is None else [pltpu.VMEM((rows, width), BF), pltpu.SemaphoreType.DMA((2,))]
     return pl.pallas_call(
-        functools.partial(final_kernel, flip),
-        in_specs=specs,
-        out_specs=FAR,
-        out_shape=jax.ShapeDtypeStruct((rows, heads * 128), BF),
-        scratch_shapes=[pltpu.VMEM((rows, width), BF), pltpu.SemaphoreType.DMA((2,))],
-        input_output_aliases=aliases,
+        final_kernel,
+        in_specs=[WHOLE] * len(args),
+        out_specs=WHOLE if own is None else FAR,
+        out_shape=jax.ShapeDtypeStruct((rows, width if own is None else 2 * width), BF),
+        scratch_shapes=scratch,
         cost_estimate=CHEAP,
         compiler_params=pltpu.CompilerParams(vmem_limit_bytes=VMEM // 2),
         name="kda_out",
@@ -407,13 +402,15 @@
 
 
 def mla_kernel(reach, fresh, first, bias_ref, q_ref, ku_ref, vu_ref, *refs):
-    out_ref, held_ref, sem = refs[-3:]
     rows = q_ref.shape[0]
-    if not fresh:
-        lat_ref = refs[0]
+    copies = []
+    if fresh:
+        lat_ref, held_ref = refs[2:]
+        window_rows(lax.axis_index("ctx"), reach, rows, *refs[:2], lat_ref)
     else:
-        lat_ref = refs[2]
-        window_rows(lax.axis_index("ctx"), reach, rows, *refs[:2], lat_ref)
+        lat_ref, before_ref, out_ref, held_ref, sems = refs
+        copies.append(pltpu.make_async_copy(before_ref, out_ref.at[:, : first * 128], sems.at[0]))
+        copies[0].start()
 
     factor = math.log2(math.e) / math.sqrt(NOPE + ROPE)
     lat = lat_ref[:, :LATENT]
@@ -438,41 +435,31 @@
     for h in hs:
         total = jnp.sum(w[h], axis=1, keepdims=True)
         held_ref[:, cols[h]] = (mm(w[h].astype(BF), vals[:, cols[h]]) / total).astype(BF)
-    copy = pltpu.make_async_copy(held_ref, out_ref.at[:, part], sem)
-    copy.start()
-    copy.wait()
-
-
-def mla(bias, q, ku, vu, blocks, previous, reach, first, count):
+    if not fresh:
+        copies.append(pltpu.make_async_copy(held_ref, out_ref.at[:, part], sems.at[1]))
+        copies[1].start()
+    for copy in copies:
+        copy.wait()
+
+
+def mla(bias, q, ku, vu, blocks, before, reach, first, count):
     rows = q.shape[0]
-    heads = ku.shape[1] // NOPE
     keys = (reach + 1) * rows
-    args = [bias, q, ku, vu, *blocks]
-    specs = [WHOLE] * len(args)
-    out = jax.ShapeDtypeStruct((rows, heads * 128), BF)
-    aliases = {}
-    if previous is not None:
-        aliases = {len(args): 0}
-        args.append(previous)
-        specs.append(FAR)
+    fresh = before is None
+    args = [bias, q, ku, vu, *blocks] + ([] if fresh else [before])
+    if fresh:
+        shapes = [(keys, LATENT + ROPE), (rows, count * 128)]
+        scratch = []
+    else:
+        shapes = [(rows, (first + count) * 128)]
+        scratch = [pltpu.VMEM((rows, count * 128), BF), pltpu.SemaphoreType.DMA((2,))]
     return pl.pallas_call(
-        functools.partial(
-            mla_kernel,
-            reach,
-            previous is None,
-            first,
-        ),
-        in_specs=specs,
-        out_specs=[WHOLE, FAR] if previous is None else FAR,
-        out_shape=[jax.ShapeDtypeStruct((keys, LATENT + ROPE), BF), out]
-        if previous is None
-        else out,
-        scratch_shapes=[
-            pltpu.VMEM((rows, count * 128), BF),
-            pltpu.SemaphoreType.DMA,
-        ],
-        input_output_aliases=aliases,
-        compiler_params=pltpu.CompilerParams(vmem_limit_bytes=VMEM),
+        functools.partial(mla_kernel, reach, fresh, first),
+        in_specs=[WHOLE] * len(args),
+        out_specs=[WHOLE if fresh else FAR] * len(shapes),
+        out_shape=[jax.ShapeDtypeStruct(shape, BF) for shape in shapes],
+        scratch_shapes=scratch,
+        compiler_params=pltpu.CompilerParams(vmem_limit_bytes=VMEM * max(1, keys // 1024)),
         cost_estimate=CHEAP,
         name="mla_heads",
     )(*args)
@@ -534,7 +521,6 @@
     for _ in range(rounds - 1):
         a, b = moved[-1]
         moved.append((swap(b, up), swap(a, middle)))
-    bias = mask(after(doc_lengths, qe_away), latents.shape[0], (reach + 1) * latents.shape[0])
     lat_own, lat_send = whole_call(
         pick_kernel,
         "pick_latents",
@@ -542,8 +528,9 @@
         [(rounds + 1, *lat.shape), (rounds, *lat.shape)],
     )
     lat_mate = swap(lat_send, mate)
-    mu_got = after(mu_got, bias, lat_own)
+    mu_got = after(mu_got, lat_own)
     pm, pu = whole_call(pair_kernel, "pair_join", [mu_own, mu_got], [shape, shape])
+    bias = mask(after(doc_lengths, pm), latents.shape[0], (reach + 1) * latents.shape[0])
 
     def attend(latent_blocks, previous, first, count):
         return mla(
@@ -560,19 +547,20 @@
 
     state = pu
     for step in range(rounds):
-        a, b = swap(state, up), swap(state, middle)
+        a, b = after((swap(state, up), swap(state, middle)), bias)
         if step < rounds - 1:
             (state,) = whole_call(step_kernel, "pair_step", [pm, pu, a, b], [shape])
     lat_own, _ = lax.optimization_barrier((lat_own, state))
-    window, mla_out = attend([lat_own, lat_mate], None, 0, heads // 2)
+    early_heads = heads * 3 // 8
+    window, mla_out = attend([lat_own, lat_mate], None, 0, early_heads)
     a, b, window = lax.optimization_barrier((a, b, window))
     s_own, s_send = whole_call(split_kernel, "slab_states", [mu_own, mu_got, a, b], [shape, shape])
     s_got = swap(s_send, mate)
     window, _ = lax.optimization_barrier((window, s_send))
-    mla_out = attend([window], mla_out, heads // 2, heads // 2)
-    out = final(0, qe_own, lo_own, s_own, heads, None)
+    (mla_out,) = attend([window], mla_out, early_heads, heads - early_heads)
+    out = final(qe_own, lo_own, s_own)
     s_got, mla_out = lax.optimization_barrier((s_got, mla_out))
-    kda_out = final(1, qe_away, lo_away, s_got, heads, out)
+    kda_out = final(qe_away, lo_away, s_got, out)
     return (kda_out, mla_out)
 
 

time: 44.7 us -> 43.1 us (0.964)
  waiting for transfers between devices: 10 us -> 8.16 us
  starting transfers between devices: 13.1 us -> 14.5 us
  Pallas kernels: 20.5 us -> 19.4 us
    ppermute x7, waiting for transfers between devices: 10 us -> 8.15 us  [swap(): return lax.ppermute(x, 'ctx', list(enumerate(table)))]
    ppermute x7, starting transfers between devices: 13 us -> 14.5 us  [swap(): return lax.ppermute(x, 'ctx', list(enumerate(table)))]
    pallas_call x4, Pallas kernels: 9.3 us -> 8.02 us  [the longest x2 6.85 us: mla(): pl.pallas_call(functools.partial(mla_kernel, reach, fresh, first), in_spe...]
  transfers between devices with their start and end apart: 11 -> 11, of which waited for: 6 -> 7; matrix products, arithmetic and copies ran while one was open for 0% -> 0% of each run, Pallas kernels for 34% -> 33%
where the time goes in v6:
time: 43.1 us; the launch traced here: 43 us
  Pallas kernels  19.4 us (45%)
  starting transfers between devices  14.5 us (34%)
  waiting for transfers between devices  8.16 us (19%)
  between operations  0.91 us (2%)
    ppermute x7, starting transfers between devices, swap(): return lax.ppermute(x, 'ctx', list(enumerate(table)))  14.5 us
    pallas_call x3, Pallas kernels, kda_call(): pl.pallas_call(kernel, in_specs=in_specs, out_specs=[WHOLE] * len(shapes)...  9.71 us
    ppermute x7, waiting for transfers between devices, swap(): return lax.ppermute(x, 'ctx', list(enumerate(table)))  8.15 us
    pallas_call x2, Pallas kernels, mla(): pl.pallas_call(functools.partial(mla_kernel, reach, fresh, first), in_spe...  6.85 us
    pallas_call x2, Pallas kernels, final(): pl.pallas_call(final_kernel, in_specs=[WHOLE] * len(args), out_specs=WHOL...  1.17 us
    pallas_call x4, Pallas kernels, whole_call(): pl.pallas_call(kernel, in_specs=[WHOLE] * len(args), out_specs=[WHOLE] *...  1.04 us
  transfers between devices with their start and end apart: 11, of which 7 were waited for; matrix products, arithmetic and copies ran while one was open for 0% of the time, Pallas kernels for 33%

profile of v6, /device:TPU:0, one launch (start us, length us, event | category | flops | bytes accessed | tf_op | source)
XLA Modules:
  0.0 43.0 jit_solution(13482655135019531195)
XLA Ops:
  0.6 0.0 copy-start.4
  0.6 0.0 copy-start.3
  0.7 3.7 %kda_slab.3 = (bf16[128,1024]{1,0:T(8,128)(2,1)S(1)}, bf16[128,1024]{1,0:T(8,128)(2,1)S(1)}, bf16[128,1024]{1,0:T(8,128)(2,1)S(1)}, bf16[128,1024]{1,0:T(8,128)(...) custom-call(bf16[128,2048]{1,0:T(8,128)(2,1)} %refs_0_.1, ...), custom_call_target="tpu_custom_call" | custom-call | tf_op jit(solution)/shard_map/kda_slab/pallas_call | solution.py:203
  4.4 3.0 %collective-permute-start.2 = (bf16[8,128,256]{2,1,0:T(8,128)(2,1)S(1)}, bf16[8,128,256]{2,1,0:T(8,128)(2,1)S(1)}, u32[]{:S(2)}, u32[]{:S(2)}) collective-permute-start(bf16[8,128,256]{2,1,0:T(8,128)(2,1)S(1)} %get-tuple-element.56), channel_id=1, source_target_pairs={{0,4},{4,0},{8,12},{12,8},{16,20},{20,16},{24,28},{28,24},{1,5},{5... | collective-permute-start | bytes 1572872 | tf_op jit(solution)/shard_map/ppermute | solution.py:481
  7.4 0.0 copy-done.3
  7.4 1.6 %collective-permute-start = (bf16[576,128]{1,0:T(8,128)(2,1)S(1)}, bf16[576,128]{1,0:T(8,128)(2,1)S(1)}, u32[]{:S(2)}, u32[]{:S(2)}) collective-permute-start(bf16[576,128]{1,0:T(8,128)(2,1)S(1)} %bitcast.2), channel_id=1, source_target_pairs={{0,8},{4,12},{8,0},{12,4},{16,24},{20,28},{24,16},{28,20},{1,9},{5... | collective-permute-start | bytes 442376 | tf_op jit(solution)/shard_map/ppermute | solution.py:481
  9.0 0.0 collective-permute-start.1
  9.0 0.0 copy-done.4
  9.0 0.0 copy-start.2
  9.0 3.1 %kda_slab.4 = (bf16[8,128,256]{2,1,0:T(8,128)(2,1)S(1)}, bf16[128,1024]{1,0:T(8,128)(2,1)S(1)}, f32[128,1024]{1,0:T(8,128)S(1)}) custom-call(bf16[128,1024]{1,0:T(8,128)(2,1)S(1)} %get-tuple-element.50.refs_0_, bf16[128,1024]{1,0:T(8,128)(2,1)S(1)} %get-tuple-element.51.refs_1_, bf16[128,1024]{1,0:T(8,128)(2,1)S(1)} %get-tuple-element.52.refs_2_, ...), custom_call_target="tpu_custom_call" | custom-call | tf_op jit(solution)/shard_map/kda_slab/pallas_call | solution.py:203
  12.1 0.6 %collective-permute-done.refs_0_ = bf16[576,128]{1,0:T(8,128)(2,1)S(1)} collective-permute-done((bf16[576,128]{1,0:T(8,128)(2,1)S(1)}, bf16[576,128]{1,0:T(8,128)(2,1)S(1)}, u32[]{:S(2)}, u32[]{:S(2)}) %collective-permute-start) | collective-permute-done | bytes 147488 | tf_op jit(solution)/shard_map/ppermute | solution.py:481
  12.7 0.0 collective-permute-done.1.refs_1_
  12.7 2.7 %collective-permute-start.3 = (bf16[576,128]{1,0:T(8,128)(2,1)S(1)}, bf16[576,128]{1,0:T(8,128)(2,1)S(1)}, u32[]{:S(2)}, u32[]{:S(2)}) collective-permute-start(bf16[576,128]{1,0:T(8,128)(2,1)S(1)} %collective-permute-done.1.refs_1_), channel_id=1, source_target_pairs={{0,8},{4,12},{8,0},{12,4},{16,24},{20,28},{24,16},{28,20},{1,9},{5... | collective-permute-start | bytes 442376 | tf_op jit(solution)/shard_map/ppermute | solution.py:481
  15.4 0.0 collective-permute-start.4
  15.4 0.0 copy-start
  15.4 0.0 copy-start.1
  15.4 2.9 %kda_slab.5 = (bf16[128,1024]{1,0:T(8,128)(2,1)S(1)}, f32[128,1024]{1,0:T(8,128)S(1)}) custom-call(bf16[128,1024]{1,0:T(8,128)(2,1)S(1)} %get-tuple-element.60.refs_0_, bf16[128,1024]{1,0:T(8,128)(2,1)S(1)} %get-tuple-element.61.refs_1_, bf16[128,1024]{1,0:T(8,128)(2,1)S(1)} %get-tuple-element.62.refs_2_, bf16[128,1024]{1,0:T(8,128)(2,1)S(1)} %get-tuple-element.63.refs_3_, ...), custom_call_target="tpu_custom_call" | custom-call | tf_op jit(solution)/shard_map/kda_slab/pallas_call | solution.py:203
  18.3 0.2 collective-permute-done.3.refs_2_
  18.5 0.0 collective-permute-done.4.refs_3_
  18.5 0.1 pick_latents.1
  18.6 0.7 %collective-permute-done.2.got_ref = bf16[8,128,256]{2,1,0:T(8,128)(2,1)S(1)} collective-permute-done((bf16[8,128,256]{2,1,0:T(8,128)(2,1)S(1)}, bf16[8,128,256]{2,1,0:T(8,128)(2,1)S(1)}, u32[]{:S(2)}, u32[]{:S(2)}) %collective-permute-start.2) | collective-permute-done | bytes 524320 | tf_op jit(solution)/shard_map/ppermute | solution.py:481
  19.3 0.3 pair_join.1
  19.6 1.9 %collective-permute-start.5 = (bf16[8,128,128]{2,1,0:T(8,128)(2,1)S(1)}, bf16[8,128,128]{2,1,0:T(8,128)(2,1)S(1)}, u32[]{:S(2)}, u32[]{:S(2)}) collective-permute-start(bf16[8,128,128]{2,1,0:T(8,128)(2,1)S(1)} %get-tuple-element.70.pu_ref), channel_id=1, source_target_pairs={{0,8},{4,12},{8,0},{12,4},{16,24},{20,28},{24,16},{28,20},{1,9},{5... | collective-permute-start | bytes 786440 | tf_op jit(solution)/shard_map/ppermute | solution.py:481
  21.5 0.0 collective-permute-start.6
  21.5 1.5 %collective-permute-start.9 = (bf16[2,576,128]{2,1,0:T(8,128)(2,1)S(1)}, bf16[2,576,128]{2,1,0:T(8,128)(2,1)S(1)}, u32[]{:S(2)}, u32[]{:S(2)}) collective-permute-start(bf16[2,576,128]{2,1,0:T(8,128)(2,1)S(1)} %get-tuple-element.77), channel_id=1, source_target_pairs={{0,4},{4,0},{8,12},{12,8},{16,20},{20,16},{24,28},{28,24},{1,5},{5... | collective-permute-start | bytes 884744 | tf_op jit(solution)/shard_map/ppermute | solution.py:481
  23.0 0.7 %window_mask.1.bias_ref = f32[128,640]{1,0:T(8,128)S(1)} custom-call(s32[8]{0:T(128)S(1)} %copy-done.4), custom_call_target="tpu_custom_call" | custom-call | tf_op jit(solution)/shard_map/window_mask/pallas_call | solution.py:393
  23.7 3.8 %collective-permute-done.5.a_ref = bf16[8,128,128]{2,1,0:T(8,128)(2,1)S(1)} collective-permute-done((bf16[8,128,128]{2,1,0:T(8,128)(2,1)S(1)}, bf16[8,128,128]{2,1,0:T(8,128)(2,1)S(1)}, u32[]{:S(2)}, u32[]{:S(2)}) %collective-permute-start.5) | collective-permute-done | bytes 262176 | tf_op jit(solution)/shard_map/ppermute | solution.py:481
  27.5 0.0 collective-permute-done.6.b_ref
  27.5 0.2 pair_step.1
  27.7 2.4 %collective-permute-start.7 = (bf16[8,128,128]{2,1,0:T(8,128)(2,1)S(1)}, bf16[8,128,128]{2,1,0:T(8,128)(2,1)S(1)}, u32[]{:S(2)}, u32[]{:S(2)}) collective-permute-start(bf16[8,128,128]{2,1,0:T(8,128)(2,1)S(1)} %pair_step.1), channel_id=1, source_target_pairs={{0,8},{4,12},{8,0},{12,4},{16,24},{20,28},{24,16},{28,20},{1,9},{5... | collective-permute-start | bytes 786440 | tf_op jit(solution)/shard_map/ppermute | solution.py:481
  30.1 0.0 collective-permute-start.8
  30.1 0.8 %collective-permute-done.9.refs_1_ = bf16[2,576,128]{2,1,0:T(8,128)(2,1)S(1)} collective-permute-done((bf16[2,576,128]{2,1,0:T(8,128)(2,1)S(1)}, bf16[2,576,128]{2,1,0:T(8,128)(2,1)S(1)}, u32[]{:S(2)}, u32[]{:S(2)}) %collective-permute-start.9) | collective-permute-done | bytes 294944 | tf_op jit(solution)/shard_map/ppermute | solution.py:481
  30.9 0.0 copy-done.2
  30.9 0.0 copy-done
  30.9 0.0 copy-done.1
  30.9 2.5 %mla_heads.2 = (bf16[640,576]{1,0:T(8,128)(2,1)S(1)}, bf16[128,768]{1,0:T(8,128)(2,1)S(1)}) custom-call(f32[128,640]{1,0:T(8,128)S(1)} %window_mask.1.bias_ref, bf16[128,3072]{1,0:T(8,128)(2,1)S(1)} %copy-done.2, bf16[512,2048]{1,0:T(8,128)(2,1)S(1)} %copy-done, bf16[512,2048]{1,0:T(8,128)(2,1)S(1)} %copy-done.1, ...), custom_call_target="tpu_custom_call" | custom-call | tf_op jit(solution)/shard_map/mla_heads/pallas_call | solution.py:456
  33.4 1.3 %collective-permute-done.7.a_ref = bf16[8,128,128]{2,1,0:T(8,128)(2,1)S(1)} collective-permute-done((bf16[8,128,128]{2,1,0:T(8,128)(2,1)S(1)}, bf16[8,128,128]{2,1,0:T(8,128)(2,1)S(1)}, u32[]{:S(2)}, u32[]{:S(2)}) %collective-permute-start.7) | collective-permute-done | bytes 262176 | tf_op jit(solution)/shard_map/ppermute | solution.py:481
  34.7 0.0 collective-permute-done.8.b_ref
  34.7 0.4 %slab_states.1 = (bf16[8,128,128]{2,1,0:T(8,128)(2,1)S(1)}, bf16[8,128,128]{2,1,0:T(8,128)(2,1)S(1)}) custom-call(bf16[8,128,256]{2,1,0:T(8,128)(2,1)S(1)} %get-tuple-element.55.own_ref, bf16[8,128,256]{2,1,0:T(8,128)(2,1)S(1)} %collective-permute-done.2.got_ref, bf16[8,128,128]{2,1,0:T(8,128)(2,1)S(1)} %collective-permute-done.7.a_ref, ...), custom_call_target="tpu_custom_call" | custom-call | tf_op jit(solution)/shard_map/slab_states/pallas_call | solution.py:296
  35.1 1.4 %collective-permute-start.10 = (bf16[8,128,128]{2,1,0:T(8,128)(2,1)S(1)}, bf16[8,128,128]{2,1,0:T(8,128)(2,1)S(1)}, u32[]{:S(2)}, u32[]{:S(2)}) collective-permute-start(bf16[8,128,128]{2,1,0:T(8,128)(2,1)S(1)} %get-tuple-element.81), channel_id=1, source_target_pairs={{0,4},{4,0},{8,12},{12,8},{16,20},{20,16},{24,28},{28,24},{1,5},{5... | collective-permute-start | bytes 786440 | tf_op jit(solution)/shard_map/ppermute | solution.py:481
  36.6 4.4 %mla_heads.3 = bf16[128,2048]{1,0:T(8,128)(2,1)} custom-call(f32[128,640]{1,0:T(8,128)S(1)} %window_mask.1.bias_ref, bf16[128,3072]{1,0:T(8,128)(2,1)S(1)} %copy-done.2, bf16[512,2048]{1,0:T(8,128)(2,1)S(1)} %copy-done, bf16[512,2048]{1,0:T(8,128)(2,1)S(1)} %copy-done.1, bf16[640,576]{1,0:T(8,128)(2,1)S(1)} %get-tuple-element.83.refs_0_, ...), custom_call_target="tpu_custom_call" | custom-call | tf_op jit(solution)/shard_map/mla_heads/pallas_call | solution.py:456
  41.0 0.2 kda_out.2.refs_0_
  41.2 0.7 %collective-permute-done.10.s_ref = bf16[8,128,128]{2,1,0:T(8,128)(2,1)S(1)} collective-permute-done((bf16[8,128,128]{2,1,0:T(8,128)(2,1)S(1)}, bf16[8,128,128]{2,1,0:T(8,128)(2,1)S(1)}, u32[]{:S(2)}, u32[]{:S(2)}) %collective-permute-start.10) | collective-permute-done | bytes 262176 | tf_op jit(solution)/shard_map/ppermute | solution.py:481
  41.9 0.9 %kda_out.3 = bf16[128,2048]{1,0:T(8,128)(2,1)} custom-call(bf16[128,1024]{1,0:T(8,128)(2,1)S(1)} %get-tuple-element.64.qe_ref, f32[128,1024]{1,0:T(8,128)S(1)} %get-tuple-element.65.lo_ref, bf16[8,128,128]{2,1,0:T(8,128)(2,1)S(1)} %collective-permute-done.10.s_ref, bf16[128,1024]{1,0:T(8,128)(2,1)S(1)} %kda_out.2.refs_0_), custom_call_target="tpu_custom_call" | custom-call | tf_op jit(solution)/shard_map/kda_out/pallas_call | solution.py:335
Async XLA Ops:
  0.6 8.3 %copy-start.4 = (s32[8]{0:T(128)S(1)}, s32[8]{0:T(128)}, u32[]{:S(2)}) copy-start(s32[8]{0:T(128)} %lengths) | copy-start | bytes 100
  0.6 6.7 %copy-start.3 = (bf16[128,576]{0,1:T(8,128)(2,1)S(1)}, bf16[128,576]{0,1:T(8,128)(2,1)}, u32[]{:S(2)}) copy-start(bf16[128,576]{0,1:T(8,128)(2,1)} %param.16) | copy-start | bytes 442372
  4.4 14.9 %collective-permute-start.2 = (bf16[8,128,256]{2,1,0:T(8,128)(2,1)S(1)}, bf16[8,128,256]{2,1,0:T(8,128)(2,1)S(1)}, u32[]{:S(2)}, u32[]{:S(2)}) collective-permute-start(bf16[8,128,256]{2,1,0:T(8,128)(2,1)S(1)} %get-tuple-element.56), channel_id=1, source_target_pairs={{0,4},{4,0},{8,12},{12,8},{16,20},{20,16},{24,28},{28,24},{1,5},{5... | collective-permute-start | bytes 1572872 | tf_op jit(solution)/shard_map/ppermute | solution.py:481
  7.4 5.3 %collective-permute-start = (bf16[576,128]{1,0:T(8,128)(2,1)S(1)}, bf16[576,128]{1,0:T(8,128)(2,1)S(1)}, u32[]{:S(2)}, u32[]{:S(2)}) collective-permute-start(bf16[576,128]{1,0:T(8,128)(2,1)S(1)} %bitcast.2), channel_id=1, source_target_pairs={{0,8},{4,12},{8,0},{12,4},{16,24},{20,28},{24,16},{28,20},{1,9},{5... | collective-permute-start | bytes 442376 | tf_op jit(solution)/shard_map/ppermute | solution.py:481
  9.0 3.7 %collective-permute-start.1 = (bf16[576,128]{1,0:T(8,128)(2,1)S(1)}, bf16[576,128]{1,0:T(8,128)(2,1)S(1)}, u32[]{:S(2)}, u32[]{:S(2)}) collective-permute-start(bf16[576,128]{1,0:T(8,128)(2,1)S(1)} %bitcast.3), channel_id=1, source_target_pairs={{0,1},{1,0},{2,3},{3,2},{4,5},{5,4},{6,7},{7,6},{8,16},{9,17},{10,... | collective-permute-start | bytes 442376 | tf_op jit(solution)/shard_map/ppermute | solution.py:486
  9.0 21.9 %copy-start.2 = (bf16[128,3072]{1,0:T(8,128)(2,1)S(1)}, bf16[128,3072]{1,0:T(8,128)(2,1)}, u32[]{:S(2)}) copy-start(bf16[128,3072]{1,0:T(8,128)(2,1)} %q_ref.3) | copy-start | bytes 2359300
  12.7 5.8 %collective-permute-start.3 = (bf16[576,128]{1,0:T(8,128)(2,1)S(1)}, bf16[576,128]{1,0:T(8,128)(2,1)S(1)}, u32[]{:S(2)}, u32[]{:S(2)}) collective-permute-start(bf16[576,128]{1,0:T(8,128)(2,1)S(1)} %collective-permute-done.1.refs_1_), channel_id=1, source_target_pairs={{0,8},{4,12},{8,0},{12,4},{16,24},{20,28},{24,16},{28,20},{1,9},{5... | collective-permute-start | bytes 442376 | tf_op jit(solution)/shard_map/ppermute | solution.py:481
  15.4 3.1 %collective-permute-start.4 = (bf16[576,128]{1,0:T(8,128)(2,1)S(1)}, bf16[576,128]{1,0:T(8,128)(2,1)S(1)}, u32[]{:S(2)}, u32[]{:S(2)}) collective-permute-start(bf16[576,128]{1,0:T(8,128)(2,1)S(1)} %collective-permute-done.refs_0_), channel_id=1, source_target_pairs={{0,1},{1,0},{2,3},{3,2},{4,5},{5,4},{6,7},{7,6},{8,16},{9,17},{10,... | collective-permute-start | bytes 442376 | tf_op jit(solution)/shard_map/ppermute | solution.py:486
  15.4 15.5 %copy-start = (bf16[512,2048]{1,0:T(8,128)(2,1)S(1)}, bf16[512,2048]{1,0:T(8,128)(2,1)}, u32[]{:S(2)}) copy-start(bf16[512,2048]{1,0:T(8,128)(2,1)} %ku_ref.3) | copy-start | bytes 6291460
  15.4 15.5 %copy-start.1 = (bf16[512,2048]{1,0:T(8,128)(2,1)S(1)}, bf16[512,2048]{1,0:T(8,128)(2,1)}, u32[]{:S(2)}) copy-start(bf16[512,2048]{1,0:T(8,128)(2,1)} %vu_ref.3) | copy-start | bytes 6291460
  19.6 7.9 %collective-permute-start.5 = (bf16[8,128,128]{2,1,0:T(8,128)(2,1)S(1)}, bf16[8,128,128]{2,1,0:T(8,128)(2,1)S(1)}, u32[]{:S(2)}, u32[]{:S(2)}) collective-permute-start(bf16[8,128,128]{2,1,0:T(8,128)(2,1)S(1)} %get-tuple-element.70.pu_ref), channel_id=1, source_target_pairs={{0,8},{4,12},{8,0},{12,4},{16,24},{20,28},{24,16},{28,20},{1,9},{5... | collective-permute-start | bytes 786440 | tf_op jit(solution)/shard_map/ppermute | solution.py:481
  21.5 6.0 %collective-permute-start.6 = (bf16[8,128,128]{2,1,0:T(8,128)(2,1)S(1)}, bf16[8,128,128]{2,1,0:T(8,128)(2,1)S(1)}, u32[]{:S(2)}, u32[]{:S(2)}) collective-permute-start(bf16[8,128,128]{2,1,0:T(8,128)(2,1)S(1)} %get-tuple-element.70.pu_ref), channel_id=1, source_target_pairs={{0,1},{1,0},{2,3},{3,2},{4,5},{5,4},{6,7},{7,6},{8,16},{9,17},{10,... | collective-permute-start | bytes 786440 | tf_op jit(solution)/shard_map/ppermute | solution.py:486
  21.5 9.4 %collective-permute-start.9 = (bf16[2,576,128]{2,1,0:T(8,128)(2,1)S(1)}, bf16[2,576,128]{2,1,0:T(8,128)(2,1)S(1)}, u32[]{:S(2)}, u32[]{:S(2)}) collective-permute-start(bf16[2,576,128]{2,1,0:T(8,128)(2,1)S(1)} %get-tuple-element.77), channel_id=1, source_target_pairs={{0,4},{4,0},{8,12},{12,8},{16,20},{20,16},{24,28},{28,24},{1,5},{5... | collective-permute-start | bytes 884744 | tf_op jit(solution)/shard_map/ppermute | solution.py:481
  27.7 7.0 %collective-permute-start.7 = (bf16[8,128,128]{2,1,0:T(8,128)(2,1)S(1)}, bf16[8,128,128]{2,1,0:T(8,128)(2,1)S(1)}, u32[]{:S(2)}, u32[]{:S(2)}) collective-permute-start(bf16[8,128,128]{2,1,0:T(8,128)(2,1)S(1)} %pair_step.1), channel_id=1, source_target_pairs={{0,8},{4,12},{8,0},{12,4},{16,24},{20,28},{24,16},{28,20},{1,9},{5... | collective-permute-start | bytes 786440 | tf_op jit(solution)/shard_map/ppermute | solution.py:481
  30.1 4.6 %collective-permute-start.8 = (bf16[8,128,128]{2,1,0:T(8,128)(2,1)S(1)}, bf16[8,128,128]{2,1,0:T(8,128)(2,1)S(1)}, u32[]{:S(2)}, u32[]{:S(2)}) collective-permute-start(bf16[8,128,128]{2,1,0:T(8,128)(2,1)S(1)} %pair_step.1), channel_id=1, source_target_pairs={{0,1},{1,0},{2,3},{3,2},{4,5},{5,4},{6,7},{7,6},{8,16},{9,17},{10,... | collective-permute-start | bytes 786440 | tf_op jit(solution)/shard_map/ppermute | solution.py:486
  35.1 6.7 %collective-permute-start.10 = (bf16[8,128,128]{2,1,0:T(8,128)(2,1)S(1)}, bf16[8,128,128]{2,1,0:T(8,128)(2,1)S(1)}, u32[]{:S(2)}, u32[]{:S(2)}) collective-permute-start(bf16[8,128,128]{2,1,0:T(8,128)(2,1)S(1)} %get-tuple-element.81), channel_id=1, source_target_pairs={{0,4},{4,0},{8,12},{12,8},{16,20},{20,16},{24,28},{28,24},{1,5},{5... | collective-permute-start | bytes 786440 | tf_op jit(solution)/shard_map/ppermute | solution.py:481

commit v7 on v6

--- a/solution.py
+++ b/solution.py
@@ -262,34 +262,56 @@
         go(got_ref, own_ref)
 
 
-def arrived(place, a_ref, b_ref, h):
-    x = jnp.where((place // 2) % 2 == 1, a_ref[h].astype(F32), b_ref[h].astype(F32))
-    return jnp.where(place < 2, 0.0, x).astype(BF)
+def on_arrival(a_ref, b_ref, body):
+    pair = lax.axis_index("ctx") // 2
+
+    @pl.when(pair == 0)
+    def _():
+        body(None)
+
+    @pl.when(pair % 2 == 1)
+    def _():
+        body(a_ref)
+
+    @pl.when((pair % 2 == 0) & (pair > 0))
+    def _():
+        body(b_ref)
 
 
 def step_kernel(pm_ref, pu_ref, a_ref, b_ref, out_ref):
-    place = lax.axis_index("ctx")
-    for h in range(pm_ref.shape[0]):
-        x = arrived(place, a_ref, b_ref, h)
-        out_ref[h] = (mm(pm_ref[h], x) + pu_ref[h].astype(F32)).astype(BF)
+    def body(x_ref):
+        for h in range(pm_ref.shape[0]):
+            if x_ref is None:
+                out_ref[h] = pu_ref[h]
+            else:
+                out_ref[h] = (mm(pm_ref[h], x_ref[h]) + pu_ref[h].astype(F32)).astype(BF)
+
+    on_arrival(a_ref, b_ref, body)
 
 
 def split_kernel(own_ref, got_ref, a_ref, b_ref, mine_ref, send_ref):
-    place = lax.axis_index("ctx")
-
-    def go(mu_ref, plain_ref, moved_ref):
+    def go(x_ref, mu_ref, plain_ref, moved_ref):
         for h in range(own_ref.shape[0]):
-            x = arrived(place, a_ref, b_ref, h)
-            plain_ref[h] = x
-            moved_ref[h] = (mm(mu_ref[h, :, :128], x) + mu_ref[h, :, 128:].astype(F32)).astype(BF)
-
-    @pl.when(place % 2 == 0)
-    def _():
-        go(own_ref, mine_ref, send_ref)
-
-    @pl.when(place % 2 == 1)
-    def _():
-        go(got_ref, send_ref, mine_ref)
+            u = mu_ref[h, :, 128:]
+            if x_ref is None:
+                plain_ref[h] = jnp.zeros_like(u)
+                moved_ref[h] = u
+            else:
+                plain_ref[h] = x_ref[h]
+                moved_ref[h] = (mm(mu_ref[h, :, :128], x_ref[h]) + u.astype(F32)).astype(BF)
+
+    def body(x_ref):
+        place = lax.axis_index("ctx")
+
+        @pl.when(place % 2 == 0)
+        def _():
+            go(x_ref, own_ref, mine_ref, send_ref)
+
+        @pl.when(place % 2 == 1)
+        def _():
+            go(x_ref, got_ref, send_ref, mine_ref)
+
+    on_arrival(a_ref, b_ref, body)
 
 
 def whole_call(kernel, name, args, outs):

time: 43.1 us -> 43 us (level)
  transfers between devices with their start and end apart: 11 -> 11, of which waited for: 7 -> 7; matrix products, arithmetic and copies ran while one was open for 0% -> 0% of each run, Pallas kernels for 33% -> 32%
where the time goes in v7:
time: 43 us; the launch traced here: 42.8 us
  Pallas kernels  19.1 us (44%)
  starting transfers between devices  14.8 us (34%)
  waiting for transfers between devices  8.06 us (19%)
  between operations  0.91 us (2%)
    ppermute x7, starting transfers between devices, swap(): return lax.ppermute(x, 'ctx', list(enumerate(table)))  14.8 us
    pallas_call x3, Pallas kernels, kda_call(): pl.pallas_call(kernel, in_specs=in_specs, out_specs=[WHOLE] * len(shapes)...  9.71 us
    ppermute x7, waiting for transfers between devices, swap(): return lax.ppermute(x, 'ctx', list(enumerate(table)))  8.05 us
    pallas_call x2, Pallas kernels, mla(): pl.pallas_call(functools.partial(mla_kernel, reach, fresh, first), in_spe...  6.85 us
    pallas_call x2, Pallas kernels, final(): pl.pallas_call(final_kernel, in_specs=[WHOLE] * len(args), out_specs=WHOL...  1.17 us
  transfers between devices with their start and end apart: 11, of which 7 were waited for; matrix products, arithmetic and copies ran while one was open for 0% of the time, Pallas kernels for 32%

profile of v7, /device:TPU:0, one launch (start us, length us, event | category | flops | bytes accessed | tf_op | source)
XLA Modules:
  0.0 42.8 jit_solution(8666764741143420036)
XLA Ops:
  0.6 0.0 copy-start.4
  0.6 0.0 copy-start.3
  0.7 3.7 %kda_slab.3 = (bf16[128,1024]{1,0:T(8,128)(2,1)S(1)}, bf16[128,1024]{1,0:T(8,128)(2,1)S(1)}, bf16[128,1024]{1,0:T(8,128)(2,1)S(1)}, bf16[128,1024]{1,0:T(8,128)(...) custom-call(bf16[128,2048]{1,0:T(8,128)(2,1)} %refs_0_.1, ...), custom_call_target="tpu_custom_call" | custom-call | tf_op jit(solution)/shard_map/kda_slab/pallas_call | solution.py:203
  4.4 3.0 %collective-permute-start.2 = (bf16[8,128,256]{2,1,0:T(8,128)(2,1)S(1)}, bf16[8,128,256]{2,1,0:T(8,128)(2,1)S(1)}, u32[]{:S(2)}, u32[]{:S(2)}) collective-permute-start(bf16[8,128,256]{2,1,0:T(8,128)(2,1)S(1)} %get-tuple-element.56), channel_id=1, source_target_pairs={{0,4},{4,0},{8,12},{12,8},{16,20},{20,16},{24,28},{28,24},{1,5},{5... | collective-permute-start | bytes 1572872 | tf_op jit(solution)/shard_map/ppermute | solution.py:503
  7.4 0.0 copy-done.3
  7.4 1.6 %collective-permute-start = (bf16[576,128]{1,0:T(8,128)(2,1)S(1)}, bf16[576,128]{1,0:T(8,128)(2,1)S(1)}, u32[]{:S(2)}, u32[]{:S(2)}) collective-permute-start(bf16[576,128]{1,0:T(8,128)(2,1)S(1)} %bitcast.2), channel_id=1, source_target_pairs={{0,8},{4,12},{8,0},{12,4},{16,24},{20,28},{24,16},{28,20},{1,9},{5... | collective-permute-start | bytes 442376 | tf_op jit(solution)/shard_map/ppermute | solution.py:503
  9.0 0.0 collective-permute-start.1
  9.0 0.0 copy-done.4
  9.0 0.0 copy-start.2
  9.0 3.1 %kda_slab.4 = (bf16[8,128,256]{2,1,0:T(8,128)(2,1)S(1)}, bf16[128,1024]{1,0:T(8,128)(2,1)S(1)}, f32[128,1024]{1,0:T(8,128)S(1)}) custom-call(bf16[128,1024]{1,0:T(8,128)(2,1)S(1)} %get-tuple-element.50.refs_0_, bf16[128,1024]{1,0:T(8,128)(2,1)S(1)} %get-tuple-element.51.refs_1_, bf16[128,1024]{1,0:T(8,128)(2,1)S(1)} %get-tuple-element.52.refs_2_, ...), custom_call_target="tpu_custom_call" | custom-call | tf_op jit(solution)/shard_map/kda_slab/pallas_call | solution.py:203
  12.1 0.6 %collective-permute-done.refs_0_ = bf16[576,128]{1,0:T(8,128)(2,1)S(1)} collective-permute-done((bf16[576,128]{1,0:T(8,128)(2,1)S(1)}, bf16[576,128]{1,0:T(8,128)(2,1)S(1)}, u32[]{:S(2)}, u32[]{:S(2)}) %collective-permute-start) | collective-permute-done | bytes 147488 | tf_op jit(solution)/shard_map/ppermute | solution.py:503
  12.7 0.0 collective-permute-done.1.refs_1_
  12.7 2.7 %collective-permute-start.3 = (bf16[576,128]{1,0:T(8,128)(2,1)S(1)}, bf16[576,128]{1,0:T(8,128)(2,1)S(1)}, u32[]{:S(2)}, u32[]{:S(2)}) collective-permute-start(bf16[576,128]{1,0:T(8,128)(2,1)S(1)} %collective-permute-done.1.refs_1_), channel_id=1, source_target_pairs={{0,8},{4,12},{8,0},{12,4},{16,24},{20,28},{24,16},{28,20},{1,9},{5... | collective-permute-start | bytes 442376 | tf_op jit(solution)/shard_map/ppermute | solution.py:503
  15.4 0.0 collective-permute-start.4
  15.4 0.0 copy-start
  15.4 0.0 copy-start.1
  15.4 2.9 %kda_slab.5 = (bf16[128,1024]{1,0:T(8,128)(2,1)S(1)}, f32[128,1024]{1,0:T(8,128)S(1)}) custom-call(bf16[128,1024]{1,0:T(8,128)(2,1)S(1)} %get-tuple-element.60.refs_0_, bf16[128,1024]{1,0:T(8,128)(2,1)S(1)} %get-tuple-element.61.refs_1_, bf16[128,1024]{1,0:T(8,128)(2,1)S(1)} %get-tuple-element.62.refs_2_, bf16[128,1024]{1,0:T(8,128)(2,1)S(1)} %get-tuple-element.63.refs_3_, ...), custom_call_target="tpu_custom_call" | custom-call | tf_op jit(solution)/shard_map/kda_slab/pallas_call | solution.py:203
  18.3 0.2 collective-permute-done.3.refs_2_
  18.5 0.0 collective-permute-done.4.refs_3_
  18.5 0.1 pick_latents.1
  18.6 0.7 %collective-permute-done.2.got_ref = bf16[8,128,256]{2,1,0:T(8,128)(2,1)S(1)} collective-permute-done((bf16[8,128,256]{2,1,0:T(8,128)(2,1)S(1)}, bf16[8,128,256]{2,1,0:T(8,128)(2,1)S(1)}, u32[]{:S(2)}, u32[]{:S(2)}) %collective-permute-start.2) | collective-permute-done | bytes 524320 | tf_op jit(solution)/shard_map/ppermute | solution.py:503
  19.3 0.3 pair_join.1
  19.6 1.9 %collective-permute-start.5 = (bf16[8,128,128]{2,1,0:T(8,128)(2,1)S(1)}, bf16[8,128,128]{2,1,0:T(8,128)(2,1)S(1)}, u32[]{:S(2)}, u32[]{:S(2)}) collective-permute-start(bf16[8,128,128]{2,1,0:T(8,128)(2,1)S(1)} %get-tuple-element.70.pu_ref), channel_id=1, source_target_pairs={{0,8},{4,12},{8,0},{12,4},{16,24},{20,28},{24,16},{28,20},{1,9},{5... | collective-permute-start | bytes 786440 | tf_op jit(solution)/shard_map/ppermute | solution.py:503
  21.5 0.0 collective-permute-start.6
  21.5 1.5 %collective-permute-start.9 = (bf16[2,576,128]{2,1,0:T(8,128)(2,1)S(1)}, bf16[2,576,128]{2,1,0:T(8,128)(2,1)S(1)}, u32[]{:S(2)}, u32[]{:S(2)}) collective-permute-start(bf16[2,576,128]{2,1,0:T(8,128)(2,1)S(1)} %get-tuple-element.77), channel_id=1, source_target_pairs={{0,4},{4,0},{8,12},{12,8},{16,20},{20,16},{24,28},{28,24},{1,5},{5... | collective-permute-start | bytes 884744 | tf_op jit(solution)/shard_map/ppermute | solution.py:503
  23.0 0.7 %window_mask.1.bias_ref = f32[128,640]{1,0:T(8,128)S(1)} custom-call(s32[8]{0:T(128)S(1)} %copy-done.4), custom_call_target="tpu_custom_call" | custom-call | tf_op jit(solution)/shard_map/window_mask/pallas_call | solution.py:415
  23.7 3.8 %collective-permute-done.5.a_ref = bf16[8,128,128]{2,1,0:T(8,128)(2,1)S(1)} collective-permute-done((bf16[8,128,128]{2,1,0:T(8,128)(2,1)S(1)}, bf16[8,128,128]{2,1,0:T(8,128)(2,1)S(1)}, u32[]{:S(2)}, u32[]{:S(2)}) %collective-permute-start.5) | collective-permute-done | bytes 262176 | tf_op jit(solution)/shard_map/ppermute | solution.py:503
  27.5 0.0 collective-permute-done.6.b_ref
  27.5 2.6 %collective-permute-start.7 = (bf16[8,128,128]{2,1,0:T(8,128)(2,1)S(1)}, bf16[8,128,128]{2,1,0:T(8,128)(2,1)S(1)}, u32[]{:S(2)}, u32[]{:S(2)}) collective-permute-start(bf16[8,128,128]{2,1,0:T(8,128)(2,1)S(1)} %pair_step.1), channel_id=1, source_target_pairs={{0,8},{4,12},{8,0},{12,4},{16,24},{20,28},{24,16},{28,20},{1,9},{5... | collective-permute-start | bytes 786440 | tf_op jit(solution)/shard_map/ppermute | solution.py:503
  30.1 0.0 collective-permute-start.8
  30.1 0.8 %collective-permute-done.9.refs_1_ = bf16[2,576,128]{2,1,0:T(8,128)(2,1)S(1)} collective-permute-done((bf16[2,576,128]{2,1,0:T(8,128)(2,1)S(1)}, bf16[2,576,128]{2,1,0:T(8,128)(2,1)S(1)}, u32[]{:S(2)}, u32[]{:S(2)}) %collective-permute-start.9) | collective-permute-done | bytes 294944 | tf_op jit(solution)/shard_map/ppermute | solution.py:503
  30.9 0.0 copy-done.2
  30.9 0.0 copy-done
  30.9 0.0 copy-done.1
  30.9 2.5 %mla_heads.2 = (bf16[640,576]{1,0:T(8,128)(2,1)S(1)}, bf16[128,768]{1,0:T(8,128)(2,1)S(1)}) custom-call(f32[128,640]{1,0:T(8,128)S(1)} %window_mask.1.bias_ref, bf16[128,3072]{1,0:T(8,128)(2,1)S(1)} %copy-done.2, bf16[512,2048]{1,0:T(8,128)(2,1)S(1)} %copy-done, bf16[512,2048]{1,0:T(8,128)(2,1)S(1)} %copy-done.1, ...), custom_call_target="tpu_custom_call" | custom-call | tf_op jit(solution)/shard_map/mla_heads/pallas_call | solution.py:478
  33.4 1.2 %collective-permute-done.7.a_ref = bf16[8,128,128]{2,1,0:T(8,128)(2,1)S(1)} collective-permute-done((bf16[8,128,128]{2,1,0:T(8,128)(2,1)S(1)}, bf16[8,128,128]{2,1,0:T(8,128)(2,1)S(1)}, u32[]{:S(2)}, u32[]{:S(2)}) %collective-permute-start.7) | collective-permute-done | bytes 262176 | tf_op jit(solution)/shard_map/ppermute | solution.py:503
  34.6 0.0 collective-permute-done.8.b_ref
  34.6 0.3 slab_states.1
  34.9 1.5 %collective-permute-start.10 = (bf16[8,128,128]{2,1,0:T(8,128)(2,1)S(1)}, bf16[8,128,128]{2,1,0:T(8,128)(2,1)S(1)}, u32[]{:S(2)}, u32[]{:S(2)}) collective-permute-start(bf16[8,128,128]{2,1,0:T(8,128)(2,1)S(1)} %get-tuple-element.81), channel_id=1, source_target_pairs={{0,4},{4,0},{8,12},{12,8},{16,20},{20,16},{24,28},{28,24},{1,5},{5... | collective-permute-start | bytes 786440 | tf_op jit(solution)/shard_map/ppermute | solution.py:503
  36.4 4.4 %mla_heads.3 = bf16[128,2048]{1,0:T(8,128)(2,1)} custom-call(f32[128,640]{1,0:T(8,128)S(1)} %window_mask.1.bias_ref, bf16[128,3072]{1,0:T(8,128)(2,1)S(1)} %copy-done.2, bf16[512,2048]{1,0:T(8,128)(2,1)S(1)} %copy-done, bf16[512,2048]{1,0:T(8,128)(2,1)S(1)} %copy-done.1, bf16[640,576]{1,0:T(8,128)(2,1)S(1)} %get-tuple-element.83.refs_0_, ...), custom_call_target="tpu_custom_call" | custom-call | tf_op jit(solution)/shard_map/mla_heads/pallas_call | solution.py:478
  40.8 0.2 kda_out.2.refs_0_
  41.0 0.7 %collective-permute-done.10.s_ref = bf16[8,128,128]{2,1,0:T(8,128)(2,1)S(1)} collective-permute-done((bf16[8,128,128]{2,1,0:T(8,128)(2,1)S(1)}, bf16[8,128,128]{2,1,0:T(8,128)(2,1)S(1)}, u32[]{:S(2)}, u32[]{:S(2)}) %collective-permute-start.10) | collective-permute-done | bytes 262176 | tf_op jit(solution)/shard_map/ppermute | solution.py:503
  41.7 0.9 %kda_out.3 = bf16[128,2048]{1,0:T(8,128)(2,1)} custom-call(bf16[128,1024]{1,0:T(8,128)(2,1)S(1)} %get-tuple-element.64.qe_ref, f32[128,1024]{1,0:T(8,128)S(1)} %get-tuple-element.65.lo_ref, bf16[8,128,128]{2,1,0:T(8,128)(2,1)S(1)} %collective-permute-done.10.s_ref, bf16[128,1024]{1,0:T(8,128)(2,1)S(1)} %kda_out.2.refs_0_), custom_call_target="tpu_custom_call" | custom-call | tf_op jit(solution)/shard_map/kda_out/pallas_call | solution.py:357
  (1 shorter events, 0.0 us)
Async XLA Ops:
  0.6 8.3 %copy-start.4 = (s32[8]{0:T(128)S(1)}, s32[8]{0:T(128)}, u32[]{:S(2)}) copy-start(s32[8]{0:T(128)} %lengths) | copy-start | bytes 100
  0.6 6.7 %copy-start.3 = (bf16[128,576]{0,1:T(8,128)(2,1)S(1)}, bf16[128,576]{0,1:T(8,128)(2,1)}, u32[]{:S(2)}) copy-start(bf16[128,576]{0,1:T(8,128)(2,1)} %param.16) | copy-start | bytes 442372
  4.4 14.9 %collective-permute-start.2 = (bf16[8,128,256]{2,1,0:T(8,128)(2,1)S(1)}, bf16[8,128,256]{2,1,0:T(8,128)(2,1)S(1)}, u32[]{:S(2)}, u32[]{:S(2)}) collective-permute-start(bf16[8,128,256]{2,1,0:T(8,128)(2,1)S(1)} %get-tuple-element.56), channel_id=1, source_target_pairs={{0,4},{4,0},{8,12},{12,8},{16,20},{20,16},{24,28},{28,24},{1,5},{5... | collective-permute-start | bytes 1572872 | tf_op jit(solution)/shard_map/ppermute | solution.py:503
  7.4 5.3 %collective-permute-start = (bf16[576,128]{1,0:T(8,128)(2,1)S(1)}, bf16[576,128]{1,0:T(8,128)(2,1)S(1)}, u32[]{:S(2)}, u32[]{:S(2)}) collective-permute-start(bf16[576,128]{1,0:T(8,128)(2,1)S(1)} %bitcast.2), channel_id=1, source_target_pairs={{0,8},{4,12},{8,0},{12,4},{16,24},{20,28},{24,16},{28,20},{1,9},{5... | collective-permute-start | bytes 442376 | tf_op jit(solution)/shard_map/ppermute | solution.py:503
  9.0 3.7 %collective-permute-start.1 = (bf16[576,128]{1,0:T(8,128)(2,1)S(1)}, bf16[576,128]{1,0:T(8,128)(2,1)S(1)}, u32[]{:S(2)}, u32[]{:S(2)}) collective-permute-start(bf16[576,128]{1,0:T(8,128)(2,1)S(1)} %bitcast.3), channel_id=1, source_target_pairs={{0,1},{1,0},{2,3},{3,2},{4,5},{5,4},{6,7},{7,6},{8,16},{9,17},{10,... | collective-permute-start | bytes 442376 | tf_op jit(solution)/shard_map/ppermute | solution.py:508
  9.0 21.9 %copy-start.2 = (bf16[128,3072]{1,0:T(8,128)(2,1)S(1)}, bf16[128,3072]{1,0:T(8,128)(2,1)}, u32[]{:S(2)}) copy-start(bf16[128,3072]{1,0:T(8,128)(2,1)} %q_ref.3) | copy-start | bytes 2359300
  12.7 5.8 %collective-permute-start.3 = (bf16[576,128]{1,0:T(8,128)(2,1)S(1)}, bf16[576,128]{1,0:T(8,128)(2,1)S(1)}, u32[]{:S(2)}, u32[]{:S(2)}) collective-permute-start(bf16[576,128]{1,0:T(8,128)(2,1)S(1)} %collective-permute-done.1.refs_1_), channel_id=1, source_target_pairs={{0,8},{4,12},{8,0},{12,4},{16,24},{20,28},{24,16},{28,20},{1,9},{5... | collective-permute-start | bytes 442376 | tf_op jit(solution)/shard_map/ppermute | solution.py:503
  15.4 3.1 %collective-permute-start.4 = (bf16[576,128]{1,0:T(8,128)(2,1)S(1)}, bf16[576,128]{1,0:T(8,128)(2,1)S(1)}, u32[]{:S(2)}, u32[]{:S(2)}) collective-permute-start(bf16[576,128]{1,0:T(8,128)(2,1)S(1)} %collective-permute-done.refs_0_), channel_id=1, source_target_pairs={{0,1},{1,0},{2,3},{3,2},{4,5},{5,4},{6,7},{7,6},{8,16},{9,17},{10,... | collective-permute-start | bytes 442376 | tf_op jit(solution)/shard_map/ppermute | solution.py:508
  15.4 15.5 %copy-start = (bf16[512,2048]{1,0:T(8,128)(2,1)S(1)}, bf16[512,2048]{1,0:T(8,128)(2,1)}, u32[]{:S(2)}) copy-start(bf16[512,2048]{1,0:T(8,128)(2,1)} %ku_ref.3) | copy-start | bytes 6291460
  15.4 15.5 %copy-start.1 = (bf16[512,2048]{1,0:T(8,128)(2,1)S(1)}, bf16[512,2048]{1,0:T(8,128)(2,1)}, u32[]{:S(2)}) copy-start(bf16[512,2048]{1,0:T(8,128)(2,1)} %vu_ref.3) | copy-start | bytes 6291460
  19.6 7.9 %collective-permute-start.5 = (bf16[8,128,128]{2,1,0:T(8,128)(2,1)S(1)}, bf16[8,128,128]{2,1,0:T(8,128)(2,1)S(1)}, u32[]{:S(2)}, u32[]{:S(2)}) collective-permute-start(bf16[8,128,128]{2,1,0:T(8,128)(2,1)S(1)} %get-tuple-element.70.pu_ref), channel_id=1, source_target_pairs={{0,8},{4,12},{8,0},{12,4},{16,24},{20,28},{24,16},{28,20},{1,9},{5... | collective-permute-start | bytes 786440 | tf_op jit(solution)/shard_map/ppermute | solution.py:503
  21.5 6.0 %collective-permute-start.6 = (bf16[8,128,128]{2,1,0:T(8,128)(2,1)S(1)}, bf16[8,128,128]{2,1,0:T(8,128)(2,1)S(1)}, u32[]{:S(2)}, u32[]{:S(2)}) collective-permute-start(bf16[8,128,128]{2,1,0:T(8,128)(2,1)S(1)} %get-tuple-element.70.pu_ref), channel_id=1, source_target_pairs={{0,1},{1,0},{2,3},{3,2},{4,5},{5,4},{6,7},{7,6},{8,16},{9,17},{10,... | collective-permute-start | bytes 786440 | tf_op jit(solution)/shard_map/ppermute | solution.py:508
  21.5 9.4 %collective-permute-start.9 = (bf16[2,576,128]{2,1,0:T(8,128)(2,1)S(1)}, bf16[2,576,128]{2,1,0:T(8,128)(2,1)S(1)}, u32[]{:S(2)}, u32[]{:S(2)}) collective-permute-start(bf16[2,576,128]{2,1,0:T(8,128)(2,1)S(1)} %get-tuple-element.77), channel_id=1, source_target_pairs={{0,4},{4,0},{8,12},{12,8},{16,20},{20,16},{24,28},{28,24},{1,5},{5... | collective-permute-start | bytes 884744 | tf_op jit(solution)/shard_map/ppermute | solution.py:503
  27.5 7.1 %collective-permute-start.7 = (bf16[8,128,128]{2,1,0:T(8,128)(2,1)S(1)}, bf16[8,128,128]{2,1,0:T(8,128)(2,1)S(1)}, u32[]{:S(2)}, u32[]{:S(2)}) collective-permute-start(bf16[8,128,128]{2,1,0:T(8,128)(2,1)S(1)} %pair_step.1), channel_id=1, source_target_pairs={{0,8},{4,12},{8,0},{12,4},{16,24},{20,28},{24,16},{28,20},{1,9},{5... | collective-permute-start | bytes 786440 | tf_op jit(solution)/shard_map/ppermute | solution.py:503
  30.1 4.5 %collective-permute-start.8 = (bf16[8,128,128]{2,1,0:T(8,128)(2,1)S(1)}, bf16[8,128,128]{2,1,0:T(8,128)(2,1)S(1)}, u32[]{:S(2)}, u32[]{:S(2)}) collective-permute-start(bf16[8,128,128]{2,1,0:T(8,128)(2,1)S(1)} %pair_step.1), channel_id=1, source_target_pairs={{0,1},{1,0},{2,3},{3,2},{4,5},{5,4},{6,7},{7,6},{8,16},{9,17},{10,... | collective-permute-start | bytes 786440 | tf_op jit(solution)/shard_map/ppermute | solution.py:508
  34.9 6.8 %collective-permute-start.10 = (bf16[8,128,128]{2,1,0:T(8,128)(2,1)S(1)}, bf16[8,128,128]{2,1,0:T(8,128)(2,1)S(1)}, u32[]{:S(2)}, u32[]{:S(2)}) collective-permute-start(bf16[8,128,128]{2,1,0:T(8,128)(2,1)S(1)} %get-tuple-element.81), channel_id=1, source_target_pairs={{0,4},{4,0},{8,12},{12,8},{16,20},{20,16},{24,28},{28,24},{1,5},{5... | collective-permute-start | bytes 786440 | tf_op jit(solution)/shard_map/ppermute | solution.py:503

commit v8 on v7

--- a/solution.py
+++ b/solution.py
@@ -333,19 +333,23 @@
         own_ref, out_ref, held_ref, sems = refs
         side = lax.axis_index("ctx") % 2
 
-        def copy_out(source, which, sem):
-            start = pl.multiple_of(which * width, width)
+        def copy_out(source, which, sem, first, count):
+            start = pl.multiple_of(which * width + first, 128)
             copies.append(
-                pltpu.make_async_copy(source, out_ref.at[:, pl.ds(start, width)], sems.at[sem])
+                pltpu.make_async_copy(
+                    source.at[:, pl.ds(first, count)],
+                    out_ref.at[:, pl.ds(start, count)],
+                    sems.at[sem],
+                )
             )
             copies[-1].start()
 
-        copy_out(own_ref, side, 0)
+        copy_out(own_ref, side, 0, 0, width)
     for h in range(s_ref.shape[0]):
         cols = slice(h * 128, (h + 1) * 128)
         held_ref[:, cols] = (lo_ref[:, cols] + mm(qe_ref[:, cols], s_ref[h])).astype(BF)
-    if len(refs) > 1:
-        copy_out(held_ref, 1 - side, 1)
+        if len(refs) > 1 and (h + 1) % 4 == 0:
+            copy_out(held_ref, 1 - side, (h + 1) // 4, h * 128 - 384, 512)
     for copy in copies:
         copy.wait()
 
@@ -353,7 +357,7 @@
 def final(qe, lo, s, own=None):
     rows, width = qe.shape
     args = [qe, lo, s] + ([] if own is None else [own])
-    scratch = [] if own is None else [pltpu.VMEM((rows, width), BF), pltpu.SemaphoreType.DMA((2,))]
+    scratch = [] if own is None else [pltpu.VMEM((rows, width), BF), pltpu.SemaphoreType.DMA((3,))]
     return pl.pallas_call(
         final_kernel,
         in_specs=[WHOLE] * len(args),

time: 43 us -> 42.9 us (level)
  no operation moved by 1% of the time
where the time goes in v8:
time: 42.9 us; the launch traced here: 42.8 us
  Pallas kernels  19 us (44%)
  starting transfers between devices  14.8 us (34%)
  waiting for transfers between devices  8.06 us (19%)
  between operations  0.91 us (2%)
    ppermute x7, starting transfers between devices, swap(): return lax.ppermute(x, 'ctx', list(enumerate(table)))  14.8 us
    pallas_call x3, Pallas kernels, kda_call(): pl.pallas_call(kernel, in_specs=in_specs, out_specs=[WHOLE] * len(shapes)...  9.71 us
    ppermute x7, waiting for transfers between devices, swap(): return lax.ppermute(x, 'ctx', list(enumerate(table)))  8.05 us
    pallas_call x2, Pallas kernels, mla(): pl.pallas_call(functools.partial(mla_kernel, reach, fresh, first), in_spe...  6.85 us
    pallas_call x2, Pallas kernels, final(): pl.pallas_call(final_kernel, in_specs=[WHOLE] * len(args), out_specs=WHOL...  1.14 us
  transfers between devices with their start and end apart: 11, of which 7 were waited for; matrix products, arithmetic and copies ran while one was open for 0% of the time, Pallas kernels for 32%

profile of v8, /device:TPU:0, one launch (start us, length us, event | category | flops | bytes accessed | tf_op | source)
XLA Modules:
  0.0 42.8 jit_solution(15433901749216614452)
XLA Ops:
  0.6 0.0 copy-start.4
  0.6 0.0 copy-start.3
  0.7 3.7 %kda_slab.3 = (bf16[128,1024]{1,0:T(8,128)(2,1)S(1)}, bf16[128,1024]{1,0:T(8,128)(2,1)S(1)}, bf16[128,1024]{1,0:T(8,128)(2,1)S(1)}, bf16[128,1024]{1,0:T(8,128)(...) custom-call(bf16[128,2048]{1,0:T(8,128)(2,1)} %refs_0_.1, ...), custom_call_target="tpu_custom_call" | custom-call | tf_op jit(solution)/shard_map/kda_slab/pallas_call | solution.py:203
  4.4 3.0 %collective-permute-start.2 = (bf16[8,128,256]{2,1,0:T(8,128)(2,1)S(1)}, bf16[8,128,256]{2,1,0:T(8,128)(2,1)S(1)}, u32[]{:S(2)}, u32[]{:S(2)}) collective-permute-start(bf16[8,128,256]{2,1,0:T(8,128)(2,1)S(1)} %get-tuple-element.56), channel_id=1, source_target_pairs={{0,4},{4,0},{8,12},{12,8},{16,20},{20,16},{24,28},{28,24},{1,5},{5... | collective-permute-start | bytes 1572872 | tf_op jit(solution)/shard_map/ppermute | solution.py:507
  7.4 0.0 copy-done.3
  7.4 1.6 %collective-permute-start = (bf16[576,128]{1,0:T(8,128)(2,1)S(1)}, bf16[576,128]{1,0:T(8,128)(2,1)S(1)}, u32[]{:S(2)}, u32[]{:S(2)}) collective-permute-start(bf16[576,128]{1,0:T(8,128)(2,1)S(1)} %bitcast.2), channel_id=1, source_target_pairs={{0,8},{4,12},{8,0},{12,4},{16,24},{20,28},{24,16},{28,20},{1,9},{5... | collective-permute-start | bytes 442376 | tf_op jit(solution)/shard_map/ppermute | solution.py:507
  9.0 0.0 collective-permute-start.1
  9.0 0.0 copy-done.4
  9.0 0.0 copy-start.2
  9.0 3.1 %kda_slab.4 = (bf16[8,128,256]{2,1,0:T(8,128)(2,1)S(1)}, bf16[128,1024]{1,0:T(8,128)(2,1)S(1)}, f32[128,1024]{1,0:T(8,128)S(1)}) custom-call(bf16[128,1024]{1,0:T(8,128)(2,1)S(1)} %get-tuple-element.50.refs_0_, bf16[128,1024]{1,0:T(8,128)(2,1)S(1)} %get-tuple-element.51.refs_1_, bf16[128,1024]{1,0:T(8,128)(2,1)S(1)} %get-tuple-element.52.refs_2_, ...), custom_call_target="tpu_custom_call" | custom-call | tf_op jit(solution)/shard_map/kda_slab/pallas_call | solution.py:203
  12.1 0.6 %collective-permute-done.refs_0_ = bf16[576,128]{1,0:T(8,128)(2,1)S(1)} collective-permute-done((bf16[576,128]{1,0:T(8,128)(2,1)S(1)}, bf16[576,128]{1,0:T(8,128)(2,1)S(1)}, u32[]{:S(2)}, u32[]{:S(2)}) %collective-permute-start) | collective-permute-done | bytes 147488 | tf_op jit(solution)/shard_map/ppermute | solution.py:507
  12.7 0.0 collective-permute-done.1.refs_1_
  12.7 2.7 %collective-permute-start.3 = (bf16[576,128]{1,0:T(8,128)(2,1)S(1)}, bf16[576,128]{1,0:T(8,128)(2,1)S(1)}, u32[]{:S(2)}, u32[]{:S(2)}) collective-permute-start(bf16[576,128]{1,0:T(8,128)(2,1)S(1)} %collective-permute-done.1.refs_1_), channel_id=1, source_target_pairs={{0,8},{4,12},{8,0},{12,4},{16,24},{20,28},{24,16},{28,20},{1,9},{5... | collective-permute-start | bytes 442376 | tf_op jit(solution)/shard_map/ppermute | solution.py:507
  15.4 0.0 collective-permute-start.4
  15.4 0.0 copy-start
  15.4 0.0 copy-start.1
  15.4 2.9 %kda_slab.5 = (bf16[128,1024]{1,0:T(8,128)(2,1)S(1)}, f32[128,1024]{1,0:T(8,128)S(1)}) custom-call(bf16[128,1024]{1,0:T(8,128)(2,1)S(1)} %get-tuple-element.60.refs_0_, bf16[128,1024]{1,0:T(8,128)(2,1)S(1)} %get-tuple-element.61.refs_1_, bf16[128,1024]{1,0:T(8,128)(2,1)S(1)} %get-tuple-element.62.refs_2_, bf16[128,1024]{1,0:T(8,128)(2,1)S(1)} %get-tuple-element.63.refs_3_, ...), custom_call_target="tpu_custom_call" | custom-call | tf_op jit(solution)/shard_map/kda_slab/pallas_call | solution.py:203
  18.3 0.2 collective-permute-done.3.refs_2_
  18.5 0.0 collective-permute-done.4.refs_3_
  18.5 0.1 pick_latents.1
  18.6 0.7 %collective-permute-done.2.got_ref = bf16[8,128,256]{2,1,0:T(8,128)(2,1)S(1)} collective-permute-done((bf16[8,128,256]{2,1,0:T(8,128)(2,1)S(1)}, bf16[8,128,256]{2,1,0:T(8,128)(2,1)S(1)}, u32[]{:S(2)}, u32[]{:S(2)}) %collective-permute-start.2) | collective-permute-done | bytes 524320 | tf_op jit(solution)/shard_map/ppermute | solution.py:507
  19.3 0.3 pair_join.1
  19.6 1.9 %collective-permute-start.5 = (bf16[8,128,128]{2,1,0:T(8,128)(2,1)S(1)}, bf16[8,128,128]{2,1,0:T(8,128)(2,1)S(1)}, u32[]{:S(2)}, u32[]{:S(2)}) collective-permute-start(bf16[8,128,128]{2,1,0:T(8,128)(2,1)S(1)} %get-tuple-element.70.pu_ref), channel_id=1, source_target_pairs={{0,8},{4,12},{8,0},{12,4},{16,24},{20,28},{24,16},{28,20},{1,9},{5... | collective-permute-start | bytes 786440 | tf_op jit(solution)/shard_map/ppermute | solution.py:507
  21.5 0.0 collective-permute-start.6
  21.5 1.5 %collective-permute-start.9 = (bf16[2,576,128]{2,1,0:T(8,128)(2,1)S(1)}, bf16[2,576,128]{2,1,0:T(8,128)(2,1)S(1)}, u32[]{:S(2)}, u32[]{:S(2)}) collective-permute-start(bf16[2,576,128]{2,1,0:T(8,128)(2,1)S(1)} %get-tuple-element.77), channel_id=1, source_target_pairs={{0,4},{4,0},{8,12},{12,8},{16,20},{20,16},{24,28},{28,24},{1,5},{5... | collective-permute-start | bytes 884744 | tf_op jit(solution)/shard_map/ppermute | solution.py:507
  23.0 0.7 %window_mask.1.bias_ref = f32[128,640]{1,0:T(8,128)S(1)} custom-call(s32[8]{0:T(128)S(1)} %copy-done.4), custom_call_target="tpu_custom_call" | custom-call | tf_op jit(solution)/shard_map/window_mask/pallas_call | solution.py:419
  23.7 3.8 %collective-permute-done.5.a_ref = bf16[8,128,128]{2,1,0:T(8,128)(2,1)S(1)} collective-permute-done((bf16[8,128,128]{2,1,0:T(8,128)(2,1)S(1)}, bf16[8,128,128]{2,1,0:T(8,128)(2,1)S(1)}, u32[]{:S(2)}, u32[]{:S(2)}) %collective-permute-start.5) | collective-permute-done | bytes 262176 | tf_op jit(solution)/shard_map/ppermute | solution.py:507
  27.5 0.0 collective-permute-done.6.b_ref
  27.5 2.6 %collective-permute-start.7 = (bf16[8,128,128]{2,1,0:T(8,128)(2,1)S(1)}, bf16[8,128,128]{2,1,0:T(8,128)(2,1)S(1)}, u32[]{:S(2)}, u32[]{:S(2)}) collective-permute-start(bf16[8,128,128]{2,1,0:T(8,128)(2,1)S(1)} %pair_step.1), channel_id=1, source_target_pairs={{0,8},{4,12},{8,0},{12,4},{16,24},{20,28},{24,16},{28,20},{1,9},{5... | collective-permute-start | bytes 786440 | tf_op jit(solution)/shard_map/ppermute | solution.py:507
  30.1 0.0 collective-permute-start.8
  30.1 0.8 %collective-permute-done.9.refs_1_ = bf16[2,576,128]{2,1,0:T(8,128)(2,1)S(1)} collective-permute-done((bf16[2,576,128]{2,1,0:T(8,128)(2,1)S(1)}, bf16[2,576,128]{2,1,0:T(8,128)(2,1)S(1)}, u32[]{:S(2)}, u32[]{:S(2)}) %collective-permute-start.9) | collective-permute-done | bytes 294944 | tf_op jit(solution)/shard_map/ppermute | solution.py:507
  30.9 0.0 copy-done.2
  30.9 0.0 copy-done
  30.9 0.0 copy-done.1
  30.9 2.5 %mla_heads.2 = (bf16[640,576]{1,0:T(8,128)(2,1)S(1)}, bf16[128,768]{1,0:T(8,128)(2,1)S(1)}) custom-call(f32[128,640]{1,0:T(8,128)S(1)} %window_mask.1.bias_ref, bf16[128,3072]{1,0:T(8,128)(2,1)S(1)} %copy-done.2, bf16[512,2048]{1,0:T(8,128)(2,1)S(1)} %copy-done, bf16[512,2048]{1,0:T(8,128)(2,1)S(1)} %copy-done.1, ...), custom_call_target="tpu_custom_call" | custom-call | tf_op jit(solution)/shard_map/mla_heads/pallas_call | solution.py:482
  33.4 1.2 %collective-permute-done.7.a_ref = bf16[8,128,128]{2,1,0:T(8,128)(2,1)S(1)} collective-permute-done((bf16[8,128,128]{2,1,0:T(8,128)(2,1)S(1)}, bf16[8,128,128]{2,1,0:T(8,128)(2,1)S(1)}, u32[]{:S(2)}, u32[]{:S(2)}) %collective-permute-start.7) | collective-permute-done | bytes 262176 | tf_op jit(solution)/shard_map/ppermute | solution.py:507
  34.6 0.0 collective-permute-done.8.b_ref
  34.6 0.3 slab_states.1
  34.9 1.5 %collective-permute-start.10 = (bf16[8,128,128]{2,1,0:T(8,128)(2,1)S(1)}, bf16[8,128,128]{2,1,0:T(8,128)(2,1)S(1)}, u32[]{:S(2)}, u32[]{:S(2)}) collective-permute-start(bf16[8,128,128]{2,1,0:T(8,128)(2,1)S(1)} %get-tuple-element.81), channel_id=1, source_target_pairs={{0,4},{4,0},{8,12},{12,8},{16,20},{20,16},{24,28},{28,24},{1,5},{5... | collective-permute-start | bytes 786440 | tf_op jit(solution)/shard_map/ppermute | solution.py:507
  36.4 4.4 %mla_heads.3 = bf16[128,2048]{1,0:T(8,128)(2,1)} custom-call(f32[128,640]{1,0:T(8,128)S(1)} %window_mask.1.bias_ref, bf16[128,3072]{1,0:T(8,128)(2,1)S(1)} %copy-done.2, bf16[512,2048]{1,0:T(8,128)(2,1)S(1)} %copy-done, bf16[512,2048]{1,0:T(8,128)(2,1)S(1)} %copy-done.1, bf16[640,576]{1,0:T(8,128)(2,1)S(1)} %get-tuple-element.83.refs_0_, ...), custom_call_target="tpu_custom_call" | custom-call | tf_op jit(solution)/shard_map/mla_heads/pallas_call | solution.py:482
  40.8 0.2 kda_out.2.refs_0_
  41.0 0.7 %collective-permute-done.10.s_ref = bf16[8,128,128]{2,1,0:T(8,128)(2,1)S(1)} collective-permute-done((bf16[8,128,128]{2,1,0:T(8,128)(2,1)S(1)}, bf16[8,128,128]{2,1,0:T(8,128)(2,1)S(1)}, u32[]{:S(2)}, u32[]{:S(2)}) %collective-permute-start.10) | collective-permute-done | bytes 262176 | tf_op jit(solution)/shard_map/ppermute | solution.py:507
  41.7 0.9 %kda_out.3 = bf16[128,2048]{1,0:T(8,128)(2,1)} custom-call(bf16[128,1024]{1,0:T(8,128)(2,1)S(1)} %get-tuple-element.64.qe_ref, f32[128,1024]{1,0:T(8,128)S(1)} %get-tuple-element.65.lo_ref, bf16[8,128,128]{2,1,0:T(8,128)(2,1)S(1)} %collective-permute-done.10.s_ref, bf16[128,1024]{1,0:T(8,128)(2,1)S(1)} %kda_out.2.refs_0_), custom_call_target="tpu_custom_call" | custom-call | tf_op jit(solution)/shard_map/kda_out/pallas_call | solution.py:361
  (1 shorter events, 0.0 us)
Async XLA Ops:
  0.6 8.3 %copy-start.4 = (s32[8]{0:T(128)S(1)}, s32[8]{0:T(128)}, u32[]{:S(2)}) copy-start(s32[8]{0:T(128)} %lengths) | copy-start | bytes 100
  0.6 6.7 %copy-start.3 = (bf16[128,576]{0,1:T(8,128)(2,1)S(1)}, bf16[128,576]{0,1:T(8,128)(2,1)}, u32[]{:S(2)}) copy-start(bf16[128,576]{0,1:T(8,128)(2,1)} %param.16) | copy-start | bytes 442372
  4.4 14.9 %collective-permute-start.2 = (bf16[8,128,256]{2,1,0:T(8,128)(2,1)S(1)}, bf16[8,128,256]{2,1,0:T(8,128)(2,1)S(1)}, u32[]{:S(2)}, u32[]{:S(2)}) collective-permute-start(bf16[8,128,256]{2,1,0:T(8,128)(2,1)S(1)} %get-tuple-element.56), channel_id=1, source_target_pairs={{0,4},{4,0},{8,12},{12,8},{16,20},{20,16},{24,28},{28,24},{1,5},{5... | collective-permute-start | bytes 1572872 | tf_op jit(solution)/shard_map/ppermute | solution.py:507
  7.4 5.3 %collective-permute-start = (bf16[576,128]{1,0:T(8,128)(2,1)S(1)}, bf16[576,128]{1,0:T(8,128)(2,1)S(1)}, u32[]{:S(2)}, u32[]{:S(2)}) collective-permute-start(bf16[576,128]{1,0:T(8,128)(2,1)S(1)} %bitcast.2), channel_id=1, source_target_pairs={{0,8},{4,12},{8,0},{12,4},{16,24},{20,28},{24,16},{28,20},{1,9},{5... | collective-permute-start | bytes 442376 | tf_op jit(solution)/shard_map/ppermute | solution.py:507
  9.0 3.7 %collective-permute-start.1 = (bf16[576,128]{1,0:T(8,128)(2,1)S(1)}, bf16[576,128]{1,0:T(8,128)(2,1)S(1)}, u32[]{:S(2)}, u32[]{:S(2)}) collective-permute-start(bf16[576,128]{1,0:T(8,128)(2,1)S(1)} %bitcast.3), channel_id=1, source_target_pairs={{0,1},{1,0},{2,3},{3,2},{4,5},{5,4},{6,7},{7,6},{8,16},{9,17},{10,... | collective-permute-start | bytes 442376 | tf_op jit(solution)/shard_map/ppermute | solution.py:512
  9.0 21.9 %copy-start.2 = (bf16[128,3072]{1,0:T(8,128)(2,1)S(1)}, bf16[128,3072]{1,0:T(8,128)(2,1)}, u32[]{:S(2)}) copy-start(bf16[128,3072]{1,0:T(8,128)(2,1)} %q_ref.3) | copy-start | bytes 2359300
  12.7 5.8 %collective-permute-start.3 = (bf16[576,128]{1,0:T(8,128)(2,1)S(1)}, bf16[576,128]{1,0:T(8,128)(2,1)S(1)}, u32[]{:S(2)}, u32[]{:S(2)}) collective-permute-start(bf16[576,128]{1,0:T(8,128)(2,1)S(1)} %collective-permute-done.1.refs_1_), channel_id=1, source_target_pairs={{0,8},{4,12},{8,0},{12,4},{16,24},{20,28},{24,16},{28,20},{1,9},{5... | collective-permute-start | bytes 442376 | tf_op jit(solution)/shard_map/ppermute | solution.py:507
  15.4 3.1 %collective-permute-start.4 = (bf16[576,128]{1,0:T(8,128)(2,1)S(1)}, bf16[576,128]{1,0:T(8,128)(2,1)S(1)}, u32[]{:S(2)}, u32[]{:S(2)}) collective-permute-start(bf16[576,128]{1,0:T(8,128)(2,1)S(1)} %collective-permute-done.refs_0_), channel_id=1, source_target_pairs={{0,1},{1,0},{2,3},{3,2},{4,5},{5,4},{6,7},{7,6},{8,16},{9,17},{10,... | collective-permute-start | bytes 442376 | tf_op jit(solution)/shard_map/ppermute | solution.py:512
  15.4 15.5 %copy-start = (bf16[512,2048]{1,0:T(8,128)(2,1)S(1)}, bf16[512,2048]{1,0:T(8,128)(2,1)}, u32[]{:S(2)}) copy-start(bf16[512,2048]{1,0:T(8,128)(2,1)} %ku_ref.3) | copy-start | bytes 6291460
  15.4 15.5 %copy-start.1 = (bf16[512,2048]{1,0:T(8,128)(2,1)S(1)}, bf16[512,2048]{1,0:T(8,128)(2,1)}, u32[]{:S(2)}) copy-start(bf16[512,2048]{1,0:T(8,128)(2,1)} %vu_ref.3) | copy-start | bytes 6291460
  19.6 7.9 %collective-permute-start.5 = (bf16[8,128,128]{2,1,0:T(8,128)(2,1)S(1)}, bf16[8,128,128]{2,1,0:T(8,128)(2,1)S(1)}, u32[]{:S(2)}, u32[]{:S(2)}) collective-permute-start(bf16[8,128,128]{2,1,0:T(8,128)(2,1)S(1)} %get-tuple-element.70.pu_ref), channel_id=1, source_target_pairs={{0,8},{4,12},{8,0},{12,4},{16,24},{20,28},{24,16},{28,20},{1,9},{5... | collective-permute-start | bytes 786440 | tf_op jit(solution)/shard_map/ppermute | solution.py:507
  21.5 6.0 %collective-permute-start.6 = (bf16[8,128,128]{2,1,0:T(8,128)(2,1)S(1)}, bf16[8,128,128]{2,1,0:T(8,128)(2,1)S(1)}, u32[]{:S(2)}, u32[]{:S(2)}) collective-permute-start(bf16[8,128,128]{2,1,0:T(8,128)(2,1)S(1)} %get-tuple-element.70.pu_ref), channel_id=1, source_target_pairs={{0,1},{1,0},{2,3},{3,2},{4,5},{5,4},{6,7},{7,6},{8,16},{9,17},{10,... | collective-permute-start | bytes 786440 | tf_op jit(solution)/shard_map/ppermute | solution.py:512
  21.5 9.4 %collective-permute-start.9 = (bf16[2,576,128]{2,1,0:T(8,128)(2,1)S(1)}, bf16[2,576,128]{2,1,0:T(8,128)(2,1)S(1)}, u32[]{:S(2)}, u32[]{:S(2)}) collective-permute-start(bf16[2,576,128]{2,1,0:T(8,128)(2,1)S(1)} %get-tuple-element.77), channel_id=1, source_target_pairs={{0,4},{4,0},{8,12},{12,8},{16,20},{20,16},{24,28},{28,24},{1,5},{5... | collective-permute-start | bytes 884744 | tf_op jit(solution)/shard_map/ppermute | solution.py:507
  27.5 7.1 %collective-permute-start.7 = (bf16[8,128,128]{2,1,0:T(8,128)(2,1)S(1)}, bf16[8,128,128]{2,1,0:T(8,128)(2,1)S(1)}, u32[]{:S(2)}, u32[]{:S(2)}) collective-permute-start(bf16[8,128,128]{2,1,0:T(8,128)(2,1)S(1)} %pair_step.1), channel_id=1, source_target_pairs={{0,8},{4,12},{8,0},{12,4},{16,24},{20,28},{24,16},{28,20},{1,9},{5... | collective-permute-start | bytes 786440 | tf_op jit(solution)/shard_map/ppermute | solution.py:507
  30.1 4.5 %collective-permute-start.8 = (bf16[8,128,128]{2,1,0:T(8,128)(2,1)S(1)}, bf16[8,128,128]{2,1,0:T(8,128)(2,1)S(1)}, u32[]{:S(2)}, u32[]{:S(2)}) collective-permute-start(bf16[8,128,128]{2,1,0:T(8,128)(2,1)S(1)} %pair_step.1), channel_id=1, source_target_pairs={{0,1},{1,0},{2,3},{3,2},{4,5},{5,4},{6,7},{7,6},{8,16},{9,17},{10,... | collective-permute-start | bytes 786440 | tf_op jit(solution)/shard_map/ppermute | solution.py:512
  34.9 6.8 %collective-permute-start.10 = (bf16[8,128,128]{2,1,0:T(8,128)(2,1)S(1)}, bf16[8,128,128]{2,1,0:T(8,128)(2,1)S(1)}, u32[]{:S(2)}, u32[]{:S(2)}) collective-permute-start(bf16[8,128,128]{2,1,0:T(8,128)(2,1)S(1)} %get-tuple-element.81), channel_id=1, source_target_pairs={{0,4},{4,0},{8,12},{12,8},{16,20},{20,16},{24,28},{28,24},{1,5},{5... | collective-permute-start | bytes 786440 | tf_op jit(solution)/shard_map/ppermute | solution.py:507
